TPU v7x, 32 devices: a whole 2x2x4 slice. The times are simulated.
32 devices in a mesh: cells: 8 (over y, x, core), chrom: 4 (over z).
Axes of the slice: x: 2, y: 2, z: 4, core: 2. Of those that a mesh axis runs over, the one named last changes fastest.
Arguments:
- inputs: bfloat16 [16, 1024, 1280], P('cells', 'chrom'), may hold values from -6 to 6
- lengths: int32 [16], P('cells'), may hold values from 204 to 1024, as said below
- offsets: int32 [16, 24], P('cells'), may hold values from 1 to 1023, as said below
- cotangent: bfloat16 [16, 1024, 1280], P('cells', 'chrom'), may hold values from -6 to 6
- norm_gain: bfloat16 [1280], P('chrom'), may hold values from 0.5 to 1.5
- norm_shift: bfloat16 [1280], P('chrom'), may hold values from -1.75 to 1.75
- query_proj: bfloat16 [1280, 1280], P('chrom'), may hold values from -0.15625 to 0.15625
- query_bias: bfloat16 [1280], P('chrom'), may hold values from -1.75 to 1.75
- key_proj: bfloat16 [1280, 1280], P('chrom'), may hold values from -0.15625 to 0.15625
- value_proj: bfloat16 [1280, 1280], P('chrom'), may hold values from -0.15625 to 0.15625
- value_bias: bfloat16 [1280], P('chrom'), may hold values from -1.75 to 1.75
- output_proj: bfloat16 [1280, 1280], P('chrom'), may hold values from -1.25 to 1.25
- output_bias: bfloat16 [1280], P('chrom'), may hold values from -1.75 to 1.75
- second_gain: bfloat16 [1280], P('chrom'), may hold values from 0.5 to 1.5
- second_shift: bfloat16 [1280], P('chrom'), may hold values from -1.75 to 1.75
- inner_proj: bfloat16 [1280, 5120], P('chrom'), may hold values from -0.15625 to 0.15625
- inner_bias: bfloat16 [5120], P('chrom'), may hold values from -1.75 to 1.75
- outer_proj: bfloat16 [5120, 1280], P('chrom'), may hold values from -0.078125 to 0.078125
- outer_bias: bfloat16 [1280], P('chrom'), may hold values from -1.75 to 1.75
Outputs:
- block_out: bfloat16 [16, 1024, 1280], P('cells', 'chrom')
- input_grad: bfloat16 [16, 1024, 1280], P('cells', 'chrom')
- norm_gain_grad: float32 [1280], P('chrom')
- norm_shift_grad: float32 [1280], P('chrom')
- query_proj_grad: float32 [1280, 1280], P('chrom')
- query_bias_grad: float32 [1280], P('chrom')
- key_proj_grad: float32 [1280, 1280], P('chrom')
- value_proj_grad: float32 [1280, 1280], P('chrom')
- value_bias_grad: float32 [1280], P('chrom')
- output_proj_grad: float32 [1280, 1280], P('chrom')
- output_bias_grad: float32 [1280], P('chrom')
- second_gain_grad: float32 [1280], P('chrom')
- second_shift_grad: float32 [1280], P('chrom')
- inner_proj_grad: float32 [1280, 5120], P('chrom')
- inner_bias_grad: float32 [5120], P('chrom')
- outer_proj_grad: float32 [5120, 1280], P('chrom')
- outer_bias_grad: float32 [1280], P('chrom')
Inputs may be any that keep to these rules, and one draw needn't show every extreme that they name: `lengths`: among the 2 cells of each index of cells one cell has exactly 1024 tokens. `offsets`: each cell's row is non-decreasing, its first entry is 1 and its last is the cell's length minus 1.
All inputs are finite; a program needn't handle non-finite values.
Results may differ from a plain program's by a relative error of at most 0.02.
Values may be sent and summed in bfloat16 or wider, within the bound.
A program may use at most 384 MiB of HBM per device.

v0:
```python
import jax
import jax.numpy as jnp
from jax import lax
from jax.sharding import PartitionSpec as P

HEADS = 20
HEAD_DIM = 64


eps_norm = 1e-05
group_bias = 1.0


def layer_norm(values, gain, shift):
    center = values - jnp.mean(values, axis=-1, keepdims=True)
    spread = jnp.mean(center * center, axis=-1, keepdims=True)
    return center * lax.rsqrt(spread + eps_norm) * gain + shift


def gelu_exact(values):
    return jax.nn.gelu(values, approximate=False)


def product(left, right):
    return jnp.dot(left, right, preferred_element_type=jnp.float32)


def left_product(left, right):
    return jnp.einsum("ra,rb->ab", left, right, preferred_element_type=jnp.float32)


def right_back(left, right):
    return jnp.einsum("rb,ab->ra", left, right, preferred_element_type=jnp.float32)


def column_sum(values):
    return jnp.sum(values, axis=0, dtype=jnp.float32)


def split_rows(value, outer, inner_count):
    return value.reshape(
        (outer, inner_count, value.shape[0] // (outer * inner_count)) + value.shape[1:]
    )


def local(
    inputs,
    lengths,
    offsets,
    cotangent,
    norm_gain,
    norm_shift,
    query_proj,
    query_bias,
    key_proj,
    value_proj,
    value_bias,
    output_proj,
    output_bias,
    second_gain,
    second_shift,
    inner_proj,
    inner_bias,
    outer_proj,
    outer_bias,
):
    count_chrom = lax.axis_size("chrom")
    count_cells = lax.axis_size("cells")
    block_index = lax.axis_index("chrom")
    cells_here, tokens_here, feat_width = inputs.shape
    seq_len = tokens_here * count_chrom
    row_count = cells_here * tokens_here
    inv_root = HEAD_DIM ** (-0.5)
    places = jnp.arange(seq_len, dtype=jnp.int32)
    key_live = places[None, :] < lengths[:, None]
    groups = jnp.sum((places[None, :, None] >= offsets[:, None, :]).astype(jnp.int32), axis=2)
    query_groups = lax.dynamic_slice_in_dim(groups, block_index * tokens_here, tokens_here, 1)
    query_live = lax.dynamic_slice_in_dim(key_live, block_index * tokens_here, tokens_here, 1)
    same_group = (query_groups[:, :, None] == groups[:, None, :]).astype(jnp.float32)
    mask_bias = jnp.where(key_live[:, None, :], group_bias * same_group, -jnp.inf)[:, None]
    gathered = (
        lax.all_gather(norm_gain, "chrom", axis=0, tiled=True),
        lax.all_gather(norm_shift, "chrom", axis=0, tiled=True),
        lax.all_gather(query_proj, "chrom", axis=0, tiled=True),
        lax.all_gather(query_bias, "chrom", axis=0, tiled=True),
        lax.all_gather(key_proj, "chrom", axis=0, tiled=True),
        lax.all_gather(value_proj, "chrom", axis=0, tiled=True),
        lax.all_gather(value_bias, "chrom", axis=0, tiled=True),
        lax.all_gather(output_proj, "chrom", axis=0, tiled=True),
        lax.all_gather(output_bias, "chrom", axis=0, tiled=True),
        lax.all_gather(second_gain, "chrom", axis=0, tiled=True),
        lax.all_gather(second_shift, "chrom", axis=0, tiled=True),
        lax.all_gather(inner_proj, "chrom", axis=0, tiled=True),
        lax.all_gather(inner_bias, "chrom", axis=0, tiled=True),
        lax.all_gather(outer_proj, "chrom", axis=0, tiled=True),
        lax.all_gather(outer_bias, "chrom", axis=0, tiled=True),
    )
    gain_one = gathered[0].astype(jnp.float32)
    shift_one = gathered[1].astype(jnp.float32)
    gain_two = gathered[9].astype(jnp.float32)
    shift_two = gathered[10].astype(jnp.float32)
    states = inputs.astype(jnp.float32).reshape(row_count, feat_width)
    normed_full, norm_back = jax.vjp(layer_norm, states, gain_one, shift_one)
    normed = normed_full.astype(jnp.bfloat16)
    queries = (product(normed, gathered[2]) + gathered[3].astype(jnp.float32)).astype(jnp.bfloat16)
    key_rows = product(normed, gathered[4]).astype(jnp.bfloat16)
    vals = (product(normed, gathered[5]) + gathered[6].astype(jnp.float32)).astype(jnp.bfloat16)
    keys_all, vals_all = (
        lax.all_gather(
            key_rows.reshape(cells_here, tokens_here, feat_width), "chrom", axis=1, tiled=True
        ),
        lax.all_gather(
            vals.reshape(cells_here, tokens_here, feat_width), "chrom", axis=1, tiled=True
        ),
    )
    query_heads = queries.reshape(cells_here, tokens_here, HEADS, HEAD_DIM)
    key_heads = keys_all.reshape(cells_here, seq_len, HEADS, HEAD_DIM)
    val_heads = vals_all.reshape(cells_here, seq_len, HEADS, HEAD_DIM)

    def scores_of():
        raw = (
            jnp.einsum(
                "cqhd,ckhd->chqk", query_heads, key_heads, preferred_element_type=jnp.float32
            )
            * inv_root
        )
        return raw + mask_bias

    masked = scores_of()
    row_max = jnp.max(masked, axis=-1, keepdims=True)
    exp_scores = jnp.exp(masked - row_max)
    exp_total = jnp.sum(exp_scores, axis=-1, keepdims=True)
    attn_probs = exp_scores / exp_total
    log_total = row_max + jnp.log(exp_total)
    mixed_out = jnp.einsum(
        "chqk,ckhd->cqhd",
        attn_probs.astype(jnp.bfloat16),
        val_heads,
        preferred_element_type=jnp.float32,
    )
    mixed_out = mixed_out.astype(jnp.bfloat16).reshape(row_count, feat_width)
    attended = product(mixed_out, gathered[7]) + gathered[8].astype(jnp.float32)
    middle = states + attended
    second_full, second_back = jax.vjp(layer_norm, middle, gain_two, shift_two)
    second = second_full.astype(jnp.bfloat16)
    inner_pre = product(second, gathered[11]) + gathered[12].astype(jnp.float32)
    active_full, gelu_back = jax.vjp(gelu_exact, inner_pre)
    active = active_full.astype(jnp.bfloat16)
    result = middle + product(active, gathered[13]) + gathered[14].astype(jnp.float32)
    live_rows = query_live.reshape(row_count, 1)
    block_out = (
        jnp.where(live_rows, result, 0.0)
        .astype(jnp.bfloat16)
        .reshape(cells_here, tokens_here, feat_width)
    )
    upstream = jnp.where(
        live_rows, cotangent.reshape(row_count, feat_width), jnp.zeros((), jnp.bfloat16)
    )
    outer_bias_grad = column_sum(upstream)
    outer_proj_grad = left_product(active, upstream)
    grad_active = right_back(upstream, gathered[13])
    (grad_inner_full,) = gelu_back(grad_active)
    grad_inner = grad_inner_full.astype(jnp.bfloat16)
    inner_bias_grad = column_sum(grad_inner)
    inner_proj_grad = left_product(second, grad_inner)
    grad_second = right_back(grad_inner, gathered[11])
    grad_middle_norm, second_gain_grad, second_shift_grad = second_back(grad_second)
    grad_middle = upstream.astype(jnp.float32) + grad_middle_norm
    grad_attended = grad_middle.astype(jnp.bfloat16)
    output_bias_grad = column_sum(grad_attended)
    output_proj_grad = left_product(mixed_out, grad_attended)
    grad_mixed = right_back(grad_attended, gathered[7]).astype(jnp.bfloat16)
    grad_mixed = grad_mixed.reshape(cells_here, tokens_here, HEADS, HEAD_DIM)
    attn_again = jnp.exp(scores_of() - log_total)
    grad_probs = jnp.einsum(
        "cqhd,ckhd->chqk", grad_mixed, val_heads, preferred_element_type=jnp.float32
    )
    row_dot = jnp.sum(attn_again * grad_probs, axis=-1, keepdims=True)
    grad_raw = (attn_again * (grad_probs - row_dot)).astype(jnp.bfloat16)
    grad_vals_part = jnp.einsum(
        "chqk,cqhd->ckhd",
        attn_again.astype(jnp.bfloat16),
        grad_mixed,
        preferred_element_type=jnp.float32,
    )
    grad_keys_part = (
        jnp.einsum("chqk,cqhd->ckhd", grad_raw, query_heads, preferred_element_type=jnp.float32)
        * inv_root
    )
    grad_queries = (
        jnp.einsum("chqk,ckhd->cqhd", grad_raw, key_heads, preferred_element_type=jnp.float32)
        * inv_root
    ).astype(jnp.bfloat16)
    grad_queries = grad_queries.reshape(row_count, feat_width)
    grad_keys_sum, grad_vals_sum = (
        lax.psum_scatter(
            grad_keys_part.reshape(cells_here, seq_len, feat_width).astype(jnp.bfloat16),
            "chrom",
            scatter_dimension=1,
            tiled=True,
        ).astype(jnp.float32),
        lax.psum_scatter(
            grad_vals_part.reshape(cells_here, seq_len, feat_width).astype(jnp.bfloat16),
            "chrom",
            scatter_dimension=1,
            tiled=True,
        ).astype(jnp.float32),
    )
    grad_keys = grad_keys_sum.astype(jnp.bfloat16).reshape(row_count, feat_width)
    grad_vals = grad_vals_sum.astype(jnp.bfloat16).reshape(row_count, feat_width)
    query_proj_grad = left_product(normed, grad_queries)
    query_bias_grad = column_sum(grad_queries)
    key_proj_grad = left_product(normed, grad_keys)
    value_proj_grad = left_product(normed, grad_vals)
    value_bias_grad = column_sum(grad_vals)
    grad_normed = (
        right_back(grad_queries, gathered[2])
        + right_back(grad_keys, gathered[4])
        + right_back(grad_vals, gathered[5])
    )
    grad_states_norm, norm_gain_grad, norm_shift_grad = norm_back(grad_normed)
    input_grad = (
        (grad_middle + grad_states_norm)
        .astype(jnp.bfloat16)
        .reshape(cells_here, tokens_here, feat_width)
    )
    grad_list = (
        norm_gain_grad,
        norm_shift_grad,
        query_proj_grad,
        query_bias_grad,
        key_proj_grad,
        value_proj_grad,
        value_bias_grad,
        output_proj_grad,
        output_bias_grad,
        second_gain_grad,
        second_shift_grad,
        inner_proj_grad,
        inner_bias_grad,
        outer_proj_grad,
        outer_bias_grad,
    )
    pieces = tuple((split_rows(member, count_chrom, count_cells) for member in grad_list))
    section_one = (
        lax.psum_scatter(
            pieces[0].astype(jnp.bfloat16), "cells", scatter_dimension=1, tiled=True
        ).astype(jnp.float32),
        lax.psum_scatter(
            pieces[1].astype(jnp.bfloat16), "cells", scatter_dimension=1, tiled=True
        ).astype(jnp.float32),
        lax.psum_scatter(
            pieces[2].astype(jnp.bfloat16), "cells", scatter_dimension=1, tiled=True
        ).astype(jnp.float32),
        lax.psum_scatter(
            pieces[3].astype(jnp.bfloat16), "cells", scatter_dimension=1, tiled=True
        ).astype(jnp.float32),
        lax.psum_scatter(
            pieces[4].astype(jnp.bfloat16), "cells", scatter_dimension=1, tiled=True
        ).astype(jnp.float32),
        lax.psum_scatter(
            pieces[5].astype(jnp.bfloat16), "cells", scatter_dimension=1, tiled=True
        ).astype(jnp.float32),
        lax.psum_scatter(
            pieces[6].astype(jnp.bfloat16), "cells", scatter_dimension=1, tiled=True
        ).astype(jnp.float32),
        lax.psum_scatter(
            pieces[7].astype(jnp.bfloat16), "cells", scatter_dimension=1, tiled=True
        ).astype(jnp.float32),
        lax.psum_scatter(
            pieces[8].astype(jnp.bfloat16), "cells", scatter_dimension=1, tiled=True
        ).astype(jnp.float32),
        lax.psum_scatter(
            pieces[9].astype(jnp.bfloat16), "cells", scatter_dimension=1, tiled=True
        ).astype(jnp.float32),
        lax.psum_scatter(
            pieces[10].astype(jnp.bfloat16), "cells", scatter_dimension=1, tiled=True
        ).astype(jnp.float32),
        lax.psum_scatter(
            pieces[11].astype(jnp.bfloat16), "cells", scatter_dimension=1, tiled=True
        ).astype(jnp.float32),
        lax.psum_scatter(
            pieces[12].astype(jnp.bfloat16), "cells", scatter_dimension=1, tiled=True
        ).astype(jnp.float32),
        lax.psum_scatter(
            pieces[13].astype(jnp.bfloat16), "cells", scatter_dimension=1, tiled=True
        ).astype(jnp.float32),
        lax.psum_scatter(
            pieces[14].astype(jnp.bfloat16), "cells", scatter_dimension=1, tiled=True
        ).astype(jnp.float32),
    )
    section_two = (
        lax.psum_scatter(
            section_one[0].astype(jnp.bfloat16), "chrom", scatter_dimension=0, tiled=True
        ).astype(jnp.float32),
        lax.psum_scatter(
            section_one[1].astype(jnp.bfloat16), "chrom", scatter_dimension=0, tiled=True
        ).astype(jnp.float32),
        lax.psum_scatter(
            section_one[2].astype(jnp.bfloat16), "chrom", scatter_dimension=0, tiled=True
        ).astype(jnp.float32),
        lax.psum_scatter(
            section_one[3].astype(jnp.bfloat16), "chrom", scatter_dimension=0, tiled=True
        ).astype(jnp.float32),
        lax.psum_scatter(
            section_one[4].astype(jnp.bfloat16), "chrom", scatter_dimension=0, tiled=True
        ).astype(jnp.float32),
        lax.psum_scatter(
            section_one[5].astype(jnp.bfloat16), "chrom", scatter_dimension=0, tiled=True
        ).astype(jnp.float32),
        lax.psum_scatter(
            section_one[6].astype(jnp.bfloat16), "chrom", scatter_dimension=0, tiled=True
        ).astype(jnp.float32),
        lax.psum_scatter(
            section_one[7].astype(jnp.bfloat16), "chrom", scatter_dimension=0, tiled=True
        ).astype(jnp.float32),
        lax.psum_scatter(
            section_one[8].astype(jnp.bfloat16), "chrom", scatter_dimension=0, tiled=True
        ).astype(jnp.float32),
        lax.psum_scatter(
            section_one[9].astype(jnp.bfloat16), "chrom", scatter_dimension=0, tiled=True
        ).astype(jnp.float32),
        lax.psum_scatter(
            section_one[10].astype(jnp.bfloat16), "chrom", scatter_dimension=0, tiled=True
        ).astype(jnp.float32),
        lax.psum_scatter(
            section_one[11].astype(jnp.bfloat16), "chrom", scatter_dimension=0, tiled=True
        ).astype(jnp.float32),
        lax.psum_scatter(
            section_one[12].astype(jnp.bfloat16), "chrom", scatter_dimension=0, tiled=True
        ).astype(jnp.float32),
        lax.psum_scatter(
            section_one[13].astype(jnp.bfloat16), "chrom", scatter_dimension=0, tiled=True
        ).astype(jnp.float32),
        lax.psum_scatter(
            section_one[14].astype(jnp.bfloat16), "chrom", scatter_dimension=0, tiled=True
        ).astype(jnp.float32),
    )
    rejoined = (
        lax.all_gather(section_two[0].astype(jnp.bfloat16), "cells", axis=1, tiled=True).astype(
            jnp.float32
        ),
        lax.all_gather(section_two[1].astype(jnp.bfloat16), "cells", axis=1, tiled=True).astype(
            jnp.float32
        ),
        lax.all_gather(section_two[2].astype(jnp.bfloat16), "cells", axis=1, tiled=True).astype(
            jnp.float32
        ),
        lax.all_gather(section_two[3].astype(jnp.bfloat16), "cells", axis=1, tiled=True).astype(
            jnp.float32
        ),
        lax.all_gather(section_two[4].astype(jnp.bfloat16), "cells", axis=1, tiled=True).astype(
            jnp.float32
        ),
        lax.all_gather(section_two[5].astype(jnp.bfloat16), "cells", axis=1, tiled=True).astype(
            jnp.float32
        ),
        lax.all_gather(section_two[6].astype(jnp.bfloat16), "cells", axis=1, tiled=True).astype(
            jnp.float32
        ),
        lax.all_gather(section_two[7].astype(jnp.bfloat16), "cells", axis=1, tiled=True).astype(
            jnp.float32
        ),
        lax.all_gather(section_two[8].astype(jnp.bfloat16), "cells", axis=1, tiled=True).astype(
            jnp.float32
        ),
        lax.all_gather(section_two[9].astype(jnp.bfloat16), "cells", axis=1, tiled=True).astype(
            jnp.float32
        ),
        lax.all_gather(section_two[10].astype(jnp.bfloat16), "cells", axis=1, tiled=True).astype(
            jnp.float32
        ),
        lax.all_gather(section_two[11].astype(jnp.bfloat16), "cells", axis=1, tiled=True).astype(
            jnp.float32
        ),
        lax.all_gather(section_two[12].astype(jnp.bfloat16), "cells", axis=1, tiled=True).astype(
            jnp.float32
        ),
        lax.all_gather(section_two[13].astype(jnp.bfloat16), "cells", axis=1, tiled=True).astype(
            jnp.float32
        ),
        lax.all_gather(section_two[14].astype(jnp.bfloat16), "cells", axis=1, tiled=True).astype(
            jnp.float32
        ),
    )
    final = tuple(
        (
            member.reshape(
                (member.shape[0] * member.shape[1] * member.shape[2],) + member.shape[3:]
            )
            for member in rejoined
        )
    )
    return (block_out, input_grad) + tuple(final)


def solution(mesh):
    placed = (
        P("cells", "chrom", None),
        P("cells"),
        P("cells", None),
        P("cells", "chrom", None),
        P("chrom"),
        P("chrom"),
        P("chrom", None),
        P("chrom"),
        P("chrom", None),
        P("chrom", None),
        P("chrom"),
        P("chrom", None),
        P("chrom"),
        P("chrom"),
        P("chrom"),
        P("chrom", None),
        P("chrom"),
        P("chrom", None),
        P("chrom"),
    )
    return jax.shard_map(
        local,
        mesh=mesh,
        in_specs=placed,
        out_specs=(
            P("cells", "chrom", None),
            P("cells", "chrom", None),
            P("chrom"),
            P("chrom"),
            P("chrom", None),
            P("chrom"),
            P("chrom", None),
            P("chrom", None),
            P("chrom"),
            P("chrom", None),
            P("chrom"),
            P("chrom"),
            P("chrom"),
            P("chrom", None),
            P("chrom"),
            P("chrom", None),
            P("chrom"),
        ),
        check_vma=False,
    )
```

profile of v0, /device:TPU:0, one launch (start us, length us, event | category | flops | bytes accessed | tf_op | source)
XLA Modules:
  0.0 2007.6 jit_solution(11351912896352667235)
XLA Ops:
  17.6 22.2 %all-reduce.35 = (bf16[1280]{0:T(1024)(128)(2,1)S(1)}, bf16[1280]{0:T(1024)(128)(2,1)S(1)}, bf16[1280]{0:T(1024)(128)(2,1)S(1)}, bf16[1280]{0:T(1024)(128)(2,1)S...) all-reduce(bf16[1280]{0:T(1024)(128)(2,1)S(1)} %dynamic-update-slic, ...), channel_id=1, replica_groups=mesh['cells'=8,'chrom'=4] {'chrom'}, use_global_device_ids=true, to_apply=%add.1 | all-reduce | flops 8960 | bytes 35840
  42.4 36.6 %all-gather.18.cloned.1.call-done = bf16[1280,1280]{1,0:T(8,128)(2,1)} async-done(((bf16[320,1280]{1,0:T(8,128)(2,1)}), bf16[1280,1280]{1,0:T(8,128)(2,1)}) %all-gather.18.cloned.1.call-update) | async-done | bytes 3276816 | tf_op jit(solution)/shard_map/all_gather | solution.py:86
  83.9 60.9 %all-gather.12.cloned.1.call-done = bf16[1280,1280]{1,0:T(8,128)(2,1)} async-done(((bf16[320,1280]{1,0:T(8,128)(2,1)}), bf16[1280,1280]{1,0:T(8,128)(2,1)}) %all-gather.12.cloned.1.call-update) | async-done | bytes 3276816 | tf_op jit(solution)/shard_map/all_gather | solution.py:87
  169.2 41.8 %all-gather.16.cloned.1.call-done = bf16[1280,1280]{1,0:T(8,128)(2,1)} async-done(((bf16[320,1280]{1,0:T(8,128)(2,1)}), bf16[1280,1280]{1,0:T(8,128)(2,1)}) %all-gather.16.cloned.1.call-update) | async-done | bytes 3276816 | tf_op jit(solution)/shard_map/all_gather | solution.py:84
  219.9 89.9 %all-gather.20.cloned.1.call-done = bf16[2,1024,1280]{2,1,0:T(8,128)(2,1)} async-done(((bf16[2,256,1280]{2,1,0:T(8,128)(2,1)}), bf16[2,1024,1280]{2,1,0:T(8,128)(2,1)}) %all-gather.20.cloned.1.call-update) | async-done | bytes 5242896 | tf_op jit(solution)/shard_map/all_gather | solution.py:109
  317.7 19.9 fusion.75
  337.6 70.6 %all-gather.14.cloned.1.call-done = bf16[2,1024,1280]{2,1,0:T(8,128)(2,1)} async-done(((bf16[2,256,1280]{2,1,0:T(8,128)(2,1)}), bf16[2,1024,1280]{2,1,0:T(8,128)(2,1)}) %all-gather.14.cloned.1.call-update) | async-done | bytes 5242896 | tf_op jit(solution)/shard_map/all_gather | solution.py:112
  416.2 18.0 fusion
  434.1 15.8 fusion.45
  451.6 22.1 %all-gather.22.cloned.1.call-done = bf16[1280,1280]{1,0:T(8,128)(2,1)} async-done(((bf16[320,1280]{1,0:T(8,128)(2,1)}), bf16[1280,1280]{1,0:T(8,128)(2,1)}) %all-gather.22.cloned.1.call-update) | async-done | bytes 3276816 | tf_op jit(solution)/shard_map/all_gather | solution.py:89
  480.4 220.3 %all-gather.24.cloned.1.call-done = bf16[1280,5120]{1,0:T(8,128)(2,1)} async-done(((bf16[320,5120]{1,0:T(8,128)(2,1)}), bf16[1280,5120]{1,0:T(8,128)(2,1)}) %all-gather.24.cloned.1.call-update) | async-done | bytes 13107216 | tf_op jit(solution)/shard_map/all_gather | solution.py:93
  700.7 34.5 %fusion.9 = (bf16[5120,512]{0,1:T(8,128)(2,1)}, f32[512,5120]{1,0:T(8,128)}) fusion(f32[5120]{0:T(1024)S(1)} %bitcast.285, bf16[1280,5120]{1,0:T(8,128)(2,1)} %all-gather.24.cloned.1.call-done, f32[512,1280]{1,0:T(8,128)} %copy-done.3, f32[1280]{0:T(1024)S(1)} %convert_element_type.286, f32[1280]{0:T(1024)S(1)} %convert_element_type.285, ...), kind=kOutput, calls=%fused_computation.18 | convolution fusion | flops 6887178240 | bytes 31492096 | tf_op jit(solution)/shard_map/dot_general | solution.py:25
  735.2 192.1 %all-gather.26.cloned.1.call-done = bf16[5120,1280]{1,0:T(8,128)(2,1)} async-done(((bf16[1280,1280]{1,0:T(8,128)(2,1)}), bf16[5120,1280]{1,0:T(8,128)(2,1)}) %all-gather.26.cloned.1.call-update) | async-done | bytes 13107216 | tf_op jit(solution)/shard_map/all_gather | solution.py:95
  927.3 36.3 %fusion.69 = (bf16[5120]{0:T(1024)(128)(2,1)}, bf16[512,5120]{1,0:T(8,128)(2,1)}, f32[512,5120]{1,0:T(8,128)}) fusion(f32[512,5120]{1,0:T(8,128)} %get-tuple-element.80, f32[5120]{0:T(1024)S(1)} %bitcast.286, bf16[512,1280]{1,0:T(8,128)(2,1)} %bitcast_select_fusion, bf16[5120,1280]{1,0:T(8,128)(2,1)} %all-gather.26.cloned.1.call-done), kind=kOutput, calls=%fused_computation.174 | convolution fusion | flops 6904867840 | bytes 40663040 | tf_op jit(solution)/shard_map/rb,ab->ra/dot_general | solution.py:33
  963.6 14.9 multiply_reduce_fusion.1
  994.5 29.8 %multiply_reduce_fusion = (f32[2,20,256]{2,1,0:T(8,128)S(1)}, f32[2,20,256,1024]{3,2,1,0:T(8,128)}) fusion(f32[2,20,256,1024]{3,2,1,0:T(8,128)} %get-tuple-element.70, f32[2,20,256]{2,1,0:T(8,128)S(1)} %copy-done.21, bf16[2,1024,20,64]{1,3,2,0:T(8,128)(2,1)} %bitcast.249, bf16[2,256,20,64]{1,0,3,2:T(2,128)(2,1)} %reshape.349), kind=kOutput, calls=%fused_computation.1 | convolution fusion | flops 1373624320 | bytes 90521600 | tf_op jit(solution)/shard_map/cqhd,ckhd->chqk/dot_general | solution.py:175
  1024.3 34.0 %multiply_convert_fusion = bf16[2,20,256,1024]{3,2,1,0:T(8,128)(2,1)} fusion(f32[2,20,256,1024]{3,2,1,0:T(8,128)} %get-tuple-element.75, f32[2,20,256,1024]{3,2,1,0:T(8,128)} %get-tuple-element.70, f32[2,20,256]{2,1,0:T(8,128)S(1)} %get-tuple-element.74, f32[2,20,256]{2,1,0:T(8,128)S(1)} %copy-done.21), kind=kLoop, calls=%fused_computation | loop fusion | flops 41943040 | bytes 104939520 | tf_op jit(solution)/shard_map/convert_element_type | solution.py:179
  1071.8 19.4 fusion.36
  1170.9 89.4 %reduce-scatter.19.cloned.1.call-done = bf16[2,256,1280]{1,2,0:T(8,128)(2,1)} async-done(((bf16[2,1024,1280]{1,2,0:T(8,128)(2,1)}), bf16[2,256,1280]{1,2,0:T(8,128)(2,1)}) %reduce-scatter.19.cloned.1.call-update) | async-done | bytes 1310736 | tf_op jit(solution)/shard_map/reduce_scatter | solution.py:202
  1268.1 463.1 %all-reduce.38.cloned.1.call-done = (bf16[4,8,40,1280]{3,2,1,0:T(8,128)(2,1)}, bf16[4,8,40,1280]{3,2,1,0:T(8,128)(2,1)}, bf16[4,8,40,1280]{3,2,1,0:T(8,128)(2,1)...) async-done(((bf16[4,8,40,1280]{3,2,1,0:T(8,128)(2,1)}, bf16[4,8,40,1280]{3,2,1,0:T(8,128)(2,1)}, ...) | async-done | bytes 39321616
  1779.7 25.8 %all-reduce.32 = (bf16[4,8,40]{2,0,1:T(4,128)(2,1)S(1)}, bf16[4,8,40]{2,0,1:T(4,128)(2,1)S(1)}, bf16[4,8,40]{2,0,1:T(4,128)(2,1)S(1)}, bf16[4,8,40]{2,0,1:T(4,12...) all-reduce(bf16[4,8,40]{2,0,1:T(4,128)(2,1)S(1)} %copy.162, ...), channel_id=4, replica_groups=mesh['cells'=8,'chrom'=4] {'cells'}, use_global_device_ids=true, to_apply=%region_15.16.clone | all-reduce | flops 15360 | bytes 61440
  1808.9 17.3 all-reduce.34
  1888.7 19.5 fusion.39
  1949.7 14.2 all_gather.117
  (332 shorter events, 383.2 us)
Async XLA Ops:
  7.2 71.8 %all-gather.18.cloned.1.call-start = ((), (), s32[]{:S(2)}) async-start(), calls=%async_computation.11 | async-start | bytes 4096000 | tf_op jit(solution)/shard_map/all_gather | solution.py:86
  7.9 136.9 %all-gather.12.cloned.1.call-start = ((), (), s32[]{:S(2)}) async-start(), calls=%async_computation.8 | async-start | bytes 4096000 | tf_op jit(solution)/shard_map/all_gather | solution.py:87
  8.7 202.3 %all-gather.16.cloned.1.call-start = ((), (), s32[]{:S(2)}) async-start(), calls=%async_computation.10 | async-start | bytes 4096000 | tf_op jit(solution)/shard_map/all_gather | solution.py:84
  9.4 300.3 %all-gather.20.cloned.1.call-start = ((), (), s32[]{:S(2)}) async-start(), calls=%async_computation.12 | async-start | bytes 6553600 | tf_op jit(solution)/shard_map/all_gather | solution.py:109
  83.9 324.4 %all-gather.14.cloned.1.call-start = ((), (), s32[]{:S(2)}) async-start(), calls=%async_computation.9 | async-start | bytes 6553600 | tf_op jit(solution)/shard_map/all_gather | solution.py:112
  149.7 324.0 %all-gather.22.cloned.1.call-start = ((), (), s32[]{:S(2)}) async-start(), calls=%async_computation.13 | async-start | bytes 4096000 | tf_op jit(solution)/shard_map/all_gather | solution.py:89
  150.3 550.4 %all-gather.24.cloned.1.call-start = ((), (), s32[]{:S(2)}) async-start(), calls=%async_computation.14 | async-start | bytes 16384000 | tf_op jit(solution)/shard_map/all_gather | solution.py:93
  151.1 776.2 %all-gather.26.cloned.1.call-start = ((), (), s32[]{:S(2)}) async-start(), calls=%async_computation.15 | async-start | bytes 16384000 | tf_op jit(solution)/shard_map/all_gather | solution.py:95
  151.9 1012.0 %reduce-scatter.17.cloned.1.call-start = ((), (), s32[]{:S(2)}) async-start(), calls=%async_computation.16 | async-start | bytes 6553600 | tf_op jit(solution)/shard_map/reduce_scatter | solution.py:196
  167.8 759.5 %copy-start.28 = (f32[4,1,1280]{2,1,0:T(1,128)}, f32[4,1,1280]{2,1,0:T(1,128)S(1)}, u32[]{:S(2)}) copy-start(f32[4,1,1280]{2,1,0:T(1,128)S(1)} %convert_element_type.328) | copy-start | bytes 61444
  167.8 532.9 %copy-start.38 = (f32[1280]{0:T(1024)}, f32[1280]{0:T(1024)S(1)}, u32[]{:S(2)}) copy-start(f32[1280]{0:T(1024)S(1)} %convert_element_type.286) | copy-start | bytes 15364
  479.8 255.4 %copy-start.30 = (f32[512]{0:T(512)}, f32[512]{0:T(512)S(1)}, u32[]{:S(2)}) copy-start(f32[512]{0:T(512)S(1)} %multiply_reduce_fusion.5) | copy-start | bytes 6148
  1071.8 188.6 %reduce-scatter.19.cloned.1.call-start = ((), (), s32[]{:S(2)}) async-start(), calls=%async_computation.17 | async-start | bytes 6553600 | tf_op jit(solution)/shard_map/reduce_scatter | solution.py:202
  1091.2 639.9 %all-reduce.38.cloned.1.call-start = ((), (), s32[]{:S(2)}) async-start(), calls=%async_computation.26 | async-start | bytes 78643200
  1266.9 504.2 %reduce-scatter.29.cloned.1.call-start = ((), (), s32[]{:S(2)}) async-start(), calls=%async_computation.22 | async-start | bytes 2048000 | tf_op jit(solution)/shard_map/reduce_scatter | solution.py:326
  1734.5 173.7 %reduce-scatter.31.cloned.1.call-start = ((), (), s32[]{:S(2)}) async-start(), calls=%async_computation.24 | async-start | bytes 2048000 | tf_op jit(solution)/shard_map/reduce_scatter | solution.py:332
  1737.9 198.4 %reduce-scatter.21.cloned.1.call-start = ((), (), s32[]{:S(2)}) async-start(), calls=%async_computation.18 | async-start | bytes 512000 | tf_op jit(solution)/shard_map/reduce_scatter | solution.py:299
  1740.5 209.2 %reduce-scatter.23.cloned.1.call-start = ((), (), s32[]{:S(2)}) async-start(), calls=%async_computation.19 | async-start | bytes 512000 | tf_op jit(solution)/shard_map/reduce_scatter | solution.py:305
  1743.1 220.8 %reduce-scatter.25.cloned.1.call-start = ((), (), s32[]{:S(2)}) async-start(), calls=%async_computation.20 | async-start | bytes 512000 | tf_op jit(solution)/shard_map/reduce_scatter | solution.py:308
  1745.6 229.1 %reduce-scatter.27.cloned.1.call-start = ((), (), s32[]{:S(2)}) async-start(), calls=%async_computation.21 | async-start | bytes 512000 | tf_op jit(solution)/shard_map/reduce_scatter | solution.py:314
  1748.5 241.7 %all-gather.28.cloned.1.call-start = ((), (), s32[]{:S(2)}) async-start(), calls=%async_computation.23 | async-start | bytes 3686400 | tf_op jit(solution)/shard_map/all_gather | solution.py:373
  1771.1 224.6 %all-gather.30.cloned.1.call-start = ((), (), s32[]{:S(2)}) async-start(), calls=%async_computation.25 | async-start | bytes 3686400 | tf_op jit(solution)/shard_map/all_gather | solution.py:379
  1776.5 112.1 %copy-start.29 = (f32[4,1,1280]{2,1,0:T(1,128)S(1)}, f32[4,1,1280]{2,1,0:T(1,128)}, u32[]{:S(2)}) copy-start(f32[4,1,1280]{2,1,0:T(1,128)} %copy-done.28) | copy-start | bytes 61444
  1776.5 112.1 %copy-start.42 = (pred[512]{0:T(512)(128)(4,1)S(1)}, pred[512]{0:T(512)(128)(4,1)}, u32[]{:S(2)}) copy-start(pred[512]{0:T(512)(128)(4,1)} %copy-done.40) | copy-start | bytes 1540
  (51 other events, 755.7 us)
Sparse Core Ops, SparseCore 0:
  9.6 69.3 all-gather.17
  80.6 64.2 all-gather.11
  146.4 64.5 all-gather.15
  213.0 96.7 all-gather.19
  311.8 96.4 all-gather.13
  409.6 64.0 all-gather.21
  475.3 225.3 all-gather.23
  702.3 224.9 all-gather.25
  1071.9 91.9 reduce-scatter.16
  1166.0 94.2 reduce-scatter.18
  1267.0 464.1 all-reduce.37
  1734.6 36.4 reduce-scatter.28
  1774.1 35.3 reduce-scatter.30
  1812.2 19.7 reduce-scatter.20
  1834.8 19.1 reduce-scatter.22
  1856.7 19.0 reduce-scatter.24
  1878.0 19.1 reduce-scatter.26
  1898.9 31.1 all-gather.27
  1932.0 35.7 all-gather.29
where the time goes:
time: 2010 us
  waiting for transfers between devices  1310 us (65%)
  matrix products  295 us (15%)
  blocking collectives  202 us (10%)
  local copies, waits for them, and re-layouts  95 us (5%)
  other arithmetic  85.5 us (4%)
    unnamed x20, waiting for transfers between devices  467 us
    all_gather x1, waiting for transfers between devices, local(): lax.all_gather(inner_proj, 'chrom', axis=0, tiled=True)  220 us
    all_gather x1, waiting for transfers between devices, local(): lax.all_gather(outer_proj, 'chrom', axis=0, tiled=True)  192 us
    all_gather x1, waiting for transfers between devices, local(): lax.all_gather(key_rows.reshape(cells_here, tokens_here, feat_width), 'ch...  89.9 us
    reduce_scatter x1, waiting for transfers between devices, local(): lax.psum_scatter(grad_vals_part.reshape(cells_here, seq_len, feat_width)....  89.4 us
    dot_general x6, matrix products, product(): return jnp.dot(left, right, preferred_element_type=jnp.float32)  72 us
    dot_general x6, matrix products, right_back(): jnp.einsum('rb,ab->ra', left, right, preferred_element_type=jnp.float32)  71.1 us
    all_gather x1, waiting for transfers between devices, local(): lax.all_gather(vals.reshape(cells_here, tokens_here, feat_width), 'chrom'...  70.6 us
  transfers between devices with their start and end apart: 19, of which 12 were waited for; matrix products, arithmetic and copies ran while one was open for 15% of the time, Pallas kernels for 0%

commit v1 on v0

--- a/solution.py
+++ b/solution.py
@@ -1,6 +1,10 @@
+import functools
+
 import jax
 import jax.numpy as jnp
 from jax import lax
+from jax.experimental import pallas as pl
+from jax.experimental.pallas import tpu as pltpu
 from jax.sharding import PartitionSpec as P
 
 HEADS = 20
@@ -43,7 +47,7 @@
     )
 
 
-def local(
+def general(
     inputs,
     lengths,
     offsets,
@@ -394,7 +398,501 @@
     return (block_out, input_grad) + tuple(final)
 
 
+PLANE = 4
+LINE = 4
+
+
+def rows_of(start, count):
+    return pl.ds(pl.multiple_of(start, 16), count)
+
+
+def cols_of(start, count):
+    return pl.ds(pl.multiple_of(start, 128), count)
+
+
+def gather_kernel(
+    small_ref, x_ref, ct_ref, wq_ref, wk_ref, wv_ref, wo_ref, w1_ref, w2_ref,
+    smalls, xf, cf, wa, wb, wc, wob,
+    sm_s, sm_r, ex_s, ex_r, fw_s, fw_r, un_s, un_r, loc, wo_s, wo_r,
+):
+    i, z = lax.axis_index("cells"), lax.axis_index("chrom")
+    p, c = i // 2, lax.rem(i, 2)
+    px, py = lax.rem(p, 2), p // 2
+    x_nb, y_nb, core_nb = i + 2 - 4 * px, i + 4 - 8 * py, i + 1 - 2 * c
+    p_x, p_y = p + 1 - 2 * px, p + 2 - 4 * py
+    right = lax.rem(z + 1, LINE)
+    rows = wq_ref.shape[0]
+    feat = wq_ref.shape[1]
+    half = feat // 2
+    hid = w2_ref.shape[0]
+    block = x_ref.shape[1]
+    part, hid_part = rows // PLANE, hid // 2 // PLANE
+
+    barrier = pltpu.get_barrier_semaphore()
+    line_ids = [
+        (i - c + lax.rem(c + dc, 2), lax.rem(z + dz, LINE))
+        for dc in range(2)
+        for dz in range(LINE)
+        if dc or dz
+    ]
+    for who in line_ids + [(x_nb, z), (y_nb, z)]:
+        pl.semaphore_signal(barrier, inc=1, device_id=who, device_id_type=pl.DeviceIdType.MESH)
+    pl.semaphore_wait(barrier, len(line_ids) + 2)
+
+    def send(src, dst, s, r, who):
+        return pltpu.make_async_remote_copy(
+            src_ref=src, dst_ref=dst, send_sem=s, recv_sem=r, device_id=who,
+            device_id_type=pl.DeviceIdType.MESH,
+        )
+
+    small_own = pltpu.make_async_copy(small_ref, smalls.at[z], loc.at[0])
+    small_out = [
+        send(small_ref, smalls.at[z], sm_s.at[d], sm_r.at[d], (i, lax.rem(z + d + 1, LINE)))
+        for d in range(LINE - 1)
+    ]
+
+    def exchange(src, dst, which):
+        stay = c == z // 2
+        mine, outs = None, []
+        for k in range(2):
+            j = lax.rem(z + k, 2)
+            to = dst.at[rows_of(z * block, block), :]
+            r = ex_r.at[2 * which + k]
+            outs.append(send(src.at[j], to, ex_s.at[2 * which + k], r, (i - c + z // 2, 2 * c + j)))
+            if k == 0:
+                mine = pltpu.make_async_copy(src.at[j], to, r)
+
+        def start():
+            pl.when(stay)(mine.start)
+            pl.when(jnp.logical_not(stay))(outs[0].start)
+            outs[1].start()
+
+        def arrived():
+            pl.when(stay)(mine.wait)
+            pl.when(jnp.logical_not(stay))(outs[0].wait_recv)
+            outs[1].wait_recv()
+
+        def sent():
+            pl.when(jnp.logical_not(stay))(outs[0].wait_send)
+            outs[1].wait_send()
+
+        return start, arrived, sent
+
+    def forward(dst, which):
+        return [
+            send(
+                dst.at[rows_of((2 * c + b) * block, block), :],
+                dst.at[rows_of((2 * c + b) * block, block), :],
+                fw_s.at[2 * which + b], fw_r.at[2 * which + b], (core_nb, z),
+            )
+            for b in range(2)
+        ]
+
+    x_start, x_arrived, x_sent = exchange(x_ref, xf, 0)
+    c_start, c_arrived, c_sent = exchange(ct_ref, cf, 1)
+    x_fw, c_fw = forward(xf, 0), forward(cf, 1)
+
+    lands = (wa, wb, wc)
+
+    def own_parts(g, row, count):
+        if g == 0:
+            return [
+                (ref.at[rows_of(row, count), cols_of(c * half, half)], cols_of(n * half, half))
+                for n, ref in enumerate((wq_ref, wk_ref, wv_ref, wo_ref))
+            ]
+        if g == 1:
+            return [
+                (w1_ref.at[rows_of(row, count), cols_of(n * hid + c * (hid // 2), hid // 2)], cols_of(n * (hid // 2), hid // 2))
+                for n in range(LINE)
+            ]
+        return [(w2_ref.at[rows_of(c * (hid // 2) + row, count), :], pl.ds(0, feat))]
+
+    def shape_of(g):
+        return (rows, part) if g < 2 else (hid // 2, hid_part)
+
+    def piece(g, s, at):
+        shard, count = shape_of(g)
+        return lands[g].at[rows_of(s * shard + at * count, count), :]
+
+    def half_piece(g, s, at, side):
+        shard, count = shape_of(g)
+        width = lands[g].shape[1] // 2
+        return lands[g].at[rows_of(s * shard + at * count, count), pl.ds(side * width, width)]
+
+    def shard_at(k):
+        return lax.rem(z - k + LINE, LINE)
+
+    class Unit:
+        def __init__(self, g, k):
+            self.g, self.k, self.n = g, k, g * (LINE - 1) + k - 1
+
+        def sems(self, e):
+            return un_s.at[self.n, e], un_r.at[self.n, e]
+
+        def turn(self):
+            s = shard_at(self.k - 1)
+            return send(piece(self.g, s, p), piece(self.g, s, p), *self.sems(0), (i, right))
+
+        def turn_start(self):
+            if self.k > 1:
+                self.turn().start()
+                return
+            shard, count = shape_of(self.g)
+            for src, cols in own_parts(self.g, p * count, count):
+                dst = lands[self.g].at[rows_of(z * shard + p * count, count), cols]
+                send(src, dst, *self.sems(0), (i, right)).start()
+
+        def spread(self):
+            s = shard_at(self.k)
+            own = piece(self.g, s, p)
+            return [
+                send(own, own, *self.sems(1), (x_nb, z)),
+                send(own, own, *self.sems(2), (y_nb, z)),
+            ]
+
+        def cross(self):
+            s = shard_at(self.k)
+            left = half_piece(self.g, s, p_x, 0)
+            rest = half_piece(self.g, s, p_y, 1)
+            return [
+                send(left, left, *self.sems(3), (y_nb, z)),
+                send(rest, rest, *self.sems(4), (x_nb, z)),
+            ]
+
+        def arrived(self):
+            self.turn().wait_recv()
+
+        def spread_start(self):
+            for d in self.spread():
+                d.start()
+
+        def cross_start(self):
+            for d in self.spread():
+                d.wait_recv()
+            for d in self.cross():
+                d.start()
+
+        def done(self):
+            for d in self.cross():
+                d.wait_recv()
+
+        def sent(self):
+            for d in [self.turn()] + self.spread() + self.cross():
+                d.wait_send()
+
+    a, b, w = ([Unit(g, k) for k in range(1, LINE)] for g in range(3))
+
+    def own_start(g):
+        shard, _ = shape_of(g)
+        for src, cols in own_parts(g, 0, shard):
+            pltpu.make_async_copy(src, lands[g].at[rows_of(z * shard, shard), cols], loc.at[1 + g]).start()
+
+    def own_wait(g):
+        shard, _ = shape_of(g)
+        ref = lands[g].at[rows_of(z * shard, shard), :]
+        pltpu.make_async_copy(ref, ref, loc.at[1 + g]).wait()
+
+    small_own.start()
+    for d in small_out:
+        d.start()
+    a[0].turn_start()
+    x_start()
+    for g in range(3):
+        own_start(g)
+    a[0].arrived()
+    a[1].turn_start()
+    a[0].spread_start()
+    b[0].turn_start()
+    a[1].arrived()
+    a[2].turn_start()
+    a[1].spread_start()
+    a[0].cross_start()
+    x_arrived()
+    for d in x_fw:
+        d.start()
+    a[2].arrived()
+    a[2].spread_start()
+    b[0].arrived()
+    b[1].turn_start()
+    b[0].spread_start()
+    a[1].cross_start()
+    a[2].cross_start()
+    b[1].arrived()
+    b[2].turn_start()
+    w[0].turn_start()
+    b[1].spread_start()
+    b[0].cross_start()
+    for u in a:
+        u.done()
+    own_wait(0)
+    wo_own = pltpu.make_async_copy(
+        wa.at[rows_of(c * half, half), pl.ds(3 * half, half)], wob.at[:, cols_of(c * half, half)], loc.at[4]
+    )
+    wo_out = send(
+        wa.at[rows_of((1 - c) * half, half), pl.ds(3 * half, half)],
+        wob.at[:, cols_of(c * half, half)], wo_s.at[0], wo_r.at[0], (core_nb, z),
+    )
+    wo_own.start()
+    wo_out.start()
+    b[2].arrived()
+    b[2].spread_start()
+    w[0].arrived()
+    w[1].turn_start()
+    w[0].spread_start()
+    c_start()
+    b[1].cross_start()
+    b[2].cross_start()
+    w[1].arrived()
+    w[2].turn_start()
+    w[1].spread_start()
+    w[0].cross_start()
+    w[2].arrived()
+    w[2].spread_start()
+    w[1].cross_start()
+    c_arrived()
+    for d in c_fw:
+        d.start()
+    w[2].cross_start()
+    for u in b + w:
+        u.done()
+    for g in (1, 2):
+        own_wait(g)
+    small_own.wait()
+    wo_own.wait()
+    for d in small_out + x_fw + c_fw + [wo_out]:
+        d.wait()
+    x_sent()
+    c_sent()
+    for u in a + b + w:
+        u.sent()
+
+
+def gather_all(small, x, ct, wq, wk, wv, wo, w1, w2):
+    rows, feat = wq.shape
+    hid = w2.shape[0]
+    seq = x.shape[1] * LINE
+    bf = jnp.bfloat16
+    dma = pltpu.SemaphoreType.DMA
+    anywhere = pl.BlockSpec(memory_space=pl.ANY)
+    return pl.pallas_call(
+        gather_kernel,
+        out_shape=(
+            jax.ShapeDtypeStruct((LINE,) + small.shape, bf),
+            jax.ShapeDtypeStruct((seq, feat), bf),
+            jax.ShapeDtypeStruct((seq, feat), bf),
+            jax.ShapeDtypeStruct((rows * LINE, 2 * feat), bf),
+            jax.ShapeDtypeStruct((rows * LINE, hid * LINE // 2), bf),
+            jax.ShapeDtypeStruct((hid * LINE // 2, feat), bf),
+            jax.ShapeDtypeStruct((feat // 2, feat), bf),
+        ),
+        in_specs=[anywhere] * 9,
+        out_specs=(anywhere,) * 7,
+        scratch_shapes=[
+            dma((3,)), dma((3,)), dma((4,)), dma((4,)), dma((4,)), dma((4,)),
+            dma((9, 5)), dma((9, 5)), dma((5,)), dma((1,)), dma((1,)),
+        ],
+        compiler_params=pltpu.CompilerParams(collective_id=0, has_side_effects=True),
+        name="gather_all",
+    )(small, x, ct, wq, wk, wv, wo, w1, w2)
+
+
+def flip(value, step):
+    count = lax.axis_size("cells")
+    return lax.ppermute(value, "cells", [(n, n ^ step) for n in range(count)])
+
+
+def take(value, index, axis):
+    return lax.dynamic_index_in_dim(value, index, axis, keepdims=False)
+
+
+def plus(left, right):
+    return (left.astype(jnp.float32) + right.astype(jnp.float32)).astype(jnp.bfloat16)
+
+
+def plane_sum(value, px, py):
+    two = value.reshape((2, LINE // 2, 2, 2) + value.shape[2:])
+    first, later = two[0], two[1]
+    first = plus(take(first, px, 2), flip(take(first, 1 - px, 2), 2))
+    later = plus(take(later, py, 1), flip(take(later, 1 - py, 1), 4))
+    first = plus(take(first, py, 1), flip(take(first, 1 - py, 1), 4))
+    later = plus(take(later, px, 1), flip(take(later, 1 - px, 1), 2))
+    return jnp.concatenate([first, later], axis=0)
+
+
+def reduce_group(value, px, py):
+    mine = plane_sum(value, px, py)
+    summed = lax.psum_scatter(mine, "chrom", scatter_dimension=0, tiled=True)[0]
+    whole = lax.all_gather(summed, "cells", axis=0, tiled=False)
+    return whole.reshape((PLANE, 2) + summed.shape)
+
+
+def send_home(value, core, place):
+    half, feat = value.shape
+    two = value.reshape(2, half // 2, feat)
+    got = []
+    for k in range(2):
+        pairs = []
+        for cells in range(lax.axis_size("cells")):
+            for z in range(LINE):
+                home, c = cells - cells % 2, cells % 2
+                to_z = 2 * c + (z + k) % 2
+                pairs.append((cells * LINE + z, (home + z // 2) * LINE + to_z))
+        block = take(two, lax.rem(place + k, 2), 0)
+        got.append(lax.ppermute(block, ("cells", "chrom"), pairs))
+    even = lax.rem(place, 2) == 0
+    return jnp.stack([jnp.where(even, got[0], got[1]), jnp.where(even, got[1], got[0])])
+
+
+def paired_local(
+    inputs, lengths, offsets, cotangent, norm_gain, norm_shift, query_proj, query_bias, key_proj, value_proj,
+    value_bias, output_proj, output_bias, second_gain, second_shift, inner_proj, inner_bias, outer_proj, outer_bias,
+):
+    f32, bf = jnp.float32, jnp.bfloat16
+    i, z = lax.axis_index("cells"), lax.axis_index("chrom")
+    p, c = i // 2, i % 2
+    px, py = p % 2, p // 2
+    cells_here, block, feat = inputs.shape
+    seq = block * LINE
+    half_seq, half = seq // 2, feat // 2
+    rows = feat // LINE
+    hid = outer_proj.shape[0]
+    inv_root = HEAD_DIM ** (-0.5)
+    heads = HEADS // 2
+
+    vectors = (norm_gain, norm_shift, query_bias, value_bias, output_bias, second_gain, second_shift, outer_bias)
+    small = jnp.concatenate([v.reshape(1, rows) for v in vectors] + [inner_bias.reshape(hid // rows, rows)], axis=0)
+    small = jnp.pad(small, ((0, 16 - small.shape[0]), (0, 384 - rows)))
+    smalls, xf, cf, wa, wb, wc, wob = gather_all(
+        small, inputs, cotangent, query_proj, key_proj, value_proj, output_proj, inner_proj, outer_proj
+    )
+    flat = smalls[:, :8, :rows].astype(f32).transpose(1, 0, 2).reshape(8, feat)
+    gain_one, shift_one, bias_q, bias_v, bias_o, gain_two, shift_two, bias_out = (flat[n] for n in range(8))
+    bias_in = lax.dynamic_slice_in_dim(smalls[:, 8:12, :rows], 2 * c, 2, 1).astype(f32).reshape(2 * hid)
+    bias_q = lax.dynamic_slice_in_dim(bias_q, c * half, half, 0)
+    bias_v = lax.dynamic_slice_in_dim(bias_v, c * half, half, 0)
+
+    ragged = jnp.concatenate([lengths[:, None], offsets], axis=1)
+    other = flip(ragged, 1)
+    ragged = take(jnp.where(z // 2 == c, ragged, other), z % 2, 0)
+    length, starts = ragged[0], ragged[1:]
+    places = jnp.arange(seq, dtype=jnp.int32)
+    live = places < length
+    groups = jnp.sum((places[:, None] >= starts[None, :]).astype(jnp.int32), axis=1)
+    bias = jnp.where(live[None, :], group_bias * (groups[:, None] == groups[None, :]).astype(f32), -jnp.inf)
+
+    states = xf.astype(f32)
+    normed_full, norm_back = jax.vjp(layer_norm, states, gain_one, shift_one)
+    normed = normed_full.astype(bf)
+    qkv = product(normed, wa[:, : 3 * half])
+    queries = (qkv[:, :half] + bias_q).astype(bf)
+    key_rows = qkv[:, half : 2 * half].astype(bf)
+    vals = (qkv[:, 2 * half :] + bias_v).astype(bf)
+    qh = queries.reshape(seq, heads, HEAD_DIM)
+    kh = key_rows.reshape(seq, heads, HEAD_DIM)
+    vh = vals.reshape(seq, heads, HEAD_DIM)
+
+    def scores_of():
+        raw = jnp.einsum("qhd,khd->hqk", qh, kh, preferred_element_type=f32) * inv_root
+        return raw + bias[None]
+
+    masked = scores_of()
+    row_max = jnp.max(masked, axis=-1, keepdims=True)
+    exp_scores = jnp.exp(masked - row_max)
+    exp_total = jnp.sum(exp_scores, axis=-1, keepdims=True)
+    log_total = row_max + jnp.log(exp_total)
+    probs = (exp_scores / exp_total).astype(bf)
+    mixed = jnp.einsum("hqk,khd->qhd", probs, vh, preferred_element_type=f32).astype(bf).reshape(seq, half)
+    part = product(mixed, wob).astype(bf)
+    attended = part.astype(f32) + flip(part, 1).astype(f32) + bias_o
+    middle = states + attended
+    second_full, second_back = jax.vjp(layer_norm, middle, gain_two, shift_two)
+    second = second_full.astype(bf)
+    inner = product(second, wb) + bias_in
+    active_full, gelu_back = jax.vjp(gelu_exact, inner)
+    active = active_full.astype(bf)
+    upstream = jnp.where(live[:, None], cf, jnp.zeros((), bf))
+    out_part = product(active, wc)
+    mine = lax.dynamic_slice_in_dim(out_part, c * half_seq, half_seq, 0)
+    theirs = lax.dynamic_slice_in_dim(out_part, (1 - c) * half_seq, half_seq, 0).astype(bf)
+    result = (
+        lax.dynamic_slice_in_dim(middle, c * half_seq, half_seq, 0) + mine + flip(theirs, 1).astype(f32) + bias_out
+    )
+    live_half = lax.dynamic_slice_in_dim(live, c * half_seq, half_seq, 0)
+    block_out = send_home(jnp.where(live_half[:, None], result, 0.0).astype(bf), c, z)
+
+    outer_grad = left_product(active, upstream).astype(bf)
+    outer_sum = reduce_group(outer_grad.reshape(LINE, PLANE, hid // 2 // PLANE, feat), px, py)
+    (grad_inner_full,) = gelu_back(right_back(upstream, wc))
+    grad_inner = grad_inner_full.astype(bf)
+    inner_grad = left_product(second, grad_inner).astype(bf)
+    inner_sum = reduce_group(inner_grad.reshape(LINE, PLANE, rows // PLANE, 2 * hid), px, py)
+    second_part = right_back(grad_inner, wb).astype(bf)
+    grad_second = second_part.astype(f32) + flip(second_part, 1).astype(f32)
+    grad_norm, gain_two_grad, shift_two_grad = second_back(grad_second)
+    grad_middle = upstream.astype(f32) + grad_norm
+    grad_attended = grad_middle.astype(bf)
+    out_grad = left_product(mixed, grad_attended).astype(bf)
+    grad_mixed = right_back(grad_attended, wob).astype(bf)
+    gh = grad_mixed.reshape(seq, heads, HEAD_DIM)
+    again = jnp.exp(scores_of() - log_total)
+    grad_probs = jnp.einsum("qhd,khd->hqk", gh, vh, preferred_element_type=f32)
+    row_dot = jnp.sum(again * grad_probs, axis=-1, keepdims=True)
+    grad_raw = (again * (grad_probs - row_dot)).astype(bf)
+    dv = jnp.einsum("hqk,qhd->khd", again.astype(bf), gh, preferred_element_type=f32).astype(bf).reshape(seq, half)
+    dk = (jnp.einsum("hqk,qhd->khd", grad_raw, qh, preferred_element_type=f32) * inv_root).astype(bf).reshape(seq, half)
+    dq = (jnp.einsum("hqk,khd->qhd", grad_raw, kh, preferred_element_type=f32) * inv_root).astype(bf).reshape(seq, half)
+    dqkv = jnp.concatenate([dq, dk, dv], axis=1)
+    qkv_grad = left_product(normed, dqkv).astype(bf)
+    keep = lax.dynamic_slice_in_dim(out_grad, c * half, half, 1)
+    swap = flip(lax.dynamic_slice_in_dim(out_grad, (1 - c) * half, half, 1), 1)
+    out_cols = jnp.where(c == 0, jnp.concatenate([keep, swap], 0), jnp.concatenate([swap, keep], 0))
+    attn_grad = jnp.concatenate([qkv_grad, out_cols], axis=1)
+    attn_sum = reduce_group(attn_grad.reshape(LINE, PLANE, rows // PLANE, 2 * feat), px, py)
+    normed_part = right_back(dqkv, wa[:, : 3 * half])
+    mine = lax.dynamic_slice_in_dim(normed_part, c * half_seq, half_seq, 0)
+    theirs = lax.dynamic_slice_in_dim(normed_part, (1 - c) * half_seq, half_seq, 0).astype(bf)
+    grad_normed = mine + flip(theirs, 1).astype(f32)
+    states_half = lax.dynamic_slice_in_dim(states, c * half_seq, half_seq, 0)
+    _, half_back = jax.vjp(layer_norm, states_half, gain_one, shift_one)
+    grad_states, gain_one_grad, shift_one_grad = half_back(grad_normed)
+    grad_mid_half = lax.dynamic_slice_in_dim(grad_middle, c * half_seq, half_seq, 0)
+    input_grad = send_home((grad_mid_half + grad_states).astype(bf), c, z)
+
+    def once(v):
+        return jnp.where(c == 0, v, 0.0)
+
+    def placed(v):
+        return lax.dynamic_update_slice_in_dim(jnp.zeros((feat,), f32), v, c * half, 0)
+
+    in_bias = jnp.zeros((LINE, 2, hid // 2), f32)
+    in_bias = lax.dynamic_update_slice(in_bias, column_sum(grad_inner).reshape(LINE, 1, hid // 2), (0, c, 0))
+    packed = jnp.concatenate(
+        [
+            gain_one_grad, shift_one_grad, placed(column_sum(dq)), placed(column_sum(dv)),
+            once(column_sum(grad_attended)), once(gain_two_grad), once(shift_two_grad), once(column_sum(upstream)),
+            in_bias.reshape(LINE * hid),
+        ]
+    ).reshape(12, feat)
+    packed = lax.psum(packed, ("cells", "chrom"))
+
+    def shard(v):
+        return lax.dynamic_slice_in_dim(v, z * (v.shape[0] // LINE), v.shape[0] // LINE, 0)
+
+    s = [shard(packed[n]) for n in range(8)]
+    inner_bias_grad = shard(packed[8:].reshape(LINE * hid))
+    w2_grad = outer_sum.transpose(1, 0, 2, 3).reshape(hid, feat).astype(f32)
+    w1_grad = inner_sum.reshape(PLANE, 2, rows // PLANE, LINE, hid // 2).transpose(0, 2, 3, 1, 4)
+    w1_grad = w1_grad.reshape(rows, LINE * hid).astype(f32)
+    wx = attn_sum.reshape(PLANE, 2, rows // PLANE, 4, half).transpose(3, 0, 2, 1, 4).reshape(4, rows, feat)
+    wx = [wx[n].astype(f32) for n in range(4)]
+    return (
+        block_out, input_grad, s[0], s[1], wx[0], s[2], wx[1], wx[2], s[3], wx[3], s[4], s[5], s[6],
+        w1_grad, inner_bias_grad, w2_grad, s[7],
+    )
+
+
 def solution(mesh):
+    paired = mesh.shape["chrom"] == 4 and mesh.shape["cells"] == 8
     placed = (
         P("cells", "chrom", None),
         P("cells"),
@@ -417,7 +915,7 @@
         P("chrom"),
     )
     return jax.shard_map(
-        local,
+        paired_local if paired else general,
         mesh=mesh,
         in_specs=placed,
         out_specs=(

time: 2010 us -> 917 us (0.46)
  waiting for transfers between devices: 1310 us -> 150 us
  Pallas kernels: 0 us -> 226 us
  blocking collectives: 202 us -> 65.9 us
  matrix products: 295 us -> 226 us
  other arithmetic: 85.5 us -> 117 us
    all_gather x10 -> x3, waiting for transfers between devices: 734 us -> 0.01 us  [reduce_group(): whole = lax.all_gather(summed, 'cells', axis=0, tiled=False)]
    unnamed x20 -> x6, waiting for transfers between devices: 467 us -> 1.06 us
    pallas_call x0 -> x1, Pallas kernels: none -> 226 us  [gather_all(): pl.pallas_call(gather_kernel, out_shape=(jax.ShapeDtypeStruct((LINE,) + s...]
    ppermute x0 -> x22, waiting for transfers between devices: none -> 149 us  [the longest x18 146 us: flip(): return lax.ppermute(value, 'cells', [(n, n ^ step) for n in range(count)])]
    all_gather x14 -> x0, blocking collectives: 137 us -> none  [the longest x1 14.2 us: local(): lax.all_gather(section_two[4].astype(jnp.bfloat16), 'cells', axis=1, tile...]
    reduce_scatter x8 -> x3, waiting for transfers between devices: 112 us -> 0.06 us  [reduce_group(): summed = lax.psum_scatter(mine, 'chrom', scatter_dimension=0, tiled=True)[0]]
    psum x0 -> x1, blocking collectives: none -> 65.9 us  [paired_local(): packed = lax.psum(packed, ('cells', 'chrom'))]
    unnamed x3 -> x0, blocking collectives: 65.3 us -> none
  transfers between devices with their start and end apart: 19 -> 28, of which waited for: 12 -> 10; matrix products, arithmetic and copies ran while one was open for 15% -> 28% of each run, Pallas kernels for 0% -> 25%
where the time goes in v1:
time: 917 us; the launch traced here: 912 us
  Pallas kernels  226 us (25%)
  matrix products  226 us (25%)
  waiting for transfers between devices  150 us (16%)
  other arithmetic  117 us (13%)
  local copies, waits for them, and re-layouts  91.3 us (10%)
  blocking collectives  65.9 us (7%)
  starting transfers between devices  21 us (2%)
  between operations  15.5 us (2%)
    pallas_call x1, Pallas kernels, gather_all(): pl.pallas_call(gather_kernel, out_shape=(jax.ShapeDtypeStruct((LINE,) + s...  226 us
    ppermute x18, waiting for transfers between devices, flip(): return lax.ppermute(value, 'cells', [(n, n ^ step) for n in range(count)])  146 us
    psum x1, blocking collectives, paired_local(): packed = lax.psum(packed, ('cells', 'chrom'))  65.9 us
    dot_general x4, matrix products, product(): return jnp.dot(left, right, preferred_element_type=jnp.float32)  55.6 us
    dot_general x4, matrix products, right_back(): jnp.einsum('rb,ab->ra', left, right, preferred_element_type=jnp.float32)  38.7 us
    convert_element_type x1, other arithmetic, paired_local(): grad_raw = (again * (grad_probs - row_dot)).astype(bf)  33.8 us
    dot_general x4, matrix products, left_product(): jnp.einsum('ra,rb->ab', left, right, preferred_element_type=jnp.float32)  29.1 us
    dot_general x1, matrix products, paired_local(): grad_probs = jnp.einsum('qhd,khd->hqk', gh, vh, preferred_element_type=f32)  27 us
  transfers between devices with their start and end apart: 28, of which 10 were waited for; matrix products, arithmetic and copies ran while one was open for 28% of the time, Pallas kernels for 25%

profile of v1, /device:TPU:0, one launch (start us, length us, event | category | flops | bytes accessed | tf_op | source)
XLA Modules:
  0.0 912.4 jit_solution(2804600615921510154)
XLA Ops:
  16.1 226.4 %gather_all.1 = (bf16[4,16,384]{2,1,0:T(8,128)(2,1)}, bf16[1024,1280]{1,0:T(8,128)(2,1)}, bf16[1024,1280]{1,0:T(8,128)(2,1)}, bf16[1280,2560]{1,0:T(8,128)(2,1)}...) custom-call(bf16[16,384]{1,0:T(8,128)(2,1)} %pad.4.small_ref, ...), custom_call_target="tpu_custom_call" | custom-call | tf_op jit(solution)/shard_map/gather_all/pallas_call | solution.py:677
  268.1 18.5 %fusion.61 = (f32[10,1024]{1,0:T(8,128)S(1)}, f32[10,1024,1024]{1,2,0:T(8,128)}) fusion(f32[1024,1024]{0,1:T(8,128)} %convert_select_fusion, bf16[1024,10,64]{0,2,1:T(8,128)(2,1)} %bitcast.171, bf16[1024,10,64]{0,2,1:T(8,128)(2,1)} %bitcast.173), kind=kOutput, calls=%fused_computation.228 | convolution fusion | flops 1373624320 | bytes 48799744 | tf_op jit(solution)/shard_map/qhd,khd->hqk/dot_general | solution.py:795
  286.6 16.3 %fusion = f32[10,1024]{1,0:T(8,128)S(1)} fusion(f32[10,1024,1024]{1,2,0:T(8,128)} %get-tuple-element.99, f32[10,1024]{1,0:T(8,128)S(1)} %get-tuple-element.98), kind=kLoop, calls=%fused_computation.6 | loop fusion | flops 20961280 | bytes 42024960 | tf_op jit(solution)/shard_map/reduce_sum | solution.py:801
  302.9 18.3 %fusion.35 = bf16[10,64,1024]{2,1,0:T(8,128)(2,1)} fusion(bf16[1024,10,64]{0,2,1:T(8,128)(2,1)} %bitcast.193, f32[10,1024,1024]{1,2,0:T(8,128)} %get-tuple-element.99, f32[10,1024]{1,0:T(8,128)S(1)} %fusion, f32[10,1024]{1,0:T(8,128)S(1)} %get-tuple-element.98), kind=kOutput, calls=%fused_computation.124 | convolution fusion | flops 1374289920 | bytes 44646400 | tf_op jit(solution)/shard_map/hqk,khd->qhd/dot_general | solution.py:804
  337.5 31.1 %multiply_convert_fusion.1 = (bf16[1024,2560]{1,0:T(8,128)(2,1)}, f32[1024,2560]{1,0:T(8,128)}, f32[1024,2560]{1,0:T(8,128)}) fusion(f32[2560]{0:T(1024)S(1)} %reshape.359, bf16[1280,2560]{1,0:T(8,128)(2,1)S(1)} %bitcast.210, f32[1024,1280]{1,0:T(8,128)S(1)} %get-tuple-element.54, f32[1280]{0:T(1024)S(1)} %add.320, f32[1280]{0:T(1024)S(1)} %mul.227, ...), kind=kOutput, calls=%fused_computation.17 | convolution fusion | flops 6890455040 | bytes 38039552 | tf_op jit(solution)/shard_map/dot_general | solution.py:29
  368.7 17.5 %convert_reduce_fusion = (f32[2560]{0:T(1024)}, bf16[1024,2560]{1,0:T(8,128)(2,1)}) fusion(f32[1024,2560]{1,0:T(8,128)} %get-tuple-element.52, bf16[2560,1280]{1,0:T(8,128)(2,1)} %get-tuple-element.29, bf16[1024,1280]{1,0:T(8,128)(2,1)S(1)} %copy-done.16, pred[1024]{0:T(1024)(128)(4,1)S(1)} %copy-done.43, f32[1024,2560]{1,0:T(8,128)} %get-tuple-element.100, ...), kind=kOutput, calls=%fused_computation.15 | convolution fusion | flops 6756759040 | bytes 35410944 | tf_op jit(solution)/shard_map/rb,ab->ra/dot_general | solution.py:37
  386.2 11.1 %convolution_convert_fusion.4 = bf16[1024,1280]{1,0:T(8,128)(2,1)S(1)} fusion(bf16[1024,2560]{1,0:T(8,128)(2,1)} %get-tuple-element.108, bf16[1280,2560]{1,0:T(8,128)(2,1)} %get-tuple-element.28), kind=kOutput, calls=%fused_computation.57 | convolution fusion | flops 6712197120 | bytes 14417920 | tf_op jit(solution)/shard_map/rb,ab->ra/dot_general | solution.py:37
  397.4 10.4 %convolution_convert_fusion.1 = bf16[1280,2560]{1,0:T(8,128)(2,1)S(1)} fusion(bf16[1024,2560]{1,0:T(8,128)(2,1)} %get-tuple-element.108, f32[1024,1280]{1,0:T(8,128)S(1)} %copy-done.1, f32[1280]{0:T(1024)S(1)} %add.320, f32[1280]{0:T(1024)S(1)} %mul.227, f32[1024]{0:T(1024)S(1)} %fusion.37, f32[1024]{0:T(1024)S(1)} %broadcast_multiply_fusion), kind=kOutput, calls=%fused_computation.13 | convolution fusion | flops 6720716800 | bytes 17057792 | tf_op jit(solution)/shard_map/ra,rb->ab/dot_general | solution.py:33
  407.8 9.3 %convolution_convert_fusion = bf16[2560,1280]{1,0:T(8,128)(2,1)} fusion(bf16[1024,2560]{1,0:T(8,128)(2,1)S(1)} %bitcast.216, bf16[1024,1280]{1,0:T(8,128)(2,1)S(1)} %copy-done.17, pred[1024]{0:T(1024)(128)(4,1)S(1)} %copy-done.43), kind=kOutput, calls=%fused_computation.12 | convolution fusion | flops 6715473920 | bytes 14418944 | tf_op jit(solution)/shard_map/ra,rb->ab/dot_general | solution.py:33
  427.8 33.2 %collective-permute-done.20 = bf16[2,2,160,1280]{3,2,0,1:T(8,128)(2,1)} collective-permute-done((bf16[2,2,160,1280]{3,2,0,1:T(8,128)(2,1)}, bf16[2,2,160,1280]{3,2,0,1:T(8,128)(2,1)}, u32[]{:S(2)}, u32[]{:S(2)}) %collective-permute-start.20) | collective-permute-done | bytes 1638432 | tf_op jit(solution)/shard_map/ppermute | solution.py:701
  464.5 30.7 %collective-permute-done.16 = bf16[2,2,80,2560]{3,2,0,1:T(8,128)(2,1)S(1)} collective-permute-done((bf16[2,2,80,2560]{3,2,0,1:T(8,128)(2,1)S(1)}, bf16[2,2,80,2560]{3,2,0,1:T(8,128)(2,1)S(1)}, u32[]{:S(2)}, u32[]{:S(2)}) %collective-permute-start.16) | collective-permute-done | bytes 1638432 | tf_op jit(solution)/shard_map/ppermute | solution.py:701
  503.2 29.5 %collective-permute-done.17 = bf16[2,80,2560]{2,1,0:T(8,128)(2,1)S(1)} collective-permute-done((bf16[2,80,2560]{2,1,0:T(8,128)(2,1)S(1)}, bf16[2,80,2560]{2,1,0:T(8,128)(2,1)S(1)}, u32[]{:S(2)}, u32[]{:S(2)}) %collective-permute-start.17) | collective-permute-done | bytes 819232 | tf_op jit(solution)/shard_map/ppermute | solution.py:701
  552.6 16.5 %convert_reduce_fusion.4 = (f32[10,64]{1,0:T(8,128)S(1)}, bf16[10,64,1024]{2,1,0:T(8,128)(2,1)}) fusion(bf16[1024,10,64]{0,2,1:T(8,128)(2,1)S(1)} %bitcast.189, f32[10,1024,1024]{1,2,0:T(8,128)} %get-tuple-element.99, f32[10,1024]{1,0:T(8,128)S(1)} %copy-done.21), kind=kOutput, calls=%fused_computation.79 | convolution fusion | flops 1365114240 | bytes 44608000 | tf_op jit(solution)/shard_map/hqk,qhd->khd/dot_general | solution.py:841
  569.2 27.0 %multiply_reduce_fusion = (f32[10,1024]{1,0:T(8,128)S(1)}, f32[10,1024,1024]{1,2,0:T(8,128)}) fusion(f32[10,1024,1024]{1,2,0:T(8,128)} %get-tuple-element.99, f32[10,1024]{1,0:T(8,128)S(1)} %copy-done.21, bf16[1024,10,64]{0,2,1:T(8,128)(2,1)S(1)} %bitcast.190, bf16[1024,10,64]{0,2,1:T(8,128)(2,1)S(1)} %bitcast.194), kind=kOutput, calls=%fused_computation.1 | convolution fusion | flops 1373624320 | bytes 86589440 | tf_op jit(solution)/shard_map/qhd,khd->hqk/dot_general | solution.py:838
  596.1 33.8 %multiply_convert_fusion = bf16[10,1024,1024]{1,2,0:T(8,128)(2,1)} fusion(f32[10,1024,1024]{1,2,0:T(8,128)} %get-tuple-element.102, f32[10,1024,1024]{1,2,0:T(8,128)} %get-tuple-element.99, f32[10,1024]{1,0:T(8,128)S(1)} %get-tuple-element.101, f32[10,1024]{1,0:T(8,128)S(1)} %copy-done.21), kind=kLoop, calls=%fused_computation | loop fusion | flops 41943040 | bytes 104939520 | tf_op jit(solution)/shard_map/convert_element_type | solution.py:840
  629.9 10.9 %multiply_convert_fusion.2 = bf16[10,64,1024]{2,1,0:T(8,128)(2,1)S(1)} fusion(bf16[1024,10,64]{0,2,1:T(8,128)(2,1)S(1)} %bitcast.172, bf16[10,1024,1024]{1,2,0:T(8,128)(2,1)} %multiply_convert_fusion), kind=kOutput, calls=%fused_computation.87 | convolution fusion | flops 1343488000 | bytes 23592960 | tf_op jit(solution)/shard_map/hqk,qhd->khd/dot_general | solution.py:842
  640.9 11.4 %convert_reduce_fusion.5 = (f32[10,64]{1,0:T(8,128)S(1)}, bf16[10,64,1024]{2,1,0:T(8,128)(2,1)S(1)}) fusion(bf16[1024,10,64]{0,2,1:T(8,128)(2,1)S(1)} %bitcast.174, bf16[10,1024,1024]{1,2,0:T(8,128)(2,1)} %multiply_convert_fusion), kind=kOutput, calls=%fused_computation.80 | convolution fusion | flops 1344798080 | bytes 23595520 | tf_op jit(solution)/shard_map/hqk,khd->qhd/dot_general | solution.py:843
  673.8 27.8 %collective-permute-done.12 = bf16[2,2,80,2560]{3,2,0,1:T(8,128)(2,1)} collective-permute-done((bf16[2,2,80,2560]{3,2,0,1:T(8,128)(2,1)}, bf16[2,2,80,2560]{3,2,0,1:T(8,128)(2,1)}, u32[]{:S(2)}, u32[]{:S(2)}) %collective-permute-start.12) | collective-permute-done | bytes 1638432 | tf_op jit(solution)/shard_map/ppermute | solution.py:701
  711.3 13.0 %collective-permute-done.13 = bf16[2,80,2560]{2,1,0:T(8,128)(2,1)S(1)} collective-permute-done((bf16[2,80,2560]{2,1,0:T(8,128)(2,1)S(1)}, bf16[2,80,2560]{2,1,0:T(8,128)(2,1)S(1)}, u32[]{:S(2)}, u32[]{:S(2)}) %collective-permute-start.13) | collective-permute-done | bytes 819232 | tf_op jit(solution)/shard_map/ppermute | solution.py:701
  729.3 11.1 %fusion.62 = f32[1024,1280]{1,0:T(8,128)S(1)} fusion(bf16[1024,2560]{1,0:T(8,128)(2,1)} %get-tuple-element.51, bf16[2560,1280]{1,0:T(8,128)(2,1)} %get-tuple-element.29), kind=kOutput, calls=%fused_computation.229 | convolution fusion | flops 6710886400 | bytes 17039360 | tf_op jit(solution)/shard_map/dot_general | solution.py:29
  754.0 8.1 fusion.12
  786.7 65.9 %psum.7 = f32[12,1280]{1,0:T(8,128)S(1)} all-reduce(f32[12,1280]{1,0:T(8,128)S(1)} %reshape.357), channel_id=1, replica_groups=mesh['cells'=8,'chrom'=4] {'cells','chrom'}, use_global_device_ids=true, to_apply=%region_23.24 | all-reduce | flops 15360 | bytes 122880 | tf_op jit(solution)/shard_map/psum | solution.py:876
  864.4 10.7 %copy.168 = f32[4,80,4,2,640]{4,3,2,1,0:T(2,128)} copy(f32[4,80,4,2,640]{4,2,1,3,0:T(4,128)} %bitcast.170) | data formatting | bytes 13107200 | tf_op jit(solution)/shard_map/convert_element_type | solution.py:885
  875.1 9.1 reshape.372
  (329 shorter events, 199.4 us)
Async XLA Ops:
  7.2 721.0 %reduce-scatter.6.cloned.1.call-start = ((), (), s32[]{:S(2)}) async-start(), calls=%async_computation.5 | async-start | bytes 2048000 | tf_op jit(solution)/shard_map/reduce_scatter | solution.py:724
  8.7 256.6 %collective-permute-start = (s32[2,25]{1,0:T(2,128)S(1)}, s32[2,25]{1,0:T(2,128)S(1)}, u32[]{:S(2)}, u32[]{:S(2)}) collective-permute-start(s32[2,25]{1,0:T(2,128)S(1)} %pad_add_fusion), channel_id=1, source_target_pairs={{0,4},{4,0},{8,12},{12,8},{16,20},{20,16},{24,28},{28,24},{1,5},{5... | collective-permute-start | bytes 608 | tf_op jit(solution)/shard_map/ppermute | solution.py:701
  422.0 39.0 %collective-permute-start.20 = (bf16[2,2,160,1280]{3,2,0,1:T(8,128)(2,1)}, bf16[2,2,160,1280]{3,2,0,1:T(8,128)(2,1)}, u32[]{:S(2)}, u32[]{:S(2)}) collective-permute-start(bf16[2,2,160,1280]{3,2,0,1:T(8,128)(2,1)} %bitcast.163), channel_id=1, source_target_pairs={{0,16},{4,20},{8,24},{12,28},{16,0},{20,4},{24,8},{28,12},{1,17},{... | collective-permute-start | bytes 4915208 | tf_op jit(solution)/shard_map/ppermute | solution.py:701
  424.3 70.9 %collective-permute-start.16 = (bf16[2,2,80,2560]{3,2,0,1:T(8,128)(2,1)S(1)}, bf16[2,2,80,2560]{3,2,0,1:T(8,128)(2,1)S(1)}, u32[]{:S(2)}, u32[]{:S(2)}) collective-permute-start(bf16[2,2,80,2560]{3,2,0,1:T(8,128)(2,1)S(1)} %bitcast.204), channel_id=1, source_target_pairs={{0,16},{4,20},{8,24},{12,28},{16,0},{20,4},{24,8},{28,12},{1,17},{... | collective-permute-start | bytes 4915208 | tf_op jit(solution)/shard_map/ppermute | solution.py:701
  425.2 76.0 %collective-permute-start.18 = (bf16[2,2,160,1280]{3,2,0,1:T(8,128)(2,1)S(1)}, bf16[2,2,160,1280]{3,2,0,1:T(8,128)(2,1)S(1)}, u32[]{:S(2)}, u32[]{:S(2)}) collective-permute-start(bf16[2,2,160,1280]{3,2,0,1:T(8,128)(2,1)S(1)} %bitcast.200), channel_id=1, source_target_pairs={{0,8},{4,12},{8,0},{12,4},{16,24},{20,28},{24,16},{28,20},{1,9},{5... | collective-permute-start | bytes 4915208 | tf_op jit(solution)/shard_map/ppermute | solution.py:701
  426.8 107.8 %collective-permute-start.5 = (bf16[1024,1280]{1,0:T(8,128)(2,1)S(1)}, bf16[1024,1280]{1,0:T(8,128)(2,1)}, u32[]{:S(2)}, u32[]{:S(2)}) collective-permute-start(bf16[1024,1280]{1,0:T(8,128)(2,1)S(1)} %convolution_convert_fusion.4), channel_id=1, source_target_pairs={{0,4},{4,0},{8,12},{12,8},{16,20},{20,16},{24,28},{28,24},{1,5},{5... | collective-permute-start | bytes 7864328 | tf_op jit(solution)/shard_map/ppermute | solution.py:701
  427.2 72.0 %collective-permute-start.14 = (bf16[2,2,80,2560]{3,2,0,1:T(8,128)(2,1)S(1)}, bf16[2,2,80,2560]{3,2,0,1:T(8,128)(2,1)S(1)}, u32[]{:S(2)}, u32[]{:S(2)}) collective-permute-start(bf16[2,2,80,2560]{3,2,0,1:T(8,128)(2,1)S(1)} %bitcast.206), channel_id=1, source_target_pairs={{0,8},{4,12},{8,0},{12,4},{16,24},{20,28},{24,16},{28,20},{1,9},{5... | collective-permute-start | bytes 4915208 | tf_op jit(solution)/shard_map/ppermute | solution.py:701
  462.9 203.3 %collective-permute-start.21 = (bf16[2,160,1280]{2,1,0:T(8,128)(2,1)S(1)}, bf16[2,160,1280]{2,1,0:T(8,128)(2,1)}, u32[]{:S(2)}, u32[]{:S(2)}) collective-permute-start(bf16[2,160,1280]{2,1,0:T(8,128)(2,1)S(1)} %dynamic-slice_bitcast_fusion), channel_id=1, source_target_pairs={{0,8},{4,12},{8,0},{12,4},{16,24},{20,28},{24,16},{28,20},{1,9},{5... | collective-permute-start | bytes 2457608 | tf_op jit(solution)/shard_map/ppermute | solution.py:701
  495.6 37.1 %collective-permute-start.17 = (bf16[2,80,2560]{2,1,0:T(8,128)(2,1)S(1)}, bf16[2,80,2560]{2,1,0:T(8,128)(2,1)S(1)}, u32[]{:S(2)}, u32[]{:S(2)}) collective-permute-start(bf16[2,80,2560]{2,1,0:T(8,128)(2,1)S(1)} %dynamic-slice_bitcast_fusion.2), channel_id=1, source_target_pairs={{0,8},{4,12},{8,0},{12,4},{16,24},{20,28},{24,16},{28,20},{1,9},{5... | collective-permute-start | bytes 2457608 | tf_op jit(solution)/shard_map/ppermute | solution.py:701
  499.7 33.3 %collective-permute-start.15 = (bf16[2,80,2560]{2,1,0:T(8,128)(2,1)S(1)}, bf16[2,80,2560]{2,1,0:T(8,128)(2,1)S(1)}, u32[]{:S(2)}, u32[]{:S(2)}) collective-permute-start(bf16[2,80,2560]{2,1,0:T(8,128)(2,1)S(1)} %dynamic-slice_bitcast_fusion.3), channel_id=1, source_target_pairs={{0,16},{4,20},{8,24},{12,28},{16,0},{20,4},{24,8},{28,12},{1,17},{... | collective-permute-start | bytes 2457608 | tf_op jit(solution)/shard_map/ppermute | solution.py:701
  502.7 168.3 %collective-permute-start.19 = (bf16[2,160,1280]{2,1,0:T(8,128)(2,1)}, bf16[2,160,1280]{2,1,0:T(8,128)(2,1)}, u32[]{:S(2)}, u32[]{:S(2)}) collective-permute-start(bf16[2,160,1280]{2,1,0:T(8,128)(2,1)} %dynamic-slice_bitcast_fusion.1), channel_id=1, source_target_pairs={{0,16},{4,20},{8,24},{12,28},{16,0},{20,4},{24,8},{28,12},{1,17},{... | collective-permute-start | bytes 2457608 | tf_op jit(solution)/shard_map/ppermute | solution.py:701
  534.5 194.2 %reduce-scatter.8.cloned.1.call-start = ((), (), s32[]{:S(2)}) async-start(), calls=%async_computation.7 | async-start | bytes 2048000 | tf_op jit(solution)/shard_map/reduce_scatter | solution.py:724
  664.9 36.6 %collective-permute-start.12 = (bf16[2,2,80,2560]{3,2,0,1:T(8,128)(2,1)}, bf16[2,2,80,2560]{3,2,0,1:T(8,128)(2,1)}, u32[]{:S(2)}, u32[]{:S(2)}) collective-permute-start(bf16[2,2,80,2560]{3,2,0,1:T(8,128)(2,1)} %bitcast.167), channel_id=1, source_target_pairs={{0,16},{4,20},{8,24},{12,28},{16,0},{20,4},{24,8},{28,12},{1,17},{... | collective-permute-start | bytes 4915208 | tf_op jit(solution)/shard_map/ppermute | solution.py:701
  670.3 38.7 %collective-permute-start.10 = (bf16[2,2,80,2560]{3,2,0,1:T(8,128)(2,1)}, bf16[2,2,80,2560]{3,2,0,1:T(8,128)(2,1)}, u32[]{:S(2)}, u32[]{:S(2)}) collective-permute-start(bf16[2,2,80,2560]{3,2,0,1:T(8,128)(2,1)} %bitcast.168), channel_id=1, source_target_pairs={{0,8},{4,12},{8,0},{12,4},{16,24},{20,28},{24,16},{28,20},{1,9},{5... | collective-permute-start | bytes 4915208 | tf_op jit(solution)/shard_map/ppermute | solution.py:701
  673.7 101.9 %reduce-scatter.4.cloned.1.call-start = ((), (), s32[]{:S(2)}) async-start(), calls=%async_computation.3 | async-start | bytes 2048000 | tf_op jit(solution)/shard_map/reduce_scatter | solution.py:724
  704.1 20.2 %collective-permute-start.13 = (bf16[2,80,2560]{2,1,0:T(8,128)(2,1)S(1)}, bf16[2,80,2560]{2,1,0:T(8,128)(2,1)S(1)}, u32[]{:S(2)}, u32[]{:S(2)}) collective-permute-start(bf16[2,80,2560]{2,1,0:T(8,128)(2,1)S(1)} %dynamic-slice_bitcast_fusion.4), channel_id=1, source_target_pairs={{0,8},{4,12},{8,0},{12,4},{16,24},{20,28},{24,16},{28,20},{1,9},{5... | collective-permute-start | bytes 2457608 | tf_op jit(solution)/shard_map/ppermute | solution.py:701
  710.9 15.7 %collective-permute-start.11 = (bf16[2,80,2560]{2,1,0:T(8,128)(2,1)S(1)}, bf16[2,80,2560]{2,1,0:T(8,128)(2,1)S(1)}, u32[]{:S(2)}, u32[]{:S(2)}) collective-permute-start(bf16[2,80,2560]{2,1,0:T(8,128)(2,1)S(1)} %dynamic-slice_bitcast_fusion.5), channel_id=1, source_target_pairs={{0,16},{4,20},{8,24},{12,28},{16,0},{20,4},{24,8},{28,12},{1,17},{... | collective-permute-start | bytes 2457608 | tf_op jit(solution)/shard_map/ppermute | solution.py:701
  728.1 129.2 %all-gather.6.cloned.1.call-start = ((), (), s32[]{:S(2)}) async-start(), calls=%async_computation.6 | async-start | bytes 3686400 | tf_op jit(solution)/shard_map/all_gather | solution.py:725
  728.7 155.5 %all-gather.8.cloned.1.call-start = ((), (), s32[]{:S(2)}) async-start(), calls=%async_computation.8 | async-start | bytes 3686400 | tf_op jit(solution)/shard_map/all_gather | solution.py:725
  729.2 160.7 %all-gather.4.cloned.1.call-start = ((), (), s32[]{:S(2)}) async-start(), calls=%async_computation.4 | async-start | bytes 3686400 | tf_op jit(solution)/shard_map/all_gather | solution.py:725
  752.5 19.1 %collective-permute-start.3 = (bf16[256,1280]{1,0:T(8,128)(2,1)S(1)}, bf16[256,1280]{1,0:T(8,128)(2,1)S(1)}, u32[]{:S(2)}, u32[]{:S(2)}) collective-permute-start(bf16[256,1280]{1,0:T(8,128)(2,1)S(1)} %get-tuple-element.88), channel_id=1, source_target_pairs={{0,0},{1,1},{2,4},{3,5},{4,2},{5,3},{6,6},{7,7},{8,8},{9,9},{10,12... | collective-permute-start | bytes 1966088 | tf_op jit(solution)/shard_map/ppermute | solution.py:741
  753.6 20.8 %collective-permute-start.4 = (bf16[256,1280]{1,0:T(8,128)(2,1)S(1)}, bf16[256,1280]{1,0:T(8,128)(2,1)}, u32[]{:S(2)}, u32[]{:S(2)}) collective-permute-start(bf16[256,1280]{1,0:T(8,128)(2,1)S(1)} %get-tuple-element.89), channel_id=1, source_target_pairs={{0,1},{1,0},{2,5},{3,4},{4,3},{5,2},{6,7},{7,6},{8,9},{9,8},{10,13... | collective-permute-start | bytes 1966088 | tf_op jit(solution)/shard_map/ppermute | solution.py:741
  784.9 71.1 %collective-permute-start.7 = (bf16[256,1280]{1,0:T(8,128)(2,1)S(1)}, bf16[256,1280]{1,0:T(8,128)(2,1)S(1)}, u32[]{:S(2)}, u32[]{:S(2)}) collective-permute-start(bf16[256,1280]{1,0:T(8,128)(2,1)S(1)} %get-tuple-element.84), channel_id=1, source_target_pairs={{0,0},{1,1},{2,4},{3,5},{4,2},{5,3},{6,6},{7,7},{8,8},{9,9},{10,12... | collective-permute-start | bytes 1966088 | tf_op jit(solution)/shard_map/ppermute | solution.py:741
  785.6 70.4 %collective-permute-start.8 = (bf16[256,1280]{1,0:T(8,128)(2,1)S(1)}, bf16[256,1280]{1,0:T(8,128)(2,1)S(1)}, u32[]{:S(2)}, u32[]{:S(2)}) collective-permute-start(bf16[256,1280]{1,0:T(8,128)(2,1)S(1)} %get-tuple-element.85), channel_id=1, source_target_pairs={{0,1},{1,0},{2,5},{3,4},{4,3},{5,2},{6,7},{7,6},{8,9},{9,8},{10,13... | collective-permute-start | bytes 1966088 | tf_op jit(solution)/shard_map/ppermute | solution.py:741
  (59 other events, 513.6 us)
Sparse Core Ops, SparseCore 0:
  534.7 33.5 reduce-scatter.5
  673.9 33.5 reduce-scatter.7
  728.2 37.8 reduce-scatter.3
  768.0 33.8 all-gather.5
  803.8 33.0 all-gather.7
  838.8 33.1 all-gather.3

commit v2 on v1

--- a/solution.py
+++ b/solution.py
@@ -410,23 +410,55 @@
     return pl.ds(pl.multiple_of(start, 128), count)
 
 
-def gather_kernel(
-    small_ref, x_ref, ct_ref, wq_ref, wk_ref, wv_ref, wo_ref, w1_ref, w2_ref,
-    smalls, xf, cf, wa, wb, wc, wob,
-    sm_s, sm_r, ex_s, ex_r, fw_s, fw_r, un_s, un_r, loc, wo_s, wo_r,
+VECTORS = 8
+TILE = 256
+
+
+def nt(left, right):
+    return lax.dot_general(left, right, (((1,), (1,)), ((), ())), preferred_element_type=jnp.float32)
+
+
+def nn(left, right):
+    return jnp.dot(left, right, preferred_element_type=jnp.float32)
+
+
+def moments(values):
+    center = values - jnp.mean(values, axis=-1, keepdims=True)
+    spread = jnp.mean(center * center, axis=-1, keepdims=True)
+    return center, lax.rsqrt(spread + eps_norm)
+
+
+def gelu_and_slope(u):
+    gauss = jnp.exp(u * u * -0.5)
+    t = 1.0 / (1.0 + jnp.abs(u) * (0.3275911 * 0.5 ** 0.5))
+    poly = 0.5 * 1.061405429
+    for factor in (-1.453152027, 1.421413741, -0.284496736, 0.254829592):
+        poly = poly * t + 0.5 * factor
+    tail = poly * t * gauss
+    phi_sum = jnp.where(u < 0.0, tail, 1.0 - tail)
+    return u * phi_sum, phi_sum + u * gauss * 0.3989422804014327
+
+
+def forward_kernel(
+    small_ref, x_ref, ct_ref, wq_ref, wk_ref, wv_ref, wo_ref, w1_ref, w2_ref, gq_ref, gk_ref,
+    vec_o, x_o, ct_o, wa_o, wob_o, wb_o, wc, normed_o, qkv_o, mixed_o, lse_o, middle_o, second_o, active_o, slope_o,
+    smalls, vec, bias_in, xf, cf, wa, wol, wob, wb, normed, qkv, gq, gk, kx, mixed, lse, part, part_in, middle, second,
+    act, slp,
+    sm_s, sm_r, ex_s, ex_r, fw_s, fw_r, ln_s, un_s, un_r, loc, wo_s, wo_r, pa_s, pa_r, out_s, act_s,
 ):
+    f32, bf = jnp.float32, jnp.bfloat16
     i, z = lax.axis_index("cells"), lax.axis_index("chrom")
     p, c = i // 2, lax.rem(i, 2)
     px, py = lax.rem(p, 2), p // 2
     x_nb, y_nb, core_nb = i + 2 - 4 * px, i + 4 - 8 * py, i + 1 - 2 * c
     p_x, p_y = p + 1 - 2 * px, p + 2 - 4 * py
-    right = lax.rem(z + 1, LINE)
     rows = wq_ref.shape[0]
     feat = wq_ref.shape[1]
     half = feat // 2
     hid = w2_ref.shape[0]
     block = x_ref.shape[1]
-    part, hid_part = rows // PLANE, hid // 2 // PLANE
+    seq = block * LINE
+    part_rows, hid_part = rows // PLANE, hid // 2 // PLANE
 
     barrier = pltpu.get_barrier_semaphore()
     line_ids = [
@@ -492,23 +524,30 @@
     c_start, c_arrived, c_sent = exchange(ct_ref, cf, 1)
     x_fw, c_fw = forward(xf, 0), forward(cf, 1)
 
-    lands = (wa, wb, wc)
+    lands = (wa, wol, wb, wc)
+    groups = range(4)
+    partner, inner = z + 1 - 2 * lax.rem(z, 2), 3 - z
+    low = z < 2
+    middle_chip = jnp.logical_or(z == 1, z == 2)
+    slot_shard = (partner, jnp.where(low, 2, 1), jnp.where(low, 3, 0))
 
     def own_parts(g, row, count):
         if g == 0:
             return [
-                (ref.at[rows_of(row, count), cols_of(c * half, half)], cols_of(n * half, half))
-                for n, ref in enumerate((wq_ref, wk_ref, wv_ref, wo_ref))
+                (ref.at[rows_of(row, count), cols_of(c * half, half)], pl.ds(n * half, half))
+                for n, ref in enumerate((wq_ref, wk_ref, wv_ref))
             ]
         if g == 1:
+            return [(wo_ref.at[rows_of(row, count), cols_of(c * half, half)], pl.ds(0, half))]
+        if g == 2:
             return [
-                (w1_ref.at[rows_of(row, count), cols_of(n * hid + c * (hid // 2), hid // 2)], cols_of(n * (hid // 2), hid // 2))
+                (w1_ref.at[rows_of(row, count), cols_of(n * hid + c * (hid // 2), hid // 2)], pl.ds(n * (hid // 2), hid // 2))
                 for n in range(LINE)
             ]
         return [(w2_ref.at[rows_of(c * (hid // 2) + row, count), :], pl.ds(0, feat))]
 
     def shape_of(g):
-        return (rows, part) if g < 2 else (hid // 2, hid_part)
+        return (rows, part_rows) if g < 3 else (hid // 2, hid_part)
 
     def piece(g, s, at):
         shard, count = shape_of(g)
@@ -516,184 +555,365 @@
 
     def half_piece(g, s, at, side):
         shard, count = shape_of(g)
-        width = lands[g].shape[1] // 2
-        return lands[g].at[rows_of(s * shard + at * count, count), pl.ds(side * width, width)]
-
-    def shard_at(k):
-        return lax.rem(z - k + LINE, LINE)
-
-    class Unit:
-        def __init__(self, g, k):
-            self.g, self.k, self.n = g, k, g * (LINE - 1) + k - 1
-
-        def sems(self, e):
-            return un_s.at[self.n, e], un_r.at[self.n, e]
-
-        def turn(self):
-            s = shard_at(self.k - 1)
-            return send(piece(self.g, s, p), piece(self.g, s, p), *self.sems(0), (i, right))
-
-        def turn_start(self):
-            if self.k > 1:
-                self.turn().start()
-                return
-            shard, count = shape_of(self.g)
-            for src, cols in own_parts(self.g, p * count, count):
-                dst = lands[self.g].at[rows_of(z * shard + p * count, count), cols]
-                send(src, dst, *self.sems(0), (i, right)).start()
-
-        def spread(self):
-            s = shard_at(self.k)
-            own = piece(self.g, s, p)
-            return [
-                send(own, own, *self.sems(1), (x_nb, z)),
-                send(own, own, *self.sems(2), (y_nb, z)),
-            ]
-
-        def cross(self):
-            s = shard_at(self.k)
-            left = half_piece(self.g, s, p_x, 0)
-            rest = half_piece(self.g, s, p_y, 1)
-            return [
-                send(left, left, *self.sems(3), (y_nb, z)),
-                send(rest, rest, *self.sems(4), (x_nb, z)),
-            ]
-
-        def arrived(self):
-            self.turn().wait_recv()
-
-        def spread_start(self):
-            for d in self.spread():
-                d.start()
-
-        def cross_start(self):
-            for d in self.spread():
-                d.wait_recv()
-            for d in self.cross():
-                d.start()
-
-        def done(self):
-            for d in self.cross():
-                d.wait_recv()
-
-        def sent(self):
-            for d in [self.turn()] + self.spread() + self.cross():
-                d.wait_send()
-
-    a, b, w = ([Unit(g, k) for k in range(1, LINE)] for g in range(3))
+        width = lands[g].shape[1]
+        cut = width // 256 * 128
+        cols = pl.ds(cut, width - cut) if side else pl.ds(0, cut)
+        return lands[g].at[rows_of(s * shard + at * count, count), cols]
+
+    def line_send(g, s, slot, e, to):
+        return send(piece(g, s, p), piece(g, s, p), ln_s.at[g, e], un_r.at[3 * g + slot, 0], (i, to))
+
+    def first(g):
+        shard, count = shape_of(g)
+        for src, cols in own_parts(g, p * count, count):
+            dst = lands[g].at[rows_of(z * shard + p * count, count), cols]
+            send(src, dst, ln_s.at[g, 0], un_r.at[3 * g, 0], (i, partner)).start()
+
+        @pl.when(middle_chip)
+        def _():
+            for src, cols in own_parts(g, p * count, count):
+                dst = lands[g].at[rows_of(z * shard + p * count, count), cols]
+                send(src, dst, ln_s.at[g, 1], un_r.at[3 * g + 1, 0], (i, inner)).start()
+
+    def passing(g, slot):
+        if slot == 0:
+            return line_send(g, slot_shard[0], 2, 2, inner)
+        return line_send(g, slot_shard[slot], slot, 2 + slot, partner)
+
+    def spread(g, slot):
+        own = piece(g, slot_shard[slot], p)
+        u = 3 * g + slot
+        return [
+            send(own, own, un_s.at[u, 0], un_r.at[u, 1], (x_nb, z)),
+            send(own, own, un_s.at[u, 1], un_r.at[u, 2], (y_nb, z)),
+        ]
+
+    def cross(g, slot):
+        u = 3 * g + slot
+        left = half_piece(g, slot_shard[slot], p_x, 0)
+        rest = half_piece(g, slot_shard[slot], p_y, 1)
+        return [
+            send(left, left, un_s.at[u, 2], un_r.at[u, 3], (y_nb, z)),
+            send(rest, rest, un_s.at[u, 3], un_r.at[u, 4], (x_nb, z)),
+        ]
+
+    def land(g, slot):
+        line_send(g, slot_shard[slot], slot, 0, partner).wait_recv()
+        pl.when(middle_chip)(passing(g, slot).start)
+        for d in spread(g, slot):
+            d.start()
+
+    def turn(g, slot):
+        for d in spread(g, slot):
+            d.wait_recv()
+        for d in cross(g, slot):
+            d.start()
 
     def own_start(g):
         shard, _ = shape_of(g)
         for src, cols in own_parts(g, 0, shard):
-            pltpu.make_async_copy(src, lands[g].at[rows_of(z * shard, shard), cols], loc.at[1 + g]).start()
+            to = second.at[pl.ds(0, shard), :] if g == 3 else lands[g].at[rows_of(z * shard, shard), cols]
+            pltpu.make_async_copy(src, to, loc.at[1 + g]).start()
 
     def own_wait(g):
         shard, _ = shape_of(g)
-        ref = lands[g].at[rows_of(z * shard, shard), :]
+        ref = second.at[pl.ds(0, shard), :] if g == 3 else lands[g].at[rows_of(z * shard, shard), :]
         pltpu.make_async_copy(ref, ref, loc.at[1 + g]).wait()
+
+    def whole(g):
+        for slot in range(3):
+            for d in cross(g, slot):
+                d.wait_recv()
+        if g < 3:
+            own_wait(g)
+
+    def all_sent(g):
+        line_send(g, z, 0, 0, partner).wait_send()
+
+        @pl.when(middle_chip)
+        def _():
+            line_send(g, z, 1, 1, inner).wait_send()
+            for slot in range(3):
+                passing(g, slot).wait_send()
+
+        for slot in range(3):
+            for d in spread(g, slot) + cross(g, slot):
+                d.wait_send()
+
+    outs = []
+
+    def keep(src, dst):
+        d = pltpu.make_async_copy(src, dst, out_s.at[len(outs)])
+        d.start()
+        outs.append(d)
 
     small_own.start()
     for d in small_out:
         d.start()
-    a[0].turn_start()
+    first(0)
     x_start()
-    for g in range(3):
+    for g in groups:
         own_start(g)
-    a[0].arrived()
-    a[1].turn_start()
-    a[0].spread_start()
-    b[0].turn_start()
-    a[1].arrived()
-    a[2].turn_start()
-    a[1].spread_start()
-    a[0].cross_start()
+    gq_in = pltpu.make_async_copy(gq_ref, gq, loc.at[6])
+    gk_in = pltpu.make_async_copy(gk_ref, gk, loc.at[7])
+    gq_in.start()
+    gk_in.start()
+    first(1)
+    land(0, 0)
+
+    small_own.wait()
+    for d in small_out:
+        d.wait()
+    width = smalls.shape[2]
+    total = jnp.zeros((smalls.shape[1], feat), f32)
+    at = lax.broadcasted_iota(jnp.int32, (width, feat), 0)
+    to = lax.broadcasted_iota(jnp.int32, (width, feat), 1)
+    for s in range(LINE):
+        place = jnp.where(jnp.logical_and(at < rows, to == at + s * rows), 1.0, 0.0).astype(bf)
+        total += nn(smalls[s], place)
+    vec[...] = total
+    at = lax.broadcasted_iota(jnp.int32, (width, hid // 2), 0)
+    to = lax.broadcasted_iota(jnp.int32, (width, hid // 2), 1)
+    which = lax.broadcasted_iota(jnp.int32, (smalls.shape[1], hid // 2), 0)
+    for s in range(LINE):
+        line_bias = jnp.zeros((1, hid // 2), f32)
+        for n in range(hid // 2 // rows):
+            place = jnp.where(jnp.logical_and(at < rows, to == at + n * rows), 1.0, 0.0).astype(bf)
+            picked = jnp.where(which == VECTORS + c * (hid // 2 // rows) + n, nn(smalls[s], place), 0.0)
+            line_bias += jnp.sum(picked, axis=0, keepdims=True)
+        bias_in[:, pl.ds(s * (hid // 2), hid // 2)] = line_bias
+    keep(vec, vec_o)
+
+    land(0, 1)
+    first(2)
+    turn(0, 0)
     x_arrived()
     for d in x_fw:
         d.start()
-    a[2].arrived()
-    a[2].spread_start()
-    b[0].arrived()
-    b[1].turn_start()
-    b[0].spread_start()
-    a[1].cross_start()
-    a[2].cross_start()
-    b[1].arrived()
-    b[2].turn_start()
-    w[0].turn_start()
-    b[1].spread_start()
-    b[0].cross_start()
-    for u in a:
-        u.done()
-    own_wait(0)
+    land(0, 2)
+    turn(0, 1)
+
+    def norm_rows(n, _):
+        at = pl.ds(pl.multiple_of(n * 64, 64), 64)
+        center, r = moments(xf[at, :].astype(f32))
+        normed[at, :] = (center * r * vec[0:1, :] + vec[1:2, :]).astype(bf)
+        return _
+
+    def norm_half(h):
+        steps = seq // 2 // 64
+        lax.fori_loop(h * steps, (h + 1) * steps, norm_rows, 0)
+
+    norm_half(c)
+    for d in x_fw:
+        d.wait_recv()
+    norm_half(1 - c)
+    keep(normed, normed_o)
+    keep(xf, x_o)
+    gq_in.wait()
+    gk_in.wait()
+    kx[:, 128:] = gk[...]
+    land(1, 0)
+    land(1, 1)
+    turn(0, 2)
+    land(1, 2)
+    land(2, 0)
+    for slot in range(3):
+        turn(1, slot)
+    whole(0)
+    keep(wa, wa_o)
+
+    bias_row = jnp.concatenate(
+        [vec[2:3, cols_of(c * half, half)], jnp.zeros((1, half), f32), vec[3:4, cols_of(c * half, half)]], axis=1
+    )
+
+    def qkv_cols(start, width):
+        got = nn(normed[...], wa[:, pl.ds(start, width)])
+        qkv[:, pl.ds(start, width)] = (got + bias_row[:, start : start + width]).astype(bf)
+
+    total_cols = 3 * half
+    for n in range(total_cols // TILE):
+        qkv_cols(n * TILE, TILE)
+        if n == 3:
+            land(2, 1)
+            first(3)
+    if total_cols % TILE:
+        qkv_cols(total_cols // TILE * TILE, total_cols % TILE)
+    turn(2, 0)
+    keep(qkv, qkv_o)
+
+    lane = lax.broadcasted_iota(jnp.int32, (TILE, 128), 1)
+
+    def attend(t):
+        k2 = qkv[:, pl.ds(half + t * 128, 128)]
+        v2t = jnp.transpose(qkv[:, pl.ds(2 * half + t * 128, 128)])
+        kx[:, :128] = k2
+
+        def chunk(n, _):
+            at = pl.ds(pl.multiple_of(n * TILE, TILE), TILE)
+            q2 = qkv[at, pl.ds(t * 128, 128)] * jnp.array(HEAD_DIM ** (-0.5), bf)
+            both = []
+            for h in range(2):
+                own = lane < HEAD_DIM if h == 0 else lane >= HEAD_DIM
+                qx = jnp.concatenate([jnp.where(own, q2, jnp.zeros((), bf)), gq[at, :]], axis=1)
+                s = nt(kx[...], qx)
+                top = jnp.max(s, axis=0, keepdims=True)
+                e = jnp.exp(s - top)
+                total = jnp.sum(e, axis=0, keepdims=True)
+                o = nn(v2t[h * HEAD_DIM : (h + 1) * HEAD_DIM, :], e.astype(bf))
+                both.append(o / total)
+                lse[2 * t + h : 2 * t + h + 1, at] = top + jnp.log(total)
+            mixed[at, pl.ds(t * 128, 128)] = jnp.transpose(jnp.concatenate(both, axis=0)).astype(bf)
+            return _
+
+        lax.fori_loop(0, seq // TILE, chunk, 0)
+
+    attend(0)
+    land(2, 2)
+    turn(2, 1)
+    attend(1)
+    whole(1)
     wo_own = pltpu.make_async_copy(
-        wa.at[rows_of(c * half, half), pl.ds(3 * half, half)], wob.at[:, cols_of(c * half, half)], loc.at[4]
+        wol.at[rows_of(c * half, half), :], wob.at[:, cols_of(c * half, half)], loc.at[5]
     )
     wo_out = send(
-        wa.at[rows_of((1 - c) * half, half), pl.ds(3 * half, half)],
+        wol.at[rows_of((1 - c) * half, half), :],
         wob.at[:, cols_of(c * half, half)], wo_s.at[0], wo_r.at[0], (core_nb, z),
     )
     wo_own.start()
     wo_out.start()
-    b[2].arrived()
-    b[2].spread_start()
-    w[0].arrived()
-    w[1].turn_start()
-    w[0].spread_start()
+    attend(2)
+    land(3, 0)
+    turn(2, 2)
+    attend(3)
+    land(3, 1)
+    attend(4)
+    turn(3, 0)
+    keep(mixed, mixed_o)
+    keep(lse, lse_o)
+    wo_own.wait()
+    wo_out.wait()
+    keep(wob, wob_o)
+
+    chunks = seq // TILE
+    swaps = []
+    for n in range(chunks):
+        at = pl.ds(n * TILE, TILE)
+        part[at, :] = nn(mixed[at, :], wob[...]).astype(bf)
+        d = send(part.at[at, :], part_in.at[at, :], pa_s.at[n], pa_r.at[n], (core_nb, z))
+        d.start()
+        swaps.append(d)
+    land(3, 2)
     c_start()
-    b[1].cross_start()
-    b[2].cross_start()
-    w[1].arrived()
-    w[2].turn_start()
-    w[1].spread_start()
-    w[0].cross_start()
-    w[2].arrived()
-    w[2].spread_start()
-    w[1].cross_start()
+    own_wait(3)
+    out_own = pltpu.make_async_copy(
+        second.at[pl.ds(0, hid // 2), :], wc.at[rows_of(z * (hid // 2), hid // 2), :], loc.at[4]
+    )
+    out_own.start()
+    out_own.wait()
+
+    def second_rows(n, _):
+        at = pl.ds(pl.multiple_of(n * 64, 64), 64)
+        sums = xf[at, :].astype(f32) + (part[at, :].astype(f32) + part_in[at, :].astype(f32) + vec[4:5, :])
+        middle[at, :] = sums
+        center, r = moments(sums)
+        second[at, :] = (center * r * vec[5:6, :] + vec[6:7, :]).astype(bf)
+        return _
+
+    for n in range(chunks):
+        swaps[n].wait_recv()
+        lax.fori_loop(n * TILE // 64, (n + 1) * TILE // 64, second_rows, 0)
+    keep(middle, middle_o)
+    keep(second, second_o)
+    turn(3, 1)
+    whole(2)
+    keep(wb, wb_o)
+
+    tiles = 2 * hid // TILE
+
+    def tile_out(n, slot):
+        cols = pl.ds(n * TILE, TILE)
+        return [
+            pltpu.make_async_copy(act.at[slot], active_o.at[:, cols], act_s.at[slot, 0]),
+            pltpu.make_async_copy(slp.at[slot], slope_o.at[:, cols], act_s.at[slot, 1]),
+        ]
+
+    for n in range(tiles):
+        slot = n % 2
+        cols = pl.ds(n * TILE, TILE)
+        if n >= 2:
+            for d in tile_out(n - 2, slot):
+                d.wait()
+
+        def tile_rows(m, _, cols=cols, slot=slot):
+            at = pl.ds(pl.multiple_of(m * TILE, TILE), TILE)
+            u = nn(second[at, :], wb[:, cols]) + bias_in[:, cols]
+            value, slope = gelu_and_slope(u)
+            act[slot, at, :] = value.astype(bf)
+            slp[slot, at, :] = slope.astype(bf)
+            return _
+
+        lax.fori_loop(0, chunks, tile_rows, 0)
+        for d in tile_out(n, slot):
+            d.start()
+        if n == 3:
+            turn(3, 2)
     c_arrived()
     for d in c_fw:
         d.start()
-    w[2].cross_start()
-    for u in b + w:
-        u.done()
-    for g in (1, 2):
-        own_wait(g)
-    small_own.wait()
-    wo_own.wait()
-    for d in small_out + x_fw + c_fw + [wo_out]:
+    for n in (tiles - 2, tiles - 1):
+        for d in tile_out(n, n % 2):
+            d.wait()
+    whole(3)
+    for d in c_fw:
         d.wait()
+    keep(cf, ct_o)
+    for d in x_fw + swaps:
+        d.wait_send()
     x_sent()
     c_sent()
-    for u in a + b + w:
-        u.sent()
-
-
-def gather_all(small, x, ct, wq, wk, wv, wo, w1, w2):
+    for g in groups:
+        all_sent(g)
+    for d in outs:
+        d.wait()
+
+
+def run_forward(small, x, ct, wq, wk, wv, wo, w1, w2, gq, gk):
     rows, feat = wq.shape
     hid = w2.shape[0]
     seq = x.shape[1] * LINE
-    bf = jnp.bfloat16
+    half = feat // 2
+    heads = half // HEAD_DIM
+    f32, bf = jnp.float32, jnp.bfloat16
     dma = pltpu.SemaphoreType.DMA
     anywhere = pl.BlockSpec(memory_space=pl.ANY)
+    made = [
+        ((small.shape[0], feat), f32), ((seq, feat), bf), ((seq, feat), bf), ((feat, 3 * half), bf), ((half, feat), bf),
+        ((feat, 2 * hid), bf), ((2 * hid, feat), bf), ((seq, feat), bf), ((seq, 3 * half), bf), ((seq, half), bf),
+        ((16, seq), f32), ((seq, feat), f32), ((seq, feat), bf), ((seq, 2 * hid), bf), ((seq, 2 * hid), bf),
+    ]
+    held = [
+        ((LINE,) + small.shape, bf), ((small.shape[0], feat), f32), ((1, 2 * hid), f32), ((seq, feat), bf), ((seq, feat), bf),
+        ((feat, 3 * half), bf), ((feat, half), bf), ((half, feat), bf), ((feat, 2 * hid), bf), ((seq, feat), bf),
+        ((seq, 3 * half), bf), ((seq, 128), bf), ((seq, 128), bf), ((seq, 256), bf), ((seq, half), bf),
+        ((16, seq), f32), ((seq, feat), bf), ((seq, feat), bf), ((seq, feat), f32), ((seq, feat), bf),
+        ((2, seq, TILE), bf), ((2, seq, TILE), bf),
+    ]
     return pl.pallas_call(
-        gather_kernel,
-        out_shape=(
-            jax.ShapeDtypeStruct((LINE,) + small.shape, bf),
-            jax.ShapeDtypeStruct((seq, feat), bf),
-            jax.ShapeDtypeStruct((seq, feat), bf),
-            jax.ShapeDtypeStruct((rows * LINE, 2 * feat), bf),
-            jax.ShapeDtypeStruct((rows * LINE, hid * LINE // 2), bf),
-            jax.ShapeDtypeStruct((hid * LINE // 2, feat), bf),
-            jax.ShapeDtypeStruct((feat // 2, feat), bf),
-        ),
-        in_specs=[anywhere] * 9,
-        out_specs=(anywhere,) * 7,
-        scratch_shapes=[
+        forward_kernel,
+        out_shape=tuple(jax.ShapeDtypeStruct(shape, dtype) for shape, dtype in made),
+        in_specs=[anywhere] * 11,
+        out_specs=(anywhere,) * len(made),
+        scratch_shapes=[pltpu.VMEM(shape, dtype) for shape, dtype in held]
+        + [
             dma((3,)), dma((3,)), dma((4,)), dma((4,)), dma((4,)), dma((4,)),
-            dma((9, 5)), dma((9, 5)), dma((5,)), dma((1,)), dma((1,)),
+            dma((4, 5)), dma((12, 4)), dma((12, 5)), dma((8,)), dma((1,)), dma((1,)),
+            dma((4,)), dma((4,)), dma((16,)), dma((2, 2)),
         ],
-        compiler_params=pltpu.CompilerParams(collective_id=0, has_side_effects=True),
-        name="gather_all",
-    )(small, x, ct, wq, wk, wv, wo, w1, w2)
+        compiler_params=pltpu.CompilerParams(
+            collective_id=0, has_side_effects=True, vmem_limit_bytes=60 * 1024 * 1024
+        ),
+        name="forward",
+    )(small, x, ct, wq, wk, wv, wo, w1, w2, gq, gk)
 
 
 def flip(value, step):
@@ -762,15 +982,6 @@
     vectors = (norm_gain, norm_shift, query_bias, value_bias, output_bias, second_gain, second_shift, outer_bias)
     small = jnp.concatenate([v.reshape(1, rows) for v in vectors] + [inner_bias.reshape(hid // rows, rows)], axis=0)
     small = jnp.pad(small, ((0, 16 - small.shape[0]), (0, 384 - rows)))
-    smalls, xf, cf, wa, wb, wc, wob = gather_all(
-        small, inputs, cotangent, query_proj, key_proj, value_proj, output_proj, inner_proj, outer_proj
-    )
-    flat = smalls[:, :8, :rows].astype(f32).transpose(1, 0, 2).reshape(8, feat)
-    gain_one, shift_one, bias_q, bias_v, bias_o, gain_two, shift_two, bias_out = (flat[n] for n in range(8))
-    bias_in = lax.dynamic_slice_in_dim(smalls[:, 8:12, :rows], 2 * c, 2, 1).astype(f32).reshape(2 * hid)
-    bias_q = lax.dynamic_slice_in_dim(bias_q, c * half, half, 0)
-    bias_v = lax.dynamic_slice_in_dim(bias_v, c * half, half, 0)
-
     ragged = jnp.concatenate([lengths[:, None], offsets], axis=1)
     other = flip(ragged, 1)
     ragged = take(jnp.where(z // 2 == c, ragged, other), z % 2, 0)
@@ -778,38 +989,26 @@
     places = jnp.arange(seq, dtype=jnp.int32)
     live = places < length
     groups = jnp.sum((places[:, None] >= starts[None, :]).astype(jnp.int32), axis=1)
+    lanes = jnp.arange(128, dtype=jnp.int32)[None, :]
+    same = (groups[:, None] == lanes).astype(bf)
+    mark_q = jnp.where(lanes == 127, jnp.ones((), bf), same * jnp.array(group_bias, bf))
+    mark_k = jnp.where(lanes == 127, jnp.where(live, 0.0, -1e30).astype(bf)[:, None], same)
+    (
+        vec, xf, cf, wa, wob, wb, wc, normed, qkv, mixed, lse, middle, second, active, slope,
+    ) = run_forward(
+        small, inputs, cotangent, query_proj, key_proj, value_proj, output_proj, inner_proj, outer_proj, mark_q, mark_k
+    )
+    gain_one, shift_one, _, _, _, gain_two, shift_two, bias_out = (vec[n] for n in range(8))
+    states = xf.astype(f32)
+    qh, kh, vh = (qkv[:, n * half : (n + 1) * half].reshape(seq, heads, HEAD_DIM) for n in range(3))
     bias = jnp.where(live[None, :], group_bias * (groups[:, None] == groups[None, :]).astype(f32), -jnp.inf)
-
-    states = xf.astype(f32)
-    normed_full, norm_back = jax.vjp(layer_norm, states, gain_one, shift_one)
-    normed = normed_full.astype(bf)
-    qkv = product(normed, wa[:, : 3 * half])
-    queries = (qkv[:, :half] + bias_q).astype(bf)
-    key_rows = qkv[:, half : 2 * half].astype(bf)
-    vals = (qkv[:, 2 * half :] + bias_v).astype(bf)
-    qh = queries.reshape(seq, heads, HEAD_DIM)
-    kh = key_rows.reshape(seq, heads, HEAD_DIM)
-    vh = vals.reshape(seq, heads, HEAD_DIM)
+    log_total = lse[:heads, :, None]
+    _, second_back = jax.vjp(layer_norm, middle, gain_two, shift_two)
 
     def scores_of():
         raw = jnp.einsum("qhd,khd->hqk", qh, kh, preferred_element_type=f32) * inv_root
         return raw + bias[None]
 
-    masked = scores_of()
-    row_max = jnp.max(masked, axis=-1, keepdims=True)
-    exp_scores = jnp.exp(masked - row_max)
-    exp_total = jnp.sum(exp_scores, axis=-1, keepdims=True)
-    log_total = row_max + jnp.log(exp_total)
-    probs = (exp_scores / exp_total).astype(bf)
-    mixed = jnp.einsum("hqk,khd->qhd", probs, vh, preferred_element_type=f32).astype(bf).reshape(seq, half)
-    part = product(mixed, wob).astype(bf)
-    attended = part.astype(f32) + flip(part, 1).astype(f32) + bias_o
-    middle = states + attended
-    second_full, second_back = jax.vjp(layer_norm, middle, gain_two, shift_two)
-    second = second_full.astype(bf)
-    inner = product(second, wb) + bias_in
-    active_full, gelu_back = jax.vjp(gelu_exact, inner)
-    active = active_full.astype(bf)
     upstream = jnp.where(live[:, None], cf, jnp.zeros((), bf))
     out_part = product(active, wc)
     mine = lax.dynamic_slice_in_dim(out_part, c * half_seq, half_seq, 0)
@@ -822,8 +1021,7 @@
 
     outer_grad = left_product(active, upstream).astype(bf)
     outer_sum = reduce_group(outer_grad.reshape(LINE, PLANE, hid // 2 // PLANE, feat), px, py)
-    (grad_inner_full,) = gelu_back(right_back(upstream, wc))
-    grad_inner = grad_inner_full.astype(bf)
+    grad_inner = (right_back(upstream, wc) * slope.astype(f32)).astype(bf)
     inner_grad = left_product(second, grad_inner).astype(bf)
     inner_sum = reduce_group(inner_grad.reshape(LINE, PLANE, rows // PLANE, 2 * hid), px, py)
     second_part = right_back(grad_inner, wb).astype(bf)
@@ -848,7 +1046,7 @@
     out_cols = jnp.where(c == 0, jnp.concatenate([keep, swap], 0), jnp.concatenate([swap, keep], 0))
     attn_grad = jnp.concatenate([qkv_grad, out_cols], axis=1)
     attn_sum = reduce_group(attn_grad.reshape(LINE, PLANE, rows // PLANE, 2 * feat), px, py)
-    normed_part = right_back(dqkv, wa[:, : 3 * half])
+    normed_part = right_back(dqkv, wa)
     mine = lax.dynamic_slice_in_dim(normed_part, c * half_seq, half_seq, 0)
     theirs = lax.dynamic_slice_in_dim(normed_part, (1 - c) * half_seq, half_seq, 0).astype(bf)
     grad_normed = mine + flip(theirs, 1).astype(f32)

time: 917 us -> 717 us (0.78)
  waiting for transfers between devices: 150 us -> 72.7 us
  matrix products: 226 us -> 157 us
  Pallas kernels: 226 us -> 182 us
  other arithmetic: 117 us -> 99.9 us
    ppermute x18 -> x17, waiting for transfers between devices: 146 us -> 64.7 us  [flip(): return lax.ppermute(value, 'cells', [(n, n ^ step) for n in range(count)])]
    dot_general x4 -> x1, matrix products: 55.6 us -> 10.8 us  [product(): return jnp.dot(left, right, preferred_element_type=jnp.float32)]
    pallas_call x1, Pallas kernels: 226 us -> 182 us  [run_forward(): pl.pallas_call(forward_kernel, out_shape=tuple((jax.ShapeDtypeStruct(shap...]
    dot_general x1 -> x0, matrix products: 18.3 us -> none  [paired_local(): jnp.einsum('hqk,khd->qhd', probs, vh, preferred_element_type=f32).astype(bf)]
    reduce_sum x1 -> x0, other arithmetic: 16.3 us -> none  [paired_local(): exp_total = jnp.sum(exp_scores, axis=-1, keepdims=True)]
  transfers between devices with their start and end apart: 28 -> 27, of which waited for: 10 -> 8; matrix products, arithmetic and copies ran while one was open for 28% -> 42% of each run, Pallas kernels for 25% -> 0%
where the time goes in v2:
time: 717 us; the launch traced here: 711 us
  Pallas kernels  182 us (25%)
  matrix products  157 us (22%)
  other arithmetic  99.9 us (14%)
  local copies, waits for them, and re-layouts  98.2 us (14%)
  waiting for transfers between devices  72.7 us (10%)
  blocking collectives  66 us (9%)
  starting transfers between devices  20 us (3%)
  between operations  15.3 us (2%)
    pallas_call x1, Pallas kernels, run_forward(): pl.pallas_call(forward_kernel, out_shape=tuple((jax.ShapeDtypeStruct(shap...  182 us
    psum x1, blocking collectives, paired_local(): packed = lax.psum(packed, ('cells', 'chrom'))  66 us
    ppermute x17, waiting for transfers between devices, flip(): return lax.ppermute(value, 'cells', [(n, n ^ step) for n in range(count)])  64.7 us
    convert_element_type x1, other arithmetic, paired_local(): grad_raw = (again * (grad_probs - row_dot)).astype(bf)  35 us
    dot_general x4, matrix products, right_back(): jnp.einsum('rb,ab->ra', left, right, preferred_element_type=jnp.float32)  33.3 us
    dot_general x1, matrix products, paired_local(): grad_probs = jnp.einsum('qhd,khd->hqk', gh, vh, preferred_element_type=f32)  28.8 us
    dot_general x4, matrix products, left_product(): jnp.einsum('ra,rb->ab', left, right, preferred_element_type=jnp.float32)  28.1 us
    convert_element_type x3, local copies, waits for them, and re-layouts, paired_local(): w1_grad = w1_grad.reshape(rows, LINE * hid).astype(f32)  26.8 us
  transfers between devices with their start and end apart: 27, of which 8 were waited for; matrix products, arithmetic and copies ran while one was open for 42% of the time, Pallas kernels for 0%

profile of v2, /device:TPU:0, one launch (start us, length us, event | category | flops | bytes accessed | tf_op | source)
XLA Modules:
  0.0 711.0 jit_solution(13668224885836102634)
XLA Ops:
  18.2 182.3 %forward.1 = (f32[16,1280]{1,0:T(8,128)}, bf16[1024,1280]{1,0:T(8,128)(2,1)}, bf16[1024,1280]{1,0:T(8,128)(2,1)}, bf16[1280,1920]{1,0:T(8,128)(2,1)}, bf16[640,1...) custom-call(bf16[16,384]{1,0:T(8,128)(2,1)} %pad.4.small_ref, ...), custom_call_target="tpu_custom_call" | custom-call | tf_op jit(solution)/shard_map/forward/pallas_call | solution.py:901
  210.1 10.0 %convolution_convert_fusion = bf16[2560,1280]{1,0:T(8,128)(2,1)S(1)} fusion(bf16[1024,2560]{1,0:T(8,128)(2,1)} %get-tuple-element.33, bf16[1024,1280]{1,0:T(8,128)(2,1)} %get-tuple-element.36, pred[1024]{0:T(1024)(128)(4,1)S(1)} %iota_compare_fusion.2), kind=kOutput, calls=%fused_computation.5 | convolution fusion | flops 6715473920 | bytes 14418944 | tf_op jit(solution)/shard_map/ra,rb->ab/dot_general | solution.py:33
  227.9 11.2 %convert_reduce_fusion = (f32[2560]{0:T(1024)}, bf16[1024,2560]{1,0:T(8,128)(2,1)}) fusion(bf16[1024,2560]{1,0:T(8,128)(2,1)} %get-tuple-element.37, bf16[2560,1280]{1,0:T(8,128)(2,1)S(1)} %bitcast.208, bf16[1024,1280]{1,0:T(8,128)(2,1)S(1)} %copy-done.16, pred[1024]{0:T(1024)(128)(4,1)S(1)} %iota_compare_fusion.2), kind=kOutput, calls=%fused_computation.7 | convolution fusion | flops 6725301760 | bytes 19672064 | tf_op jit(solution)/shard_map/rb,ab->ra/dot_general | solution.py:37
  239.2 12.2 %convolution_convert_fusion.3 = bf16[1024,1280]{1,0:T(8,128)(2,1)} fusion(bf16[1024,2560]{1,0:T(8,128)(2,1)} %get-tuple-element.115, bf16[1280,2560]{1,0:T(8,128)(2,1)} %get-tuple-element.38), kind=kOutput, calls=%fused_computation.25 | convolution fusion | flops 6712197120 | bytes 14417920 | tf_op jit(solution)/shard_map/rb,ab->ra/dot_general | solution.py:37
  251.4 7.3 %convolution_convert_fusion.1 = bf16[1280,2560]{1,0:T(8,128)(2,1)S(1)} fusion(bf16[1024,1280]{1,0:T(8,128)(2,1)S(1)} %copy-done.34, bf16[1024,2560]{1,0:T(8,128)(2,1)S(1)} %copy-done.37), kind=kOutput, calls=%fused_computation.6 | convolution fusion | flops 6714163200 | bytes 14417920 | tf_op jit(solution)/shard_map/ra,rb->ab/dot_general | solution.py:33
  266.5 16.2 %fusion.55 = f32[10,1024,1024]{1,2,0:T(8,128)} fusion(bf16[1024,10,64]{0,2,1:T(8,128)(2,1)S(1)} %bitcast.168, bf16[1024,10,64]{0,2,1:T(8,128)(2,1)S(1)} %bitcast.170), kind=kOutput, calls=%fused_computation.191 | convolution fusion | flops 1342177280 | bytes 44564480 | tf_op jit(solution)/shard_map/qhd,khd->hqk/dot_general | solution.py:1009
  310.4 11.3 %collective-permute-done.20 = bf16[2,160,1280]{2,1,0:T(8,128)(2,1)S(1)} collective-permute-done((bf16[2,160,1280]{2,1,0:T(8,128)(2,1)S(1)}, bf16[2,160,1280]{2,1,0:T(8,128)(2,1)S(1)}, u32[]{:S(2)}, u32[]{:S(2)}) %collective-permute-start.20) | collective-permute-done | bytes 819232 | tf_op jit(solution)/shard_map/ppermute | solution.py:921
  323.6 7.0 multiply_reduce_fusion.1
  341.5 17.3 %convert_reduce_fusion.4 = (f32[10,64]{1,0:T(8,128)S(1)}, bf16[10,64,1024]{2,1,0:T(8,128)(2,1)}) fusion(bf16[1024,10,64]{0,2,1:T(8,128)(2,1)S(1)} %bitcast.188, f32[10,1024,1024]{1,2,0:T(8,128)} %fusion.55, f32[10,1024]{1,0:T(8,128)S(1)} %bitcast.198, f32[1024,1024]{0,1:T(8,128)S(1)} %copy-done), kind=kOutput, calls=%fused_computation.52 | convolution fusion | flops 1386085760 | bytes 48802304 | tf_op jit(solution)/shard_map/hqk,qhd->khd/dot_general | solution.py:1039
  358.8 28.8 %multiply_reduce_fusion = (f32[10,1024]{1,0:T(8,128)S(1)}, f32[10,1024,1024]{1,2,0:T(8,128)}) fusion(f32[10,1024,1024]{1,2,0:T(8,128)} %fusion.55, f32[10,1024]{1,0:T(8,128)S(1)} %bitcast.199, f32[1024,1024]{0,1:T(8,128)S(1)} %copy-done, bf16[1024,10,64]{0,2,1:T(8,128)(2,1)} %bitcast.189, bf16[1024,10,64]{0,2,1:T(8,128)(2,1)} %bitcast.190), kind=kOutput, calls=%fused_computation.1 | convolution fusion | flops 1394595840 | bytes 90783744 | tf_op jit(solution)/shard_map/qhd,khd->hqk/dot_general | solution.py:1036
  387.6 35.0 %multiply_convert_fusion = bf16[10,1024,1024]{1,2,0:T(8,128)(2,1)} fusion(f32[10,1024,1024]{1,2,0:T(8,128)} %get-tuple-element.109, f32[10,1024,1024]{1,2,0:T(8,128)} %fusion.55, f32[10,1024]{1,0:T(8,128)S(1)} %get-tuple-element.108, f32[10,1024]{1,0:T(8,128)S(1)} %bitcast.200, f32[1024,1024]{0,1:T(8,128)S(1)} %copy-done), kind=kLoop, calls=%fused_computation | loop fusion | flops 62914560 | bytes 109133824 | tf_op jit(solution)/shard_map/convert_element_type | solution.py:1038
  422.6 10.9 %multiply_convert_fusion.2 = bf16[10,64,1024]{2,1,0:T(8,128)(2,1)S(1)} fusion(bf16[1024,10,64]{0,2,1:T(8,128)(2,1)S(1)} %bitcast.169, bf16[10,1024,1024]{1,2,0:T(8,128)(2,1)} %multiply_convert_fusion), kind=kOutput, calls=%fused_computation.57 | convolution fusion | flops 1343488000 | bytes 23592960 | tf_op jit(solution)/shard_map/hqk,qhd->khd/dot_general | solution.py:1040
  433.5 11.4 %convert_reduce_fusion.5 = (f32[10,64]{1,0:T(8,128)S(1)}, bf16[10,64,1024]{2,1,0:T(8,128)(2,1)S(1)}) fusion(bf16[1024,10,64]{0,2,1:T(8,128)(2,1)S(1)} %bitcast.171, bf16[10,1024,1024]{1,2,0:T(8,128)(2,1)} %multiply_convert_fusion), kind=kOutput, calls=%fused_computation.53 | convolution fusion | flops 1344798080 | bytes 23595520 | tf_op jit(solution)/shard_map/hqk,khd->qhd/dot_general | solution.py:1041
  451.2 5.9 convolution_convert_fusion.2
  468.6 28.7 %collective-permute-done.11 = bf16[2,2,80,2560]{3,2,0,1:T(8,128)(2,1)} collective-permute-done((bf16[2,2,80,2560]{3,2,0,1:T(8,128)(2,1)}, bf16[2,2,80,2560]{3,2,0,1:T(8,128)(2,1)}, u32[]{:S(2)}, u32[]{:S(2)}) %collective-permute-start.11) | collective-permute-done | bytes 1638432 | tf_op jit(solution)/shard_map/ppermute | solution.py:921
  504.4 14.2 %collective-permute-done.12 = bf16[2,80,2560]{2,1,0:T(8,128)(2,1)S(1)} collective-permute-done((bf16[2,80,2560]{2,1,0:T(8,128)(2,1)S(1)}, bf16[2,80,2560]{2,1,0:T(8,128)(2,1)S(1)}, u32[]{:S(2)}, u32[]{:S(2)}) %collective-permute-start.12) | collective-permute-done | bytes 819232 | tf_op jit(solution)/shard_map/ppermute | solution.py:921
  524.3 10.8 %fusion.54 = f32[1024,1280]{1,0:T(8,128)S(1)} fusion(bf16[1024,2560]{1,0:T(8,128)(2,1)} %get-tuple-element.33, bf16[2560,1280]{1,0:T(8,128)(2,1)} %get-tuple-element.34), kind=kOutput, calls=%fused_computation.190 | convolution fusion | flops 6710886400 | bytes 17039360 | tf_op jit(solution)/shard_map/dot_general | solution.py:29
  548.6 8.0 %fusion.25 = f32[1024,1280]{1,0:T(8,128)S(1)} fusion(bf16[1280,1920]{1,0:T(8,128)(2,1)} %get-tuple-element.42, bf16[1024,640]{0,1:T(8,128)(2,1)S(1)} %bitcast.202, bf16[1024,640]{0,1:T(8,128)(2,1)S(1)} %bitcast.193, bf16[1024,640]{0,1:T(8,128)(2,1)S(1)} %bitcast.204), kind=kOutput, calls=%fused_computation.90 | convolution fusion | flops 5044961280 | bytes 14090240 | tf_op jit(solution)/shard_map/rb,ab->ra/dot_general | solution.py:37
  564.2 6.9 collective-permute-done.3
  585.1 66.0 %psum.7 = f32[12,1280]{1,0:T(8,128)S(1)} all-reduce(f32[12,1280]{1,0:T(8,128)S(1)} %reshape.320), channel_id=1, replica_groups=mesh['cells'=8,'chrom'=4] {'cells','chrom'}, use_global_device_ids=true, to_apply=%region_19.20 | all-reduce | flops 15360 | bytes 122880 | tf_op jit(solution)/shard_map/psum | solution.py:1074
  661.8 7.1 reshape.340
  668.9 10.6 %copy.161 = f32[4,80,4,2,640]{4,3,2,1,0:T(2,128)} copy(f32[4,80,4,2,640]{4,2,1,3,0:T(4,128)} %bitcast.167) | data formatting | bytes 13107200 | tf_op jit(solution)/shard_map/convert_element_type | solution.py:1083
  679.5 9.1 %reshape.334 = f32[320,5120]{1,0:T(8,128)} reshape(f32[4,80,4,2,640]{4,3,2,1,0:T(2,128)} %copy.161) | data formatting | bytes 13107200 | tf_op jit(solution)/shard_map/convert_element_type | solution.py:1083
  688.6 5.8 reshape_reshape.2
  (282 shorter events, 162.0 us)
Async XLA Ops:
  7.2 516.0 %reduce-scatter.8.cloned.1.call-start = ((), (), s32[]{:S(2)}) async-start(), calls=%async_computation.7 | async-start | bytes 2048000 | tf_op jit(solution)/shard_map/reduce_scatter | solution.py:944
  225.9 66.7 %collective-permute-start.19 = (bf16[2,2,160,1280]{3,2,0,1:T(8,128)(2,1)}, bf16[2,2,160,1280]{3,2,0,1:T(8,128)(2,1)}, u32[]{:S(2)}, u32[]{:S(2)}) collective-permute-start(bf16[2,2,160,1280]{3,2,0,1:T(8,128)(2,1)} %bitcast.157), channel_id=1, source_target_pairs={{0,16},{4,20},{8,24},{12,28},{16,0},{20,4},{24,8},{28,12},{1,17},{... | collective-permute-start | bytes 4915208 | tf_op jit(solution)/shard_map/ppermute | solution.py:921
  227.4 68.1 %collective-permute-start.17 = (bf16[2,2,160,1280]{3,2,0,1:T(8,128)(2,1)}, bf16[2,2,160,1280]{3,2,0,1:T(8,128)(2,1)}, u32[]{:S(2)}, u32[]{:S(2)}) collective-permute-start(bf16[2,2,160,1280]{3,2,0,1:T(8,128)(2,1)} %bitcast.158), channel_id=1, source_target_pairs={{0,8},{4,12},{8,0},{12,4},{16,24},{20,28},{24,16},{28,20},{1,9},{5... | collective-permute-start | bytes 4915208 | tf_op jit(solution)/shard_map/ppermute | solution.py:921
  251.4 72.2 %collective-permute-start.4 = (bf16[1024,1280]{1,0:T(8,128)(2,1)}, bf16[1024,1280]{1,0:T(8,128)(2,1)}, u32[]{:S(2)}, u32[]{:S(2)}) collective-permute-start(bf16[1024,1280]{1,0:T(8,128)(2,1)} %convolution_convert_fusion.3), channel_id=1, source_target_pairs={{0,4},{4,0},{8,12},{12,8},{16,20},{20,16},{24,28},{28,24},{1,5},{5... | collective-permute-start | bytes 7864328 | tf_op jit(solution)/shard_map/ppermute | solution.py:921
  264.4 38.9 %collective-permute-start.15 = (bf16[2,2,80,2560]{3,2,0,1:T(8,128)(2,1)}, bf16[2,2,80,2560]{3,2,0,1:T(8,128)(2,1)}, u32[]{:S(2)}, u32[]{:S(2)}) collective-permute-start(bf16[2,2,80,2560]{3,2,0,1:T(8,128)(2,1)} %bitcast.159), channel_id=1, source_target_pairs={{0,16},{4,20},{8,24},{12,28},{16,0},{20,4},{24,8},{28,12},{1,17},{... | collective-permute-start | bytes 4915208 | tf_op jit(solution)/shard_map/ppermute | solution.py:921
  265.3 41.7 %collective-permute-start.13 = (bf16[2,2,80,2560]{3,2,0,1:T(8,128)(2,1)}, bf16[2,2,80,2560]{3,2,0,1:T(8,128)(2,1)}, u32[]{:S(2)}, u32[]{:S(2)}) collective-permute-start(bf16[2,2,80,2560]{3,2,0,1:T(8,128)(2,1)} %bitcast.160), channel_id=1, source_target_pairs={{0,8},{4,12},{8,0},{12,4},{16,24},{20,28},{24,16},{28,20},{1,9},{5... | collective-permute-start | bytes 4915208 | tf_op jit(solution)/shard_map/ppermute | solution.py:921
  294.6 27.1 %collective-permute-start.20 = (bf16[2,160,1280]{2,1,0:T(8,128)(2,1)S(1)}, bf16[2,160,1280]{2,1,0:T(8,128)(2,1)S(1)}, u32[]{:S(2)}, u32[]{:S(2)}) collective-permute-start(bf16[2,160,1280]{2,1,0:T(8,128)(2,1)S(1)} %dynamic-slice_bitcast_fusion), channel_id=1, source_target_pairs={{0,8},{4,12},{8,0},{12,4},{16,24},{20,28},{24,16},{28,20},{1,9},{5... | collective-permute-start | bytes 2457608 | tf_op jit(solution)/shard_map/ppermute | solution.py:921
  297.6 24.3 %collective-permute-start.18 = (bf16[2,160,1280]{2,1,0:T(8,128)(2,1)S(1)}, bf16[2,160,1280]{2,1,0:T(8,128)(2,1)S(1)}, u32[]{:S(2)}, u32[]{:S(2)}) collective-permute-start(bf16[2,160,1280]{2,1,0:T(8,128)(2,1)S(1)} %dynamic-slice_bitcast_fusion.1), channel_id=1, source_target_pairs={{0,16},{4,20},{8,24},{12,28},{16,0},{20,4},{24,8},{28,12},{1,17},{... | collective-permute-start | bytes 2457608 | tf_op jit(solution)/shard_map/ppermute | solution.py:921
  305.4 155.7 %collective-permute-start.16 = (bf16[2,80,2560]{2,1,0:T(8,128)(2,1)S(1)}, bf16[2,80,2560]{2,1,0:T(8,128)(2,1)}, u32[]{:S(2)}, u32[]{:S(2)}) collective-permute-start(bf16[2,80,2560]{2,1,0:T(8,128)(2,1)S(1)} %dynamic-slice_bitcast_fusion.2), channel_id=1, source_target_pairs={{0,8},{4,12},{8,0},{12,4},{16,24},{20,28},{24,16},{28,20},{1,9},{5... | collective-permute-start | bytes 2457608 | tf_op jit(solution)/shard_map/ppermute | solution.py:921
  310.0 155.5 %collective-permute-start.14 = (bf16[2,80,2560]{2,1,0:T(8,128)(2,1)}, bf16[2,80,2560]{2,1,0:T(8,128)(2,1)}, u32[]{:S(2)}, u32[]{:S(2)}) collective-permute-start(bf16[2,80,2560]{2,1,0:T(8,128)(2,1)} %dynamic-slice_bitcast_fusion.3), channel_id=1, source_target_pairs={{0,16},{4,20},{8,24},{12,28},{16,0},{20,4},{24,8},{28,12},{1,17},{... | collective-permute-start | bytes 2457608 | tf_op jit(solution)/shard_map/ppermute | solution.py:921
  323.5 200.3 %reduce-scatter.6.cloned.1.call-start = ((), (), s32[]{:S(2)}) async-start(), calls=%async_computation.5 | async-start | bytes 2048000 | tf_op jit(solution)/shard_map/reduce_scatter | solution.py:944
  459.8 37.5 %collective-permute-start.11 = (bf16[2,2,80,2560]{3,2,0,1:T(8,128)(2,1)}, bf16[2,2,80,2560]{3,2,0,1:T(8,128)(2,1)}, u32[]{:S(2)}, u32[]{:S(2)}) collective-permute-start(bf16[2,2,80,2560]{3,2,0,1:T(8,128)(2,1)} %bitcast.161), channel_id=1, source_target_pairs={{0,16},{4,20},{8,24},{12,28},{16,0},{20,4},{24,8},{28,12},{1,17},{... | collective-permute-start | bytes 4915208 | tf_op jit(solution)/shard_map/ppermute | solution.py:921
  464.0 37.8 %collective-permute-start.9 = (bf16[2,2,80,2560]{3,2,0,1:T(8,128)(2,1)}, bf16[2,2,80,2560]{3,2,0,1:T(8,128)(2,1)}, u32[]{:S(2)}, u32[]{:S(2)}) collective-permute-start(bf16[2,2,80,2560]{3,2,0,1:T(8,128)(2,1)} %bitcast.162), channel_id=1, source_target_pairs={{0,8},{4,12},{8,0},{12,4},{16,24},{20,28},{24,16},{28,20},{1,9},{5... | collective-permute-start | bytes 4915208 | tf_op jit(solution)/shard_map/ppermute | solution.py:921
  468.2 105.1 %reduce-scatter.4.cloned.1.call-start = ((), (), s32[]{:S(2)}) async-start(), calls=%async_computation.3 | async-start | bytes 2048000 | tf_op jit(solution)/shard_map/reduce_scatter | solution.py:944
  499.2 19.4 %collective-permute-start.12 = (bf16[2,80,2560]{2,1,0:T(8,128)(2,1)S(1)}, bf16[2,80,2560]{2,1,0:T(8,128)(2,1)S(1)}, u32[]{:S(2)}, u32[]{:S(2)}) collective-permute-start(bf16[2,80,2560]{2,1,0:T(8,128)(2,1)S(1)} %dynamic-slice_bitcast_fusion.4), channel_id=1, source_target_pairs={{0,8},{4,12},{8,0},{12,4},{16,24},{20,28},{24,16},{28,20},{1,9},{5... | collective-permute-start | bytes 2457608 | tf_op jit(solution)/shard_map/ppermute | solution.py:921
  503.6 17.9 %collective-permute-start.10 = (bf16[2,80,2560]{2,1,0:T(8,128)(2,1)S(1)}, bf16[2,80,2560]{2,1,0:T(8,128)(2,1)S(1)}, u32[]{:S(2)}, u32[]{:S(2)}) collective-permute-start(bf16[2,80,2560]{2,1,0:T(8,128)(2,1)S(1)} %dynamic-slice_bitcast_fusion.5), channel_id=1, source_target_pairs={{0,16},{4,20},{8,24},{12,28},{16,0},{20,4},{24,8},{28,12},{1,17},{... | collective-permute-start | bytes 2457608 | tf_op jit(solution)/shard_map/ppermute | solution.py:921
  523.1 132.7 %all-gather.8.cloned.1.call-start = ((), (), s32[]{:S(2)}) async-start(), calls=%async_computation.8 | async-start | bytes 3686400 | tf_op jit(solution)/shard_map/all_gather | solution.py:945
  523.7 138.1 %all-gather.6.cloned.1.call-start = ((), (), s32[]{:S(2)}) async-start(), calls=%async_computation.6 | async-start | bytes 3686400 | tf_op jit(solution)/shard_map/all_gather | solution.py:945
  524.3 164.3 %all-gather.4.cloned.1.call-start = ((), (), s32[]{:S(2)}) async-start(), calls=%async_computation.4 | async-start | bytes 3686400 | tf_op jit(solution)/shard_map/all_gather | solution.py:945
  546.7 16.6 %collective-permute-start.2 = (bf16[256,1280]{1,0:T(8,128)(2,1)}, bf16[256,1280]{1,0:T(8,128)(2,1)S(1)}, u32[]{:S(2)}, u32[]{:S(2)}) collective-permute-start(bf16[256,1280]{1,0:T(8,128)(2,1)} %get-tuple-element.96), channel_id=1, source_target_pairs={{0,0},{1,1},{2,4},{3,5},{4,2},{5,3},{6,6},{7,7},{8,8},{9,9},{10,12... | collective-permute-start | bytes 1966088 | tf_op jit(solution)/shard_map/ppermute | solution.py:961
  548.6 22.4 %collective-permute-start.3 = (bf16[256,1280]{1,0:T(8,128)(2,1)}, bf16[256,1280]{1,0:T(8,128)(2,1)}, u32[]{:S(2)}, u32[]{:S(2)}) collective-permute-start(bf16[256,1280]{1,0:T(8,128)(2,1)} %get-tuple-element.97), channel_id=1, source_target_pairs={{0,1},{1,0},{2,5},{3,4},{4,3},{5,2},{6,7},{7,6},{8,9},{9,8},{10,13... | collective-permute-start | bytes 1966088 | tf_op jit(solution)/shard_map/ppermute | solution.py:961
  560.2 16.0 %collective-permute-start.5 = (bf16[512,1280]{1,0:T(8,128)(2,1)}, bf16[512,1280]{1,0:T(8,128)(2,1)}, u32[]{:S(2)}, u32[]{:S(2)}) collective-permute-start(bf16[512,1280]{1,0:T(8,128)(2,1)} %dynamic-slice_convert_fusion), channel_id=1, source_target_pairs={{0,4},{4,0},{8,12},{12,8},{16,20},{20,16},{24,28},{28,24},{1,5},{5... | collective-permute-start | bytes 3932168 | tf_op jit(solution)/shard_map/ppermute | solution.py:921
  583.4 71.1 %collective-permute-start.6 = (bf16[256,1280]{1,0:T(8,128)(2,1)S(1)}, bf16[256,1280]{1,0:T(8,128)(2,1)S(1)}, u32[]{:S(2)}, u32[]{:S(2)}) collective-permute-start(bf16[256,1280]{1,0:T(8,128)(2,1)S(1)} %get-tuple-element.92), channel_id=1, source_target_pairs={{0,0},{1,1},{2,4},{3,5},{4,2},{5,3},{6,6},{7,7},{8,8},{9,9},{10,12... | collective-permute-start | bytes 1966088 | tf_op jit(solution)/shard_map/ppermute | solution.py:961
  584.1 70.4 %collective-permute-start.7 = (bf16[256,1280]{1,0:T(8,128)(2,1)S(1)}, bf16[256,1280]{1,0:T(8,128)(2,1)S(1)}, u32[]{:S(2)}, u32[]{:S(2)}) collective-permute-start(bf16[256,1280]{1,0:T(8,128)(2,1)S(1)} %get-tuple-element.93), channel_id=1, source_target_pairs={{0,1},{1,0},{2,5},{3,4},{4,3},{5,2},{6,7},{7,6},{8,9},{9,8},{10,13... | collective-permute-start | bytes 1966088 | tf_op jit(solution)/shard_map/ppermute | solution.py:961
  (47 other events, 264.8 us)
Sparse Core Ops, SparseCore 0:
  323.6 35.5 reduce-scatter.7
  468.3 34.3 reduce-scatter.5
  523.2 41.4 reduce-scatter.3
  566.6 33.1 all-gather.7
  601.7 33.0 all-gather.5
  636.6 33.2 all-gather.3

commit v3 on v2

--- a/solution.py
+++ b/solution.py
@@ -400,6 +400,7 @@
 
 PLANE = 4
 LINE = 4
+VMEM_LIMIT = 62 * 1024 * 1024
 
 
 def rows_of(start, count):
@@ -814,7 +815,7 @@
     def second_rows(n, _):
         at = pl.ds(pl.multiple_of(n * 64, 64), 64)
         sums = xf[at, :].astype(f32) + (part[at, :].astype(f32) + part_in[at, :].astype(f32) + vec[4:5, :])
-        middle[at, :] = sums
+        middle[at, :] = sums.astype(bf)
         center, r = moments(sums)
         second[at, :] = (center * r * vec[5:6, :] + vec[6:7, :]).astype(bf)
         return _
@@ -889,13 +890,13 @@
     made = [
         ((small.shape[0], feat), f32), ((seq, feat), bf), ((seq, feat), bf), ((feat, 3 * half), bf), ((half, feat), bf),
         ((feat, 2 * hid), bf), ((2 * hid, feat), bf), ((seq, feat), bf), ((seq, 3 * half), bf), ((seq, half), bf),
-        ((16, seq), f32), ((seq, feat), f32), ((seq, feat), bf), ((seq, 2 * hid), bf), ((seq, 2 * hid), bf),
+        ((16, seq), f32), ((seq, feat), bf), ((seq, feat), bf), ((seq, 2 * hid), bf), ((seq, 2 * hid), bf),
     ]
     held = [
         ((LINE,) + small.shape, bf), ((small.shape[0], feat), f32), ((1, 2 * hid), f32), ((seq, feat), bf), ((seq, feat), bf),
         ((feat, 3 * half), bf), ((feat, half), bf), ((half, feat), bf), ((feat, 2 * hid), bf), ((seq, feat), bf),
         ((seq, 3 * half), bf), ((seq, 128), bf), ((seq, 128), bf), ((seq, 256), bf), ((seq, half), bf),
-        ((16, seq), f32), ((seq, feat), bf), ((seq, feat), bf), ((seq, feat), f32), ((seq, feat), bf),
+        ((16, seq), f32), ((seq, feat), bf), ((seq, feat), bf), ((seq, feat), bf), ((seq, feat), bf),
         ((2, seq, TILE), bf), ((2, seq, TILE), bf),
     ]
     return pl.pallas_call(
@@ -910,10 +911,622 @@
             dma((4,)), dma((4,)), dma((16,)), dma((2, 2)),
         ],
         compiler_params=pltpu.CompilerParams(
-            collective_id=0, has_side_effects=True, vmem_limit_bytes=60 * 1024 * 1024
+            collective_id=0, has_side_effects=True, vmem_limit_bytes=VMEM_LIMIT
         ),
         name="forward",
     )(small, x, ct, wq, wk, wv, wo, w1, w2, gq, gk)
+
+
+def tn(left, right):
+    return lax.dot_general(left, right, (((0,), (0,)), ((), ())), preferred_element_type=jnp.float32)
+
+
+def backward_kernel(
+    vec_ref, x_ref, ct_ref, wa_ref, wob_ref, wb_ref, wc_ref, normed_ref, qkv_ref, mixed_ref, lse_ref, middle_ref,
+    second_ref, active_ref, slope_ref, gq_ref, gk_ref,
+    block_o, input_o, w2_o, w1_o, q_o, k_o, v_o, o_o, small_o,
+    vec, up, big, two, three, wts, dc, db, do, r1c, r2c, zc, r1b, r2b, zb, r1o, r2a, za, kx, gq, gk, lse, half_in, home,
+    acc, stage, sums, sums_in, bias_row, dkv,
+    ld, us, ur, hs, hr, cs, cr, ss, sr, os, free_x, free_y,
+):
+    f32, bf = jnp.float32, jnp.bfloat16
+    i, z = lax.axis_index("cells"), lax.axis_index("chrom")
+    p, c = i // 2, lax.rem(i, 2)
+    px, py = lax.rem(p, 2), p // 2
+    x_nb, y_nb, core_nb = i + 2 - 4 * px, i + 4 - 8 * py, i + 1 - 2 * c
+    p_x, p_y = p + 1 - 2 * px, p + 2 - 4 * py
+    seq, feat = up.shape
+    half, half_seq, block = feat // 2, seq // 2, seq // LINE
+    rows = feat // LINE
+    hid = wc_ref.shape[0] // 2
+    chunks = seq // TILE
+    mesh_id = pl.DeviceIdType.MESH
+
+    barrier = pltpu.get_barrier_semaphore()
+    line_ids = [
+        (i - c + lax.rem(c + dc_, 2), lax.rem(z + dz, LINE))
+        for dc_ in range(2)
+        for dz in range(LINE)
+        if dc_ or dz
+    ]
+    for who in line_ids + [(x_nb, z), (y_nb, z)]:
+        pl.semaphore_signal(barrier, inc=1, device_id=who, device_id_type=mesh_id)
+
+    loads = {}
+
+    def load(name, pairs):
+        n = len(loads)
+        copies = [pltpu.make_async_copy(src, dst, ld.at[n, m]) for m, (src, dst) in enumerate(pairs)]
+        loads[name] = copies
+        for d in copies:
+            d.start()
+
+    def loaded(*names):
+        for name in names:
+            for d in loads[name]:
+                d.wait()
+
+    load("ct", [(ct_ref, up)])
+    load("marks", [(gk_ref, gk), (gq_ref, gq), (vec_ref, vec), (lse_ref, lse)])
+    load("active", [(active_ref, big)])
+    load("wc", [(wc_ref, wts)])
+    load("mid half", [(middle_ref.at[rows_of(c * half_seq, half_seq), :], home)])
+    load("slope", [(slope_ref, db.at[pl.ds(0, seq), :])])
+    load("second", [(second_ref, two)])
+
+    def send(src, dst, s, r, who):
+        return pltpu.make_async_remote_copy(
+            src_ref=src, dst_ref=dst, send_sem=s, recv_sem=r, device_id=who, device_id_type=mesh_id
+        )
+
+    class Unit:
+        def __init__(self, n, d, col, r, w, r1, r2, zl, parts):
+            self.n, self.d, self.col, self.r, self.w = n, d, col, r, w
+            self.r1_at, self.r2_at, self.z_at, self.parts = r1, r2, zl, parts
+
+        def region(self, base, row, count=1):
+            ref, row0, col0 = base
+            return ref.at[rows_of(row0 + row * self.r, count * self.r), pl.ds(col0, self.w)]
+
+        def own(self, s, a, b):
+            return self.region((self.d, 0, self.col), (s * 2 + a) * 2 + b)
+
+        def r1(self, side, m, n):
+            return self.region(self.r1_at, (side * 2 + m) * 2 + n)
+
+        def r2(self, s):
+            return self.region(self.r2_at, s)
+
+        def zl(self, d):
+            return self.region(self.z_at, d)
+
+        def sems(self, e):
+            return us.at[self.n, e], ur.at[self.n, e]
+
+        def total(self, e, count):
+            ref = self.region(self.r1_at, 0, count)
+            return send(ref, ref, *self.sems(e), (x_nb, z))
+
+        def step1(self, s):
+            for n in range(2):
+                if s < 2:
+                    send(self.own(s, n, 1 - px), self.r1(0, s, n), *self.sems(0), (x_nb, z)).start()
+                else:
+                    send(self.own(s, 1 - py, n), self.r1(1, s - 2, n), *self.sems(1), (y_nb, z)).start()
+
+        def step1_all(self):
+            for s in (0, 2, 1, 3):
+                self.step1(s)
+
+        def add(self, to, *more):
+            value = to[...].astype(f32)
+            for ref in more:
+                value = value + ref[...].astype(f32)
+            to[...] = value.astype(bf)
+
+        def step2(self):
+            self.total(0, 4).wait_recv()
+            for m in range(2):
+                for n in range(2):
+                    self.add(self.r1(0, m, n), self.own(m, n, px))
+                send(self.r1(0, m, 1 - py), self.r2(m), *self.sems(2), (y_nb, z)).start()
+            self.total(1, 4).wait_recv()
+            for m in range(2):
+                for n in range(2):
+                    self.add(self.r1(1, m, n), self.own(2 + m, py, n))
+                send(self.r1(1, m, 1 - px), self.r2(2 + m), *self.sems(3), (x_nb, z)).start()
+
+        def line(self):
+            self.total(2, 2).wait_recv()
+            for m in range(2):
+                self.add(self.r2(m), self.r1(0, m, py))
+            self.total(3, 2).wait_recv()
+            for m in range(2):
+                self.add(self.r2(2 + m), self.r1(1, m, px))
+            for d in range(LINE - 1):
+                to = lax.rem(z + d + 1, LINE)
+                send(self.r2(to), self.zl(d), *self.sems(4 + d), (i, to)).start()
+
+        def spread(self):
+            for d in range(LINE - 1):
+                self.total(4 + d, 1).wait_recv()
+            self.add(self.r2(z), *[self.zl(d) for d in range(LINE - 1)])
+            for off, width, place in self.parts:
+                ref, row0, col0 = self.r2_at
+                src = ref.at[rows_of(row0 + z * self.r, self.r), pl.ds(col0 + off, width)]
+                dst = place(p, 0, width)
+                send(src, dst, *self.sems(7), (x_nb, z)).start()
+                send(src, dst, *self.sems(8), (y_nb, z)).start()
+                pltpu.make_async_copy(src, dst, os.at[self.n]).start()
+
+        def cross(self):
+            self.total(7, 1).wait_recv()
+            self.total(8, 1).wait_recv()
+            for off, width, place in self.parts:
+                cut = width // 256 * 128
+                left, rest = place(p_x, 0, cut), place(p_y, cut, width - cut)
+                send(left, left, *self.sems(9), (y_nb, z)).start()
+                send(rest, rest, *self.sems(10), (x_nb, z)).start()
+
+        def crossed(self, e):
+            off = 0
+            for _, width, _place in self.parts:
+                cut = width // 256 * 128
+                off += cut if e == 9 else width - cut
+            ref, row0, col0 = self.r1_at
+            ref = ref.at[rows_of(row0, self.r), pl.ds(col0, off)]
+            return send(ref, ref, *self.sems(e), (x_nb, z))
+
+        def to_core(self):
+            self.crossed(9).wait_recv()
+            self.crossed(10).wait_recv()
+            ref = self.region(self.r1_at, 0)
+            pltpu.make_async_copy(ref, ref, os.at[self.n]).wait()
+            for off, width, place in self.parts:
+                mine = place(None, 0, width)
+                send(mine, mine, *self.sems(11), (core_nb, z)).start()
+
+        def step2_sent(self):
+            self.total(2, 2).wait_send()
+            self.total(3, 2).wait_send()
+
+        def end(self):
+            self.total(11, 4).wait()
+            for e in range(4, 9):
+                self.total(e, 1).wait_send()
+            self.crossed(9).wait_send()
+            self.crossed(10).wait_send()
+
+        def step1_sent(self):
+            self.total(0, 4).wait_send()
+            self.total(1, 4).wait_send()
+
+    def place_w2(at, off, width):
+        first, count = (0, half) if at is None else (at * (hid // 2 // PLANE), hid // 2 // PLANE)
+        return w2_o.at[rows_of(c * (hid // 2) + first, count), pl.ds(off, width)]
+
+    def place_w1(n):
+        def place(at, off, width):
+            first, count = (0, rows) if at is None else (at * (rows // PLANE), rows // PLANE)
+            return w1_o.at[rows_of(first, count), cols_of(n * hid + c * (hid // 2) + off, width)]
+
+        return place
+
+    def place_of(ref):
+        def place(at, off, width):
+            first, count = (0, rows) if at is None else (at * (rows // PLANE), rows // PLANE)
+            return ref.at[rows_of(first, count), cols_of(c * half + off, width)]
+
+        return place
+
+    r_big, r_small = hid // 2 // PLANE, rows // PLANE
+    unit_c = Unit(0, dc, 0, r_big, feat, (r1c, 0, 0), (r2c, 0, 0), (zc, 0, 0), [(0, feat, place_w2)])
+    unit_b = [
+        Unit(
+            1 + n, db, n * hid, r_small, hid, (r1b, 0, n * hid), (r2b, 0, n * hid), (zb, 0, n * hid),
+            [(m * (hid // 2), hid // 2, place_w1(2 * n + m)) for m in range(2)],
+        )
+        for n in range(2)
+    ]
+    unit_o = Unit(3, do, 0, r_small, half, (r1o, 0, 0), (r2a, 0, 0), (za, 0, 0), [(0, half, place_of(o_o))])
+    spots = ((0, 0), (0, half), (8 * r_small, 0))
+    unit_a = [
+        Unit(
+            4 + n, db, n * half, r_small, half, (r1c,) + spots[n], (r2a, 0, (1 + n) * half), (za, 0, (1 + n) * half),
+            [(0, half, place_of(ref))],
+        )
+        for n, ref in enumerate((q_o, k_o, v_o))
+    ]
+
+    def going_home(src, dst, e):
+        stay = c == z // 2
+        mine, outs = None, []
+        for k in range(2):
+            b = lax.rem(z + k, 2)
+            part = src.at[rows_of(b * block, block), :]
+            to = dst.at[lax.rem(z, 2)]
+            outs.append(send(part, to, hs.at[e, k], hr.at[e, k], (i - c + z // 2, 2 * c + b)))
+            if k == 0:
+                mine = pltpu.make_async_copy(part, to, hr.at[e, k])
+
+        def start():
+            pl.when(stay)(mine.start)
+            pl.when(jnp.logical_not(stay))(outs[0].start)
+            outs[1].start()
+
+        def sent():
+            pl.when(stay)(mine.wait)
+            pl.when(jnp.logical_not(stay))(outs[0].wait_send)
+            outs[1].wait_send()
+
+        def arrived():
+            pl.when(jnp.logical_not(stay))(outs[0].wait_recv)
+            outs[1].wait_recv()
+
+        return start, sent, arrived
+
+    block_start, block_sent, block_arrived = going_home(home, block_o, 0)
+    input_start, input_sent, input_arrived = going_home(home, input_o, 1)
+
+    sums[0] = jnp.zeros(sums.shape[1:], f32)
+    loaded("ct", "marks")
+
+    def mask_rows(n, total):
+        at = pl.ds(pl.multiple_of(n * TILE, TILE), TILE)
+        gone = gk[at, 127:128].astype(f32) < 0.0
+        value = jnp.where(gone, 0.0, up[at, :].astype(f32))
+        up[at, :] = value.astype(bf)
+        return total + jnp.sum(value, axis=0, keepdims=True)
+
+    up_sum = lax.fori_loop(0, chunks, mask_rows, jnp.zeros((1, feat), f32))
+    first_core = jnp.where(c == 0, 1.0, 0.0)
+    sums[0, 7:8, :] = up_sum * first_core
+    loaded("active")
+    pl.semaphore_wait(barrier, len(line_ids) + 2)
+    wide = hid // 2
+    for s in (0, 2, 1, 3):
+        dc[s * wide : (s + 1) * wide, :] = tn(big[:, s * wide : (s + 1) * wide], up[...]).astype(bf)
+        unit_c.step1(s)
+
+    loaded("wc", "mid half")
+    swaps = []
+    for n in range(half_seq // TILE):
+        at = rows_of((1 - c) * half_seq + n * TILE, TILE)
+        to = pl.ds(n * TILE, TILE)
+        got = nn(big[at, :], wts[...]).astype(bf)
+        for m in range(2):
+            held = pl.ds(m * half_seq + n * TILE, TILE)
+            do[held, :] = got[:, m * half : (m + 1) * half]
+            send(
+                do.at[held, :], half_in.at[to, pl.ds(m * half, half)], cs.at[n], cr.at[n], (core_nb, z)
+            ).start()
+        swaps.append(send(half_in.at[to, :], half_in.at[to, :], cs.at[n], cr.at[n], (core_nb, z)))
+    for n in range(half_seq // TILE):
+        at = rows_of(c * half_seq + n * TILE, TILE)
+        to = pl.ds(n * TILE, TILE)
+        acc[...] = nn(big[at, :], wts[...])
+        swaps[n].wait_recv()
+        gone = gk[at, 127:128].astype(f32) < 0.0
+        value = home[to, :].astype(f32) + acc[...] + half_in[to, :].astype(f32) + vec[7:8, :]
+        home[to, :] = jnp.where(gone, 0.0, value).astype(bf)
+    block_start()
+
+    loaded("slope")
+
+    def inner_tile(n, _):
+        cols = pl.ds(pl.multiple_of(n * TILE, TILE), TILE)
+        got = (nt(up[...], wts[cols, :]) * db[pl.ds(0, seq), cols].astype(f32)).astype(bf)
+        big[:, cols] = got
+        bias_row[:, cols] = jnp.sum(got.astype(f32), axis=0, keepdims=True)
+        return _
+
+    lax.fori_loop(0, 2 * hid // TILE, inner_tile, 0)
+    for s in range(LINE):
+        sums[0, 8 + s : 9 + s, cols_of(c * wide, wide)] = bias_row[:, s * wide : (s + 1) * wide]
+    load("wb", [(wb_ref.at[:, pl.ds(n * hid, hid)], wts.at[pl.ds(n * feat, feat), :]) for n in range(2)])
+    loaded("second")
+    for n in range(2):
+
+        def inner_rows(m, _, n=n):
+            at = pl.ds(pl.multiple_of(m * TILE, TILE), TILE)
+            db[at, pl.ds(n * hid, hid)] = tn(two[:, at], big[:, pl.ds(n * hid, hid)]).astype(bf)
+            return _
+
+        lax.fori_loop(0, feat // TILE, inner_rows, 0)
+        unit_b[n].step1_all()
+
+    loaded("wb")
+    for d in swaps:
+        d.wait_send()
+    gs_swaps = []
+    for n in range(chunks):
+        at = pl.ds(n * TILE, TILE)
+        two[at, :] = (nt(big[at, pl.ds(0, hid)], wts[pl.ds(0, feat), :]) + nt(big[at, pl.ds(hid, hid)], wts[pl.ds(feat, feat), :])).astype(bf)
+        d = send(two.at[at, :], three.at[at, :], cs.at[2 + n], cr.at[2 + n], (core_nb, z))
+        d.start()
+        gs_swaps.append(d)
+    load("qkv", [(qkv_ref, big.at[:, pl.ds(0, 3 * half)]), (mixed_ref, big.at[:, pl.ds(3 * half, half)])])
+    load(
+        "wa",
+        [
+            (wa_ref.at[:, pl.ds(0, feat)], wts.at[pl.ds(0, feat), :]),
+            (wa_ref.at[:, pl.ds(feat, half)], wts.at[pl.ds(feat, feat), pl.ds(0, half)]),
+            (wob_ref.at[:, pl.ds(0, half)], wts.at[pl.ds(feat, half), pl.ds(half, half)]),
+            (wob_ref.at[:, pl.ds(half, half)], wts.at[pl.ds(feat + half, half), pl.ds(half, half)]),
+        ],
+    )
+    unit_c.step2()
+    unit_c.step1_sent()
+    load("middle", [(middle_ref, dc.at[pl.ds(0, seq), :])])
+    loaded("middle")
+
+    def back_rows(n, carry):
+        gain_sum, shift_sum, out_sum = carry
+        at = pl.ds(pl.multiple_of(n * 64, 64), 64)
+        g = two[at, :].astype(f32) + three[at, :].astype(f32)
+        center, r = moments(dc[at, :].astype(f32))
+        hat = center * r
+        gh = g * hat
+        h = g * vec[5:6, :]
+        first = jnp.mean(h, axis=-1, keepdims=True)
+        slant = jnp.mean(h * hat, axis=-1, keepdims=True)
+        got = (up[at, :].astype(f32) + r * (h - first - hat * slant)).astype(bf)
+        two[at, :] = got
+        return (
+            gain_sum + jnp.sum(gh, axis=0, keepdims=True),
+            shift_sum + jnp.sum(g, axis=0, keepdims=True),
+            out_sum + jnp.sum(got.astype(f32), axis=0, keepdims=True),
+        )
+
+    zero_row = jnp.zeros((1, feat), f32)
+    carry = (zero_row, zero_row, zero_row)
+    for n in range(chunks):
+        gs_swaps[n].wait()
+        carry = lax.fori_loop(n * TILE // 64, (n + 1) * TILE // 64, back_rows, carry)
+    sums[0, 5:6, :] = carry[0] * first_core
+    sums[0, 6:7, :] = carry[1] * first_core
+    sums[0, 4:5, :] = carry[2] * first_core
+    load("normed", [(normed_ref, three)])
+    load("x", [(x_ref.at[rows_of(c * half_seq, half_seq), :], up.at[pl.ds(0, half_seq), :])])
+
+    loaded("qkv", "wa")
+    stage[...] = tn(big[:, pl.ds(3 * half, half)], two[:, cols_of((1 - c) * half, half)]).astype(bf)
+    o_swap = send(stage, do.at[rows_of(c * half, half), :], cs.at[6], cr.at[6], (core_nb, z))
+    o_swap.start()
+    do[rows_of(c * half, half), :] = tn(big[:, pl.ds(3 * half, half)], two[:, cols_of(c * half, half)]).astype(bf)
+    o_swap.wait_recv()
+    unit_o.step1_all()
+    grad_mixed = (pl.ds(seq, seq), half)
+    for n in range(chunks):
+        at = pl.ds(n * TILE, TILE)
+        dc[pl.ds(seq + n * TILE, TILE), pl.ds(half, half)] = (
+            nt(two[at, pl.ds(0, half)], wts[pl.ds(feat, half), pl.ds(half, half)])
+            + nt(two[at, pl.ds(half, half)], wts[pl.ds(feat + half, half), pl.ds(half, half)])
+        ).astype(bf)
+    kx[:, 128:] = gk[...]
+
+    lane = lax.broadcasted_iota(jnp.int32, (TILE, 128), 1)
+    root = HEAD_DIM ** (-0.5)
+
+    def attend_back(t):
+        k2 = big[:, pl.ds(half + t * 128, 128)]
+        k2t = jnp.transpose(k2)
+        kx[:, :128] = k2
+        dkv[...] = jnp.zeros(dkv.shape, f32)
+
+        def chunk(n, _):
+            at = pl.ds(pl.multiple_of(n * TILE, TILE), TILE)
+            g_at = pl.ds(pl.multiple_of(seq + n * TILE, TILE), TILE)
+            q2 = big[at, pl.ds(t * 128, 128)] * jnp.array(root, bf)
+            g2 = dc[g_at, pl.ds(half + t * 128, 128)]
+            both = []
+            for h in range(2):
+                own = lane < HEAD_DIM if h == 0 else lane >= HEAD_DIM
+                qm = jnp.where(own, q2, jnp.zeros((), bf))
+                gm = jnp.where(own, g2, jnp.zeros((), bf))
+                s = nt(kx[...], jnp.concatenate([qm, gq[at, :]], axis=1))
+                prob = jnp.exp(s - lse[2 * t + h : 2 * t + h + 1, at])
+                grad = nt(big[:, pl.ds(2 * half + t * 128, 128)], gm)
+                both_of = prob * grad
+                dot = jnp.sum(both_of, axis=0, keepdims=True)
+                ds = (both_of - prob * dot).astype(bf)
+                dkv[0] += nn(ds, qm)
+                dkv[1] += nn(prob.astype(bf), gm)
+                both.append(nn(k2t[h * HEAD_DIM : (h + 1) * HEAD_DIM, :], ds))
+            dc[at, pl.ds(t * 128, 128)] = (jnp.transpose(jnp.concatenate(both, axis=0)) * root).astype(bf)
+            return _
+
+        lax.fori_loop(0, chunks, chunk, 0)
+        dc[pl.ds(0, seq), pl.ds(half + t * 128, 128)] = dkv[0].astype(bf)
+        dc[pl.ds(seq, seq), pl.ds(t * 128, 128)] = dkv[1].astype(bf)
+
+    attend_back(0)
+    unit_b[0].step2()
+    attend_back(1)
+    unit_c.line()
+    unit_c.step2_sent()
+    pl.semaphore_signal(free_x, inc=1, device_id=(x_nb, z), device_id_type=mesh_id)
+    pl.semaphore_signal(free_y, inc=1, device_id=(y_nb, z), device_id_type=mesh_id)
+    attend_back(2)
+    unit_b[1].step2()
+    unit_o.step2()
+    attend_back(3)
+    unit_b[0].line()
+    attend_back(4)
+    unit_b[1].line()
+    unit_o.line()
+    sums[0, 2:3, cols_of(c * half, half)] = jnp.sum(dc[pl.ds(0, seq), pl.ds(0, half)].astype(f32), axis=0, keepdims=True)
+    sums[0, 3:4, cols_of(c * half, half)] = jnp.sum(dc[pl.ds(seq, seq), pl.ds(0, half)].astype(f32), axis=0, keepdims=True)
+
+    loaded("normed")
+    for u in unit_b:
+        u.step1_sent()
+
+    def qk_rows(m, _):
+        at = pl.ds(pl.multiple_of(m * TILE, TILE), TILE)
+        db[at, pl.ds(0, feat)] = tn(three[:, at], dc[pl.ds(0, seq), :]).astype(bf)
+        return _
+
+    def v_rows(m, _):
+        at = pl.ds(pl.multiple_of(m * TILE, TILE), TILE)
+        db[at, pl.ds(feat, half)] = tn(three[:, at], dc[pl.ds(seq, seq), pl.ds(0, half)]).astype(bf)
+        return _
+
+    lax.fori_loop(0, feat // TILE, qk_rows, 0)
+    pl.semaphore_wait(free_x, 1)
+    pl.semaphore_wait(free_y, 1)
+    unit_a[0].step1_all()
+    unit_a[1].step1_all()
+    lax.fori_loop(0, feat // TILE, v_rows, 0)
+    unit_a[2].step1_all()
+    unit_c.spread()
+
+    def first_part(at):
+        at_v = rows_of(at + seq, TILE)
+        return nt(dc[rows_of(at, TILE), :], wts[pl.ds(0, feat), :]) + nt(
+            dc[at_v, pl.ds(0, half)], wts[pl.ds(feat, feat), pl.ds(0, half)]
+        )
+
+    loaded("x")
+    gn_swaps = []
+    for n in range(half_seq // TILE):
+        to = pl.ds(half_seq + n * TILE, TILE)
+        up[to, :] = first_part((1 - c) * half_seq + n * TILE).astype(bf)
+        d = send(up.at[to, :], half_in.at[pl.ds(n * TILE, TILE), :], cs.at[7 + n], cr.at[7 + n], (core_nb, z))
+        d.start()
+        gn_swaps.append(d)
+    unit_c.cross()
+    block_sent()
+    carry = (zero_row, zero_row)
+    for n in range(half_seq // TILE):
+        acc[...] = first_part(c * half_seq + n * TILE)
+        gn_swaps[n].wait_recv()
+
+        def first_rows(m, carry, n=n):
+            gain_sum, shift_sum = carry
+            at = pl.ds(pl.multiple_of(m * 64, 64), 64)
+            here = pl.ds(pl.multiple_of(n * TILE + m * 64, 64), 64)
+            g = acc[at, :] + half_in[here, :].astype(f32)
+            center, r = moments(up[here, :].astype(f32))
+            hat = center * r
+            gh = g * hat
+            h = g * vec[0:1, :]
+            first = jnp.mean(h, axis=-1, keepdims=True)
+            slant = jnp.mean(h * hat, axis=-1, keepdims=True)
+            got = two[rows_of(c * half_seq + n * TILE + m * 64, 64), :].astype(f32) + r * (h - first - hat * slant)
+            home[here, :] = got.astype(bf)
+            return (
+                gain_sum + jnp.sum(gh, axis=0, keepdims=True),
+                shift_sum + jnp.sum(g, axis=0, keepdims=True),
+            )
+
+        carry = lax.fori_loop(0, TILE // 64, first_rows, carry)
+    sums[0, 0:1, :] = carry[0]
+    sums[0, 1:2, :] = carry[1]
+    input_start()
+
+    def small_step(n, who):
+        d = send(sums.at[n], sums_in.at[n], ss.at[n], sr.at[n], who)
+        d.start()
+        return d
+
+    small = [small_step(0, (core_nb, z))]
+    unit_b[0].spread()
+    unit_c.to_core()
+    small[0].wait_recv()
+    sums[1] = sums[0] + sums_in[0]
+    small.append(small_step(1, (x_nb, z)))
+    unit_b[1].spread()
+    unit_a[0].step2()
+    unit_b[0].cross()
+    small[1].wait_recv()
+    sums[2] = sums[1] + sums_in[1]
+    small.append(small_step(2, (y_nb, z)))
+    unit_a[1].step2()
+    unit_b[1].cross()
+    unit_o.spread()
+    small[2].wait_recv()
+    sums[3] = sums[2] + sums_in[2]
+    for d in range(LINE - 1):
+        small.append(
+            send(sums.at[3], sums_in.at[3 + d], ss.at[3 + d], sr.at[3 + d], (i, lax.rem(z + d + 1, LINE)))
+        )
+        small[-1].start()
+    unit_a[2].step2()
+    unit_b[0].to_core()
+    unit_a[0].line()
+    unit_b[1].to_core()
+    unit_o.cross()
+    unit_a[1].line()
+    for d in range(LINE - 1):
+        small[3 + d].wait_recv()
+    sums[4] = sums[3] + ((sums_in[3] + sums_in[4]) + sums_in[5])
+    small_out = pltpu.make_async_copy(sums.at[4], small_o, os.at[7])
+    small_out.start()
+    unit_a[2].line()
+    unit_o.to_core()
+    unit_a[0].spread()
+    unit_a[1].spread()
+    unit_a[0].cross()
+    unit_a[2].spread()
+    unit_a[1].cross()
+    unit_a[0].to_core()
+    unit_a[2].cross()
+    unit_a[1].to_core()
+    unit_a[2].to_core()
+    small_out.wait()
+    for d in small + gn_swaps + [o_swap]:
+        d.wait_send()
+    input_sent()
+    block_arrived()
+    input_arrived()
+    units = [unit_c] + unit_b + [unit_o] + unit_a
+    for u in units[1:]:
+        u.step2_sent()
+    for u in [unit_o] + unit_a:
+        u.step1_sent()
+    for u in units:
+        u.end()
+
+
+def run_backward(vec, x, ct, wa, wob, wb, wc, normed, qkv, mixed, lse, middle, second, active, slope, gq, gk):
+    seq, feat = x.shape
+    half = feat // 2
+    hid = wc.shape[0] // 2
+    rows = feat // LINE
+    r_big, r_small = hid // 2 // PLANE, rows // PLANE
+    f32, bf = jnp.float32, jnp.bfloat16
+    dma = pltpu.SemaphoreType.DMA
+    anywhere = pl.BlockSpec(memory_space=pl.ANY)
+    made = [
+        ((2, seq // LINE, feat), bf), ((2, seq // LINE, feat), bf), ((hid, feat), bf), ((rows, LINE * hid), bf),
+        ((rows, feat), bf), ((rows, feat), bf), ((rows, feat), bf), ((rows, feat), bf), ((16, feat), f32),
+    ]
+    held = [
+        (vec.shape, f32), ((seq, feat), bf), ((seq, 2 * hid), bf), ((seq, feat), bf), ((seq, feat), bf),
+        ((2 * hid, feat), bf), ((2 * hid, feat), bf), ((feat, 2 * hid), bf), ((feat, half), bf),
+        ((8 * r_big, feat), bf), ((4 * r_big, feat), bf), ((3 * r_big, feat), bf),
+        ((8 * r_small, 2 * hid), bf), ((4 * r_small, 2 * hid), bf), ((3 * r_small, 2 * hid), bf),
+        ((8 * r_small, half), bf), ((4 * r_small, 4 * half), bf), ((3 * r_small, 4 * half), bf),
+        ((seq, 256), bf), ((seq, 128), bf), ((seq, 128), bf), ((16, seq), f32),
+        ((seq // 2, feat), bf), ((seq // 2, feat), bf), ((TILE, feat), f32), ((half, half), bf),
+        ((5, 16, feat), f32), ((6, 16, feat), f32), ((1, 2 * hid), f32), ((2, seq, 128), f32),
+    ]
+    return pl.pallas_call(
+        backward_kernel,
+        out_shape=tuple(jax.ShapeDtypeStruct(shape, dtype) for shape, dtype in made),
+        in_specs=[anywhere] * 17,
+        out_specs=(anywhere,) * len(made),
+        scratch_shapes=[pltpu.VMEM(shape, dtype) for shape, dtype in held]
+        + [
+            dma((14, 4)), dma((7, 12)), dma((7, 12)), dma((2, 2)), dma((2, 2)), dma((9,)), dma((9,)), dma((6,)), dma((6,)),
+            dma((8,)), pltpu.SemaphoreType.REGULAR, pltpu.SemaphoreType.REGULAR,
+        ],
+        compiler_params=pltpu.CompilerParams(
+            collective_id=1, has_side_effects=True, vmem_limit_bytes=VMEM_LIMIT
+        ),
+        name="backward",
+    )(vec, x, ct, wa, wob, wb, wc, normed, qkv, mixed, lse, middle, second, active, slope, gq, gk)
 
 
 def flip(value, step):
@@ -923,44 +1536,6 @@
 
 def take(value, index, axis):
     return lax.dynamic_index_in_dim(value, index, axis, keepdims=False)
-
-
-def plus(left, right):
-    return (left.astype(jnp.float32) + right.astype(jnp.float32)).astype(jnp.bfloat16)
-
-
-def plane_sum(value, px, py):
-    two = value.reshape((2, LINE // 2, 2, 2) + value.shape[2:])
-    first, later = two[0], two[1]
-    first = plus(take(first, px, 2), flip(take(first, 1 - px, 2), 2))
-    later = plus(take(later, py, 1), flip(take(later, 1 - py, 1), 4))
-    first = plus(take(first, py, 1), flip(take(first, 1 - py, 1), 4))
-    later = plus(take(later, px, 1), flip(take(later, 1 - px, 1), 2))
-    return jnp.concatenate([first, later], axis=0)
-
-
-def reduce_group(value, px, py):
-    mine = plane_sum(value, px, py)
-    summed = lax.psum_scatter(mine, "chrom", scatter_dimension=0, tiled=True)[0]
-    whole = lax.all_gather(summed, "cells", axis=0, tiled=False)
-    return whole.reshape((PLANE, 2) + summed.shape)
-
-
-def send_home(value, core, place):
-    half, feat = value.shape
-    two = value.reshape(2, half // 2, feat)
-    got = []
-    for k in range(2):
-        pairs = []
-        for cells in range(lax.axis_size("cells")):
-            for z in range(LINE):
-                home, c = cells - cells % 2, cells % 2
-                to_z = 2 * c + (z + k) % 2
-                pairs.append((cells * LINE + z, (home + z // 2) * LINE + to_z))
-        block = take(two, lax.rem(place + k, 2), 0)
-        got.append(lax.ppermute(block, ("cells", "chrom"), pairs))
-    even = lax.rem(place, 2) == 0
-    return jnp.stack([jnp.where(even, got[0], got[1]), jnp.where(even, got[1], got[0])])
 
 
 def paired_local(
@@ -998,94 +1573,18 @@
     ) = run_forward(
         small, inputs, cotangent, query_proj, key_proj, value_proj, output_proj, inner_proj, outer_proj, mark_q, mark_k
     )
-    gain_one, shift_one, _, _, _, gain_two, shift_two, bias_out = (vec[n] for n in range(8))
-    states = xf.astype(f32)
-    qh, kh, vh = (qkv[:, n * half : (n + 1) * half].reshape(seq, heads, HEAD_DIM) for n in range(3))
-    bias = jnp.where(live[None, :], group_bias * (groups[:, None] == groups[None, :]).astype(f32), -jnp.inf)
-    log_total = lse[:heads, :, None]
-    _, second_back = jax.vjp(layer_norm, middle, gain_two, shift_two)
-
-    def scores_of():
-        raw = jnp.einsum("qhd,khd->hqk", qh, kh, preferred_element_type=f32) * inv_root
-        return raw + bias[None]
-
-    upstream = jnp.where(live[:, None], cf, jnp.zeros((), bf))
-    out_part = product(active, wc)
-    mine = lax.dynamic_slice_in_dim(out_part, c * half_seq, half_seq, 0)
-    theirs = lax.dynamic_slice_in_dim(out_part, (1 - c) * half_seq, half_seq, 0).astype(bf)
-    result = (
-        lax.dynamic_slice_in_dim(middle, c * half_seq, half_seq, 0) + mine + flip(theirs, 1).astype(f32) + bias_out
-    )
-    live_half = lax.dynamic_slice_in_dim(live, c * half_seq, half_seq, 0)
-    block_out = send_home(jnp.where(live_half[:, None], result, 0.0).astype(bf), c, z)
-
-    outer_grad = left_product(active, upstream).astype(bf)
-    outer_sum = reduce_group(outer_grad.reshape(LINE, PLANE, hid // 2 // PLANE, feat), px, py)
-    grad_inner = (right_back(upstream, wc) * slope.astype(f32)).astype(bf)
-    inner_grad = left_product(second, grad_inner).astype(bf)
-    inner_sum = reduce_group(inner_grad.reshape(LINE, PLANE, rows // PLANE, 2 * hid), px, py)
-    second_part = right_back(grad_inner, wb).astype(bf)
-    grad_second = second_part.astype(f32) + flip(second_part, 1).astype(f32)
-    grad_norm, gain_two_grad, shift_two_grad = second_back(grad_second)
-    grad_middle = upstream.astype(f32) + grad_norm
-    grad_attended = grad_middle.astype(bf)
-    out_grad = left_product(mixed, grad_attended).astype(bf)
-    grad_mixed = right_back(grad_attended, wob).astype(bf)
-    gh = grad_mixed.reshape(seq, heads, HEAD_DIM)
-    again = jnp.exp(scores_of() - log_total)
-    grad_probs = jnp.einsum("qhd,khd->hqk", gh, vh, preferred_element_type=f32)
-    row_dot = jnp.sum(again * grad_probs, axis=-1, keepdims=True)
-    grad_raw = (again * (grad_probs - row_dot)).astype(bf)
-    dv = jnp.einsum("hqk,qhd->khd", again.astype(bf), gh, preferred_element_type=f32).astype(bf).reshape(seq, half)
-    dk = (jnp.einsum("hqk,qhd->khd", grad_raw, qh, preferred_element_type=f32) * inv_root).astype(bf).reshape(seq, half)
-    dq = (jnp.einsum("hqk,khd->qhd", grad_raw, kh, preferred_element_type=f32) * inv_root).astype(bf).reshape(seq, half)
-    dqkv = jnp.concatenate([dq, dk, dv], axis=1)
-    qkv_grad = left_product(normed, dqkv).astype(bf)
-    keep = lax.dynamic_slice_in_dim(out_grad, c * half, half, 1)
-    swap = flip(lax.dynamic_slice_in_dim(out_grad, (1 - c) * half, half, 1), 1)
-    out_cols = jnp.where(c == 0, jnp.concatenate([keep, swap], 0), jnp.concatenate([swap, keep], 0))
-    attn_grad = jnp.concatenate([qkv_grad, out_cols], axis=1)
-    attn_sum = reduce_group(attn_grad.reshape(LINE, PLANE, rows // PLANE, 2 * feat), px, py)
-    normed_part = right_back(dqkv, wa)
-    mine = lax.dynamic_slice_in_dim(normed_part, c * half_seq, half_seq, 0)
-    theirs = lax.dynamic_slice_in_dim(normed_part, (1 - c) * half_seq, half_seq, 0).astype(bf)
-    grad_normed = mine + flip(theirs, 1).astype(f32)
-    states_half = lax.dynamic_slice_in_dim(states, c * half_seq, half_seq, 0)
-    _, half_back = jax.vjp(layer_norm, states_half, gain_one, shift_one)
-    grad_states, gain_one_grad, shift_one_grad = half_back(grad_normed)
-    grad_mid_half = lax.dynamic_slice_in_dim(grad_middle, c * half_seq, half_seq, 0)
-    input_grad = send_home((grad_mid_half + grad_states).astype(bf), c, z)
-
-    def once(v):
-        return jnp.where(c == 0, v, 0.0)
-
-    def placed(v):
-        return lax.dynamic_update_slice_in_dim(jnp.zeros((feat,), f32), v, c * half, 0)
-
-    in_bias = jnp.zeros((LINE, 2, hid // 2), f32)
-    in_bias = lax.dynamic_update_slice(in_bias, column_sum(grad_inner).reshape(LINE, 1, hid // 2), (0, c, 0))
-    packed = jnp.concatenate(
-        [
-            gain_one_grad, shift_one_grad, placed(column_sum(dq)), placed(column_sum(dv)),
-            once(column_sum(grad_attended)), once(gain_two_grad), once(shift_two_grad), once(column_sum(upstream)),
-            in_bias.reshape(LINE * hid),
-        ]
-    ).reshape(12, feat)
-    packed = lax.psum(packed, ("cells", "chrom"))
-
-    def shard(v):
-        return lax.dynamic_slice_in_dim(v, z * (v.shape[0] // LINE), v.shape[0] // LINE, 0)
-
-    s = [shard(packed[n]) for n in range(8)]
-    inner_bias_grad = shard(packed[8:].reshape(LINE * hid))
-    w2_grad = outer_sum.transpose(1, 0, 2, 3).reshape(hid, feat).astype(f32)
-    w1_grad = inner_sum.reshape(PLANE, 2, rows // PLANE, LINE, hid // 2).transpose(0, 2, 3, 1, 4)
-    w1_grad = w1_grad.reshape(rows, LINE * hid).astype(f32)
-    wx = attn_sum.reshape(PLANE, 2, rows // PLANE, 4, half).transpose(3, 0, 2, 1, 4).reshape(4, rows, feat)
-    wx = [wx[n].astype(f32) for n in range(4)]
+    block_out, input_grad, w2_grad, w1_grad, q_grad, k_grad, v_grad, o_grad, sums = run_backward(
+        vec, xf, cf, wa, wob, wb, wc, normed, qkv, mixed, lse, middle, second, active, slope, mark_q, mark_k
+    )
+
+    def shard(n):
+        return lax.dynamic_slice_in_dim(sums[n], z * rows, rows, 0)
+
+    inner_bias_grad = take(sums[8:12], z, 0)
     return (
-        block_out, input_grad, s[0], s[1], wx[0], s[2], wx[1], wx[2], s[3], wx[3], s[4], s[5], s[6],
-        w1_grad, inner_bias_grad, w2_grad, s[7],
+        block_out, input_grad, shard(0), shard(1), q_grad.astype(f32), shard(2), k_grad.astype(f32),
+        v_grad.astype(f32), shard(3), o_grad.astype(f32), shard(4), shard(5), shard(6), w1_grad.astype(f32),
+        inner_bias_grad, w2_grad.astype(f32), shard(7),
     )
 
 

time: 717 us -> 471 us (0.66)
  Pallas kernels: 182 us -> 434 us
  matrix products: 157 us -> 0 us
  other arithmetic: 99.9 us -> 15.8 us
  local copies, waits for them, and re-layouts: 98.2 us -> 15.7 us
  waiting for transfers between devices: 72.7 us -> 0.01 us
  blocking collectives: 66 us -> 0 us
  starting transfers between devices: 20 us -> 0.45 us
  between operations: 15.3 us -> 0.91 us
    pallas_call x0 -> x1, Pallas kernels: none -> 253 us  [run_backward(): pl.pallas_call(backward_kernel, out_shape=tuple((jax.ShapeDtypeStruct(sha...]
    dot_general x14 -> x0, matrix products: 157 us -> none  [the longest x4 33.3 us: right_back(): jnp.einsum('rb,ab->ra', left, right, preferred_element_type=jnp.float32)]
    psum x1 -> x0, blocking collectives: 66 us -> none  [paired_local(): packed = lax.psum(packed, ('cells', 'chrom'))]
    ppermute x17 -> x1, waiting for transfers between devices: 64.7 us -> 0.01 us  [flip(): return lax.ppermute(value, 'cells', [(n, n ^ step) for n in range(count)])]
    convert_element_type x17 -> x6, other arithmetic: 57.1 us -> 13.1 us  [the longest x1 3.57 us: paired_local(): w1_grad.astype(f32)]
    convert_element_type x10 -> x0, local copies, waits for them, and re-layouts: 35.8 us -> none  [the longest x3 26.8 us: paired_local(): w1_grad = w1_grad.reshape(rows, LINE * hid).astype(f32)]
    reduce_sum x9 -> x0, other arithmetic: 26.6 us -> none  [the longest x4 10.5 us: layer_norm(): center = values - jnp.mean(values, axis=-1, keepdims=True)]
    ppermute x17 -> x1, starting transfers between devices: 15.9 us -> 0.45 us  [flip(): return lax.ppermute(value, 'cells', [(n, n ^ step) for n in range(count)])]
  transfers between devices with their start and end apart: 27 -> 1, of which waited for: 8 -> 0; matrix products, arithmetic and copies ran while one was open for 42% -> 1% of each run, Pallas kernels for 0% -> 0%
where the time goes in v3:
time: 471 us; the launch traced here: 467 us
  Pallas kernels  434 us (92%)
  other arithmetic  15.8 us (3%)
  local copies, waits for them, and re-layouts  15.7 us (3%)
    pallas_call x1, Pallas kernels, run_backward(): pl.pallas_call(backward_kernel, out_shape=tuple((jax.ShapeDtypeStruct(sha...  253 us
    pallas_call x1, Pallas kernels, run_forward(): pl.pallas_call(forward_kernel, out_shape=tuple((jax.ShapeDtypeStruct(shap...  181 us
  transfers between devices with their start and end apart: 1, of which 0 were waited for; matrix products, arithmetic and copies ran while one was open for 1% of the time, Pallas kernels for 0%

profile of v3, /device:TPU:0, one launch (start us, length us, event | category | flops | bytes accessed | tf_op | source)
XLA Modules:
  0.0 466.8 jit_solution(13156794106407563957)
XLA Ops:
  0.7 0.7 copy.37
  1.4 0.8 pad_add_fusion
  2.6 0.7 reshape.85
  3.3 0.7 reshape.86
  4.0 0.7 reshape.87
  4.7 0.7 reshape.88
  5.3 0.7 reshape.89
  6.0 0.7 reshape.90
  6.7 0.7 reshape.91
  8.1 0.8 reshape.93
  9.5 0.8 broadcast_select_fusion
  10.5 1.1 fusion.1
  11.6 181.3 %forward.1 = (f32[16,1280]{1,0:T(8,128)}, bf16[1024,1280]{1,0:T(8,128)(2,1)}, bf16[1024,1280]{1,0:T(8,128)(2,1)}, bf16[1280,1920]{1,0:T(8,128)(2,1)}, bf16[640,1...) custom-call(bf16[16,384]{1,0:T(8,128)(2,1)} %pad.4.small_ref, ...), custom_call_target="tpu_custom_call" | custom-call | tf_op jit(solution)/shard_map/forward/pallas_call | solution.py:902
  192.9 252.6 %backward.1 = (bf16[2,256,1280]{2,1,0:T(8,128)(2,1)}, bf16[2,256,1280]{2,1,0:T(8,128)(2,1)}, bf16[1280,1280]{1,0:T(8,128)(2,1)}, bf16[320,5120]{1,0:T(8,128)(2,1...) custom-call(f32[16,1280]{1,0:T(8,128)} %get-tuple-element.41.vec_ref, ...), custom_call_target="tpu_custom_call" | custom-call | tf_op jit(solution)/shard_map/backward/pallas_call | solution.py:1515
  445.5 0.9 slice.44
  446.4 1.2 fusion.11
  447.7 2.4 convert_element_type.36
  450.1 1.3 convert_element_type.37
  451.4 1.3 convert_element_type.38
  452.6 1.3 convert_element_type.39
  454.3 3.6 convert_element_type.40
  457.9 3.3 convert_element_type.41
  464.5 1.1 copy.40
  465.6 1.1 copy.41
  (29 shorter events, 5.8 us)
Async XLA Ops:
  2.2 7.4 %collective-permute-start = (s32[2,25]{1,0:T(2,128)S(1)}, s32[2,25]{1,0:T(2,128)S(1)}, u32[]{:S(2)}, u32[]{:S(2)}) collective-permute-start(s32[2,25]{1,0:T(2,128)S(1)} %pad_add_fusion), channel_id=1, source_target_pairs={{0,4},{4,0},{8,12},{12,8},{16,20},{20,16},{24,28},{28,24},{1,5},{5... | collective-permute-start | bytes 608 | tf_op jit(solution)/shard_map/ppermute | solution.py:1534
  445.5 4.6 copy-start.6
  445.5 5.8 %copy-start.5 = (bf16[320,1280]{1,0:T(8,128)(2,1)S(1)}, bf16[320,1280]{1,0:T(8,128)(2,1)}, u32[]{:S(2)}) copy-start(bf16[320,1280]{1,0:T(8,128)(2,1)} %get-tuple-element.61) | copy-start | bytes 2457604
  450.1 2.6 copy-start.4
  451.3 3.0 copy-start.1
  454.3 3.6 copy-start
  457.9 6.6 %copy-start.3 = (bf16[2,256,1280]{2,1,0:T(8,128)(2,1)S(1)}, bf16[2,256,1280]{2,1,0:T(8,128)(2,1)}, u32[]{:S(2)}) copy-start(bf16[2,256,1280]{2,1,0:T(8,128)(2,1)} %get-tuple-element.100) | copy-start | bytes 3932164
  461.2 4.4 copy-start.2

commit v4 on v3

--- a/solution.py
+++ b/solution.py
@@ -441,9 +441,9 @@
 
 
 def forward_kernel(
-    small_ref, x_ref, ct_ref, wq_ref, wk_ref, wv_ref, wo_ref, w1_ref, w2_ref, gq_ref, gk_ref,
-    vec_o, x_o, ct_o, wa_o, wob_o, wb_o, wc, normed_o, qkv_o, mixed_o, lse_o, middle_o, second_o, active_o, slope_o,
-    smalls, vec, bias_in, xf, cf, wa, wol, wob, wb, normed, qkv, gq, gk, kx, mixed, lse, part, part_in, middle, second,
+    small_ref, rag_ref, x_ref, ct_ref, wq_ref, wk_ref, wv_ref, wo_ref, w1_ref, w2_ref,
+    gq_o, gk_o, vec_o, x_o, ct_o, wa_o, wob_o, wb_o, wc, normed_o, qkv_o, mixed_o, lse_o, middle_o, second_o, active_o, slope_o,
+    smalls, rag, vec, bias_in, xf, cf, wa, wol, wob, wb, normed, qkv, gq, gk, kx, mixed, lse, part, part_in, middle, second,
     act, slp,
     sm_s, sm_r, ex_s, ex_r, fw_s, fw_r, ln_s, un_s, un_r, loc, wo_s, wo_r, pa_s, pa_r, out_s, act_s,
 ):
@@ -484,6 +484,9 @@
         for d in range(LINE - 1)
     ]
 
+    rag_own = pltpu.make_async_copy(rag_ref.at[lax.rem(z, 2)], rag.at[0], loc.at[6])
+    rag_out = send(rag_ref.at[lax.rem(z, 2)], rag.at[1], wo_s.at[1], wo_r.at[1], (core_nb, z))
+
     def exchange(src, dst, which):
         stay = c == z // 2
         mine, outs = None, []
@@ -648,51 +651,56 @@
         d.start()
         outs.append(d)
 
-    small_own.start()
-    for d in small_out:
-        d.start()
-    first(0)
-    x_start()
-    for g in groups:
-        own_start(g)
-    gq_in = pltpu.make_async_copy(gq_ref, gq, loc.at[6])
-    gk_in = pltpu.make_async_copy(gk_ref, gk, loc.at[7])
-    gq_in.start()
-    gk_in.start()
-    first(1)
-    land(0, 0)
-
-    small_own.wait()
-    for d in small_out:
-        d.wait()
-    width = smalls.shape[2]
-    total = jnp.zeros((smalls.shape[1], feat), f32)
-    at = lax.broadcasted_iota(jnp.int32, (width, feat), 0)
-    to = lax.broadcasted_iota(jnp.int32, (width, feat), 1)
-    for s in range(LINE):
-        place = jnp.where(jnp.logical_and(at < rows, to == at + s * rows), 1.0, 0.0).astype(bf)
-        total += nn(smalls[s], place)
-    vec[...] = total
-    at = lax.broadcasted_iota(jnp.int32, (width, hid // 2), 0)
-    to = lax.broadcasted_iota(jnp.int32, (width, hid // 2), 1)
-    which = lax.broadcasted_iota(jnp.int32, (smalls.shape[1], hid // 2), 0)
-    for s in range(LINE):
-        line_bias = jnp.zeros((1, hid // 2), f32)
-        for n in range(hid // 2 // rows):
-            place = jnp.where(jnp.logical_and(at < rows, to == at + n * rows), 1.0, 0.0).astype(bf)
-            picked = jnp.where(which == VECTORS + c * (hid // 2 // rows) + n, nn(smalls[s], place), 0.0)
-            line_bias += jnp.sum(picked, axis=0, keepdims=True)
-        bias_in[:, pl.ds(s * (hid // 2), hid // 2)] = line_bias
-    keep(vec, vec_o)
-
-    land(0, 1)
-    first(2)
-    turn(0, 0)
-    x_arrived()
-    for d in x_fw:
-        d.start()
-    land(0, 2)
-    turn(0, 1)
+    def begin():
+        small_own.start()
+        rag_own.start()
+        rag_out.start()
+        for d in small_out:
+            d.start()
+
+    def vectors():
+        small_own.wait()
+        for d in small_out:
+            d.wait()
+        width = smalls.shape[2]
+        total = jnp.zeros((smalls.shape[1], feat), f32)
+        at = lax.broadcasted_iota(jnp.int32, (width, feat), 0)
+        to = lax.broadcasted_iota(jnp.int32, (width, feat), 1)
+        for s in range(LINE):
+            place = jnp.where(jnp.logical_and(at < rows, to == at + s * rows), 1.0, 0.0).astype(bf)
+            total += nn(smalls[s], place)
+        vec[...] = total
+        at = lax.broadcasted_iota(jnp.int32, (width, hid // 2), 0)
+        to = lax.broadcasted_iota(jnp.int32, (width, hid // 2), 1)
+        which = lax.broadcasted_iota(jnp.int32, (smalls.shape[1], hid // 2), 0)
+        for s in range(LINE):
+            line_bias = jnp.zeros((1, hid // 2), f32)
+            for n in range(hid // 2 // rows):
+                place = jnp.where(jnp.logical_and(at < rows, to == at + n * rows), 1.0, 0.0).astype(bf)
+                picked = jnp.where(which == VECTORS + c * (hid // 2 // rows) + n, nn(smalls[s], place), 0.0)
+                line_bias += jnp.sum(picked, axis=0, keepdims=True)
+            bias_in[:, pl.ds(s * (hid // 2), hid // 2)] = line_bias
+        keep(vec, vec_o)
+
+        rag_own.wait()
+        rag_out.wait()
+        bounds = jnp.where(c == z // 2, rag[0], rag[1])
+        lanes = lax.broadcasted_iota(jnp.int32, (TILE, 128), 1)
+        for n in range(seq // TILE):
+            at = pl.ds(n * TILE, TILE)
+            token = lax.broadcasted_iota(jnp.int32, (TILE, 128), 0) + n * TILE
+            same = jnp.logical_and(token >= bounds[0:1, :], token < bounds[1:2, :])
+            dead = jnp.where(token < bounds[2:3, :], 0.0, -1e30)
+            gq[at, :] = jnp.where(lanes == 127, 1.0, jnp.where(same, group_bias, 0.0)).astype(bf)
+            gk[at, :] = jnp.where(lanes == 127, dead, jnp.where(same, 1.0, 0.0)).astype(bf)
+        kx[:, 128:] = gk[...]
+        keep(gq, gq_o)
+        keep(gk, gk_o)
+
+    def x_spread():
+        x_arrived()
+        for d in x_fw:
+            d.start()
 
     def norm_rows(n, _):
         at = pl.ds(pl.multiple_of(n * 64, 64), 64)
@@ -700,47 +708,29 @@
         normed[at, :] = (center * r * vec[0:1, :] + vec[1:2, :]).astype(bf)
         return _
 
-    def norm_half(h):
+    def norm_own():
         steps = seq // 2 // 64
-        lax.fori_loop(h * steps, (h + 1) * steps, norm_rows, 0)
-
-    norm_half(c)
-    for d in x_fw:
-        d.wait_recv()
-    norm_half(1 - c)
-    keep(normed, normed_o)
-    keep(xf, x_o)
-    gq_in.wait()
-    gk_in.wait()
-    kx[:, 128:] = gk[...]
-    land(1, 0)
-    land(1, 1)
-    turn(0, 2)
-    land(1, 2)
-    land(2, 0)
-    for slot in range(3):
-        turn(1, slot)
-    whole(0)
-    keep(wa, wa_o)
-
-    bias_row = jnp.concatenate(
-        [vec[2:3, cols_of(c * half, half)], jnp.zeros((1, half), f32), vec[3:4, cols_of(c * half, half)]], axis=1
-    )
-
-    def qkv_cols(start, width):
-        got = nn(normed[...], wa[:, pl.ds(start, width)])
-        qkv[:, pl.ds(start, width)] = (got + bias_row[:, start : start + width]).astype(bf)
-
-    total_cols = 3 * half
-    for n in range(total_cols // TILE):
-        qkv_cols(n * TILE, TILE)
-        if n == 3:
-            land(2, 1)
-            first(3)
-    if total_cols % TILE:
-        qkv_cols(total_cols // TILE * TILE, total_cols % TILE)
-    turn(2, 0)
-    keep(qkv, qkv_o)
+        lax.fori_loop(c * steps, (c + 1) * steps, norm_rows, 0)
+
+    def norm_other():
+        steps = seq // 2 // 64
+        for d in x_fw:
+            d.wait_recv()
+        lax.fori_loop((1 - c) * steps, (2 - c) * steps, norm_rows, 0)
+        keep(normed, normed_o)
+        keep(xf, x_o)
+
+    def project(start, stop):
+        bias_row = jnp.concatenate(
+            [vec[2:3, cols_of(c * half, half)], jnp.zeros((1, half), f32), vec[3:4, cols_of(c * half, half)]], axis=1
+        )
+        for at in range(start, stop, TILE):
+            width = min(TILE, stop - at)
+            got = nn(normed[...], wa[:, pl.ds(at, width)])
+            qkv[:, pl.ds(at, width)] = (got + bias_row[:, at : at + width]).astype(bf)
+        if stop == 3 * half:
+            keep(qkv, qkv_o)
+            keep(wa, wa_o)
 
     lane = lax.broadcasted_iota(jnp.int32, (TILE, 128), 1)
 
@@ -767,12 +757,10 @@
             return _
 
         lax.fori_loop(0, seq // TILE, chunk, 0)
-
-    attend(0)
-    land(2, 2)
-    turn(2, 1)
-    attend(1)
-    whole(1)
+        if t == half // 128 - 1:
+            keep(mixed, mixed_o)
+            keep(lse, lse_o)
+
     wo_own = pltpu.make_async_copy(
         wol.at[rows_of(c * half, half), :], wob.at[:, cols_of(c * half, half)], loc.at[5]
     )
@@ -780,37 +768,34 @@
         wol.at[rows_of((1 - c) * half, half), :],
         wob.at[:, cols_of(c * half, half)], wo_s.at[0], wo_r.at[0], (core_nb, z),
     )
-    wo_own.start()
-    wo_out.start()
-    attend(2)
-    land(3, 0)
-    turn(2, 2)
-    attend(3)
-    land(3, 1)
-    attend(4)
-    turn(3, 0)
-    keep(mixed, mixed_o)
-    keep(lse, lse_o)
-    wo_own.wait()
-    wo_out.wait()
-    keep(wob, wob_o)
+
+    def wo_swap():
+        wo_own.start()
+        wo_out.start()
+
+    def wo_ready():
+        wo_own.wait()
+        wo_out.wait()
+        keep(wob, wob_o)
 
     chunks = seq // TILE
-    swaps = []
-    for n in range(chunks):
+    swaps = [
+        send(part.at[pl.ds(n * TILE, TILE), :], part_in.at[pl.ds(n * TILE, TILE), :], pa_s.at[n], pa_r.at[n], (core_nb, z))
+        for n in range(chunks)
+    ]
+
+    def output_rows(n):
         at = pl.ds(n * TILE, TILE)
         part[at, :] = nn(mixed[at, :], wob[...]).astype(bf)
-        d = send(part.at[at, :], part_in.at[at, :], pa_s.at[n], pa_r.at[n], (core_nb, z))
-        d.start()
-        swaps.append(d)
-    land(3, 2)
-    c_start()
-    own_wait(3)
-    out_own = pltpu.make_async_copy(
-        second.at[pl.ds(0, hid // 2), :], wc.at[rows_of(z * (hid // 2), hid // 2), :], loc.at[4]
-    )
-    out_own.start()
-    out_own.wait()
+        swaps[n].start()
+
+    def own_outer():
+        own_wait(3)
+        out_own = pltpu.make_async_copy(
+            second.at[pl.ds(0, hid // 2), :], wc.at[rows_of(z * (hid // 2), hid // 2), :], loc.at[4]
+        )
+        out_own.start()
+        out_own.wait()
 
     def second_rows(n, _):
         at = pl.ds(pl.multiple_of(n * 64, 64), 64)
@@ -820,14 +805,12 @@
         second[at, :] = (center * r * vec[5:6, :] + vec[6:7, :]).astype(bf)
         return _
 
-    for n in range(chunks):
+    def second_norm(n):
         swaps[n].wait_recv()
         lax.fori_loop(n * TILE // 64, (n + 1) * TILE // 64, second_rows, 0)
-    keep(middle, middle_o)
-    keep(second, second_o)
-    turn(3, 1)
-    whole(2)
-    keep(wb, wb_o)
+        if n == chunks - 1:
+            keep(middle, middle_o)
+            keep(second, second_o)
 
     tiles = 2 * hid // TILE
 
@@ -838,14 +821,14 @@
             pltpu.make_async_copy(slp.at[slot], slope_o.at[:, cols], act_s.at[slot, 1]),
         ]
 
-    for n in range(tiles):
+    def inner_tile(n):
         slot = n % 2
         cols = pl.ds(n * TILE, TILE)
         if n >= 2:
             for d in tile_out(n - 2, slot):
                 d.wait()
 
-        def tile_rows(m, _, cols=cols, slot=slot):
+        def tile_rows(m, _):
             at = pl.ds(pl.multiple_of(m * TILE, TILE), TILE)
             u = nn(second[at, :], wb[:, cols]) + bias_in[:, cols]
             value, slope = gelu_and_slope(u)
@@ -856,15 +839,89 @@
         lax.fori_loop(0, chunks, tile_rows, 0)
         for d in tile_out(n, slot):
             d.start()
-        if n == 3:
-            turn(3, 2)
-    c_arrived()
-    for d in c_fw:
-        d.start()
+        if n == tiles - 1:
+            keep(wb, wb_o)
+
+    def c_spread():
+        c_arrived()
+        for d in c_fw:
+            d.start()
+
+    begin()
+    first(0)
+    for g in groups:
+        own_start(g)
+    first(1)
+    land(1, 1)
+    land(1, 0)
+    land(0, 0)
+    land(0, 1)
+    x_start()
+    land(1, 2)
+    turn(0, 0)
+    land(0, 2)
+    first(2)
+    turn(0, 1)
+    vectors()
+    turn(1, 1)
+    x_spread()
+    first(3)
+    turn(0, 2)
+    turn(1, 2)
+    turn(1, 0)
+    norm_own()
+    norm_other()
+    land(2, 0)
+    whole(0)
+    project(0, 512)
+    project(512, 1024)
+    project(1024, 1536)
+    project(1536, 3 * half)
+    land(3, 0)
+    land(2, 1)
+    attend(0)
+    whole(1)
+    turn(2, 0)
+    attend(1)
+    land(2, 2)
+    attend(2)
+    turn(2, 1)
+    land(3, 2)
+    attend(3)
+    wo_swap()
+    attend(4)
+    turn(2, 2)
+    land(3, 1)
+    wo_ready()
+    c_start()
+    output_rows(0)
+    output_rows(1)
+    output_rows(2)
+    output_rows(3)
+    turn(3, 0)
+    turn(3, 2)
+    own_outer()
+    second_norm(0)
+    second_norm(1)
+    whole(2)
+    second_norm(2)
+    second_norm(3)
+    inner_tile(0)
+    inner_tile(1)
+    inner_tile(2)
+    inner_tile(3)
+    inner_tile(4)
+    turn(3, 1)
+    inner_tile(5)
+    inner_tile(6)
+    inner_tile(7)
+    c_spread()
+    inner_tile(8)
+    inner_tile(9)
+    whole(3)
     for n in (tiles - 2, tiles - 1):
         for d in tile_out(n, n % 2):
             d.wait()
-    whole(3)
     for d in c_fw:
         d.wait()
     keep(cf, ct_o)
@@ -878,7 +935,7 @@
         d.wait()
 
 
-def run_forward(small, x, ct, wq, wk, wv, wo, w1, w2, gq, gk):
+def run_forward(small, bounds, x, ct, wq, wk, wv, wo, w1, w2):
     rows, feat = wq.shape
     hid = w2.shape[0]
     seq = x.shape[1] * LINE
@@ -888,12 +945,13 @@
     dma = pltpu.SemaphoreType.DMA
     anywhere = pl.BlockSpec(memory_space=pl.ANY)
     made = [
+        ((seq, 128), bf), ((seq, 128), bf),
         ((small.shape[0], feat), f32), ((seq, feat), bf), ((seq, feat), bf), ((feat, 3 * half), bf), ((half, feat), bf),
         ((feat, 2 * hid), bf), ((2 * hid, feat), bf), ((seq, feat), bf), ((seq, 3 * half), bf), ((seq, half), bf),
         ((16, seq), f32), ((seq, feat), bf), ((seq, feat), bf), ((seq, 2 * hid), bf), ((seq, 2 * hid), bf),
     ]
     held = [
-        ((LINE,) + small.shape, bf), ((small.shape[0], feat), f32), ((1, 2 * hid), f32), ((seq, feat), bf), ((seq, feat), bf),
+        ((LINE,) + small.shape, bf), (bounds.shape, jnp.int32), ((small.shape[0], feat), f32), ((1, 2 * hid), f32), ((seq, feat), bf), ((seq, feat), bf),
         ((feat, 3 * half), bf), ((feat, half), bf), ((half, feat), bf), ((feat, 2 * hid), bf), ((seq, feat), bf),
         ((seq, 3 * half), bf), ((seq, 128), bf), ((seq, 128), bf), ((seq, 256), bf), ((seq, half), bf),
         ((16, seq), f32), ((seq, feat), bf), ((seq, feat), bf), ((seq, feat), bf), ((seq, feat), bf),
@@ -902,19 +960,19 @@
     return pl.pallas_call(
         forward_kernel,
         out_shape=tuple(jax.ShapeDtypeStruct(shape, dtype) for shape, dtype in made),
-        in_specs=[anywhere] * 11,
+        in_specs=[anywhere] * 10,
         out_specs=(anywhere,) * len(made),
         scratch_shapes=[pltpu.VMEM(shape, dtype) for shape, dtype in held]
         + [
             dma((3,)), dma((3,)), dma((4,)), dma((4,)), dma((4,)), dma((4,)),
-            dma((4, 5)), dma((12, 4)), dma((12, 5)), dma((8,)), dma((1,)), dma((1,)),
+            dma((4, 5)), dma((12, 4)), dma((12, 5)), dma((7,)), dma((2,)), dma((2,)),
             dma((4,)), dma((4,)), dma((16,)), dma((2, 2)),
         ],
         compiler_params=pltpu.CompilerParams(
             collective_id=0, has_side_effects=True, vmem_limit_bytes=VMEM_LIMIT
         ),
         name="forward",
-    )(small, x, ct, wq, wk, wv, wo, w1, w2, gq, gk)
+    )(small, bounds, x, ct, wq, wk, wv, wo, w1, w2)
 
 
 def tn(left, right):
@@ -961,10 +1019,13 @@
         for d in copies:
             d.start()
 
+    here = set()
+
     def loaded(*names):
         for name in names:
-            for d in loads[name]:
+            for d in loads[name] if name not in here else ():
                 d.wait()
+            here.add(name)
 
     load("ct", [(ct_ref, up)])
     load("marks", [(gk_ref, gk), (gq_ref, gq), (vec_ref, vec), (lse_ref, lse)])
@@ -1168,97 +1229,111 @@
     block_start, block_sent, block_arrived = going_home(home, block_o, 0)
     input_start, input_sent, input_arrived = going_home(home, input_o, 1)
 
-    sums[0] = jnp.zeros(sums.shape[1:], f32)
-    loaded("ct", "marks")
-
-    def mask_rows(n, total):
-        at = pl.ds(pl.multiple_of(n * TILE, TILE), TILE)
-        gone = gk[at, 127:128].astype(f32) < 0.0
-        value = jnp.where(gone, 0.0, up[at, :].astype(f32))
-        up[at, :] = value.astype(bf)
-        return total + jnp.sum(value, axis=0, keepdims=True)
-
-    up_sum = lax.fori_loop(0, chunks, mask_rows, jnp.zeros((1, feat), f32))
     first_core = jnp.where(c == 0, 1.0, 0.0)
-    sums[0, 7:8, :] = up_sum * first_core
-    loaded("active")
-    pl.semaphore_wait(barrier, len(line_ids) + 2)
+    zero_row = jnp.zeros((1, feat), f32)
     wide = hid // 2
-    for s in (0, 2, 1, 3):
+
+    def mask():
+        sums[0] = jnp.zeros(sums.shape[1:], f32)
+        loaded("ct", "marks")
+
+        def mask_rows(n, total):
+            at = pl.ds(pl.multiple_of(n * TILE, TILE), TILE)
+            gone = gk[at, 127:128].astype(f32) < 0.0
+            value = jnp.where(gone, 0.0, up[at, :].astype(f32))
+            up[at, :] = value.astype(bf)
+            return total + jnp.sum(value, axis=0, keepdims=True)
+
+        up_sum = lax.fori_loop(0, chunks, mask_rows, zero_row)
+        sums[0, 7:8, :] = up_sum * first_core
+        loaded("active")
+
+    def outer_rows(s):
         dc[s * wide : (s + 1) * wide, :] = tn(big[:, s * wide : (s + 1) * wide], up[...]).astype(bf)
         unit_c.step1(s)
 
-    loaded("wc", "mid half")
-    swaps = []
-    for n in range(half_seq // TILE):
-        at = rows_of((1 - c) * half_seq + n * TILE, TILE)
-        to = pl.ds(n * TILE, TILE)
-        got = nn(big[at, :], wts[...]).astype(bf)
-        for m in range(2):
-            held = pl.ds(m * half_seq + n * TILE, TILE)
-            do[held, :] = got[:, m * half : (m + 1) * half]
-            send(
-                do.at[held, :], half_in.at[to, pl.ds(m * half, half)], cs.at[n], cr.at[n], (core_nb, z)
-            ).start()
-        swaps.append(send(half_in.at[to, :], half_in.at[to, :], cs.at[n], cr.at[n], (core_nb, z)))
-    for n in range(half_seq // TILE):
-        at = rows_of(c * half_seq + n * TILE, TILE)
-        to = pl.ds(n * TILE, TILE)
-        acc[...] = nn(big[at, :], wts[...])
-        swaps[n].wait_recv()
-        gone = gk[at, 127:128].astype(f32) < 0.0
-        value = home[to, :].astype(f32) + acc[...] + half_in[to, :].astype(f32) + vec[7:8, :]
-        home[to, :] = jnp.where(gone, 0.0, value).astype(bf)
-    block_start()
-
-    loaded("slope")
-
-    def inner_tile(n, _):
-        cols = pl.ds(pl.multiple_of(n * TILE, TILE), TILE)
-        got = (nt(up[...], wts[cols, :]) * db[pl.ds(0, seq), cols].astype(f32)).astype(bf)
-        big[:, cols] = got
-        bias_row[:, cols] = jnp.sum(got.astype(f32), axis=0, keepdims=True)
-        return _
-
-    lax.fori_loop(0, 2 * hid // TILE, inner_tile, 0)
-    for s in range(LINE):
-        sums[0, 8 + s : 9 + s, cols_of(c * wide, wide)] = bias_row[:, s * wide : (s + 1) * wide]
-    load("wb", [(wb_ref.at[:, pl.ds(n * hid, hid)], wts.at[pl.ds(n * feat, feat), :]) for n in range(2)])
-    loaded("second")
-    for n in range(2):
-
-        def inner_rows(m, _, n=n):
+    swaps = [
+        send(half_in.at[pl.ds(n * TILE, TILE), :], half_in.at[pl.ds(n * TILE, TILE), :], cs.at[n], cr.at[n], (core_nb, z))
+        for n in range(half_seq // TILE)
+    ]
+
+    def block_other():
+        loaded("wc", "mid half")
+        for n in range(half_seq // TILE):
+            at = rows_of((1 - c) * half_seq + n * TILE, TILE)
+            to = pl.ds(n * TILE, TILE)
+            got = nn(big[at, :], wts[...]).astype(bf)
+            for m in range(2):
+                held = pl.ds(m * half_seq + n * TILE, TILE)
+                do[held, :] = got[:, m * half : (m + 1) * half]
+                send(
+                    do.at[held, :], half_in.at[to, pl.ds(m * half, half)], cs.at[n], cr.at[n], (core_nb, z)
+                ).start()
+
+    def block_own():
+        for n in range(half_seq // TILE):
+            at = rows_of(c * half_seq + n * TILE, TILE)
+            to = pl.ds(n * TILE, TILE)
+            acc[...] = nn(big[at, :], wts[...])
+            swaps[n].wait_recv()
+            gone = gk[at, 127:128].astype(f32) < 0.0
+            value = home[to, :].astype(f32) + acc[...] + half_in[to, :].astype(f32) + vec[7:8, :]
+            home[to, :] = jnp.where(gone, 0.0, value).astype(bf)
+
+    def through_gelu():
+        loaded("wc", "slope")
+
+        def tile(n, _):
+            cols = pl.ds(pl.multiple_of(n * TILE, TILE), TILE)
+            got = (nt(up[...], wts[cols, :]) * db[pl.ds(0, seq), cols].astype(f32)).astype(bf)
+            big[:, cols] = got
+            bias_row[:, cols] = jnp.sum(got.astype(f32), axis=0, keepdims=True)
+            return _
+
+        lax.fori_loop(0, 2 * hid // TILE, tile, 0)
+        for s in range(LINE):
+            sums[0, 8 + s : 9 + s, cols_of(c * wide, wide)] = bias_row[:, s * wide : (s + 1) * wide]
+        load("wb", [(wb_ref.at[:, pl.ds(n * hid, hid)], wts.at[pl.ds(n * feat, feat), :]) for n in range(2)])
+        loaded("second")
+
+    def inner_grad(n):
+        def inner_rows(m, _):
             at = pl.ds(pl.multiple_of(m * TILE, TILE), TILE)
             db[at, pl.ds(n * hid, hid)] = tn(two[:, at], big[:, pl.ds(n * hid, hid)]).astype(bf)
             return _
 
         lax.fori_loop(0, feat // TILE, inner_rows, 0)
-        unit_b[n].step1_all()
-
-    loaded("wb")
-    for d in swaps:
-        d.wait_send()
-    gs_swaps = []
-    for n in range(chunks):
+
+    gs_swaps = [
+        send(two.at[pl.ds(n * TILE, TILE), :], three.at[pl.ds(n * TILE, TILE), :], cs.at[2 + n], cr.at[2 + n], (core_nb, z))
+        for n in range(chunks)
+    ]
+
+    def to_second(n):
+        if n == 0:
+            loaded("wb")
+            for d in swaps:
+                d.wait_send()
         at = pl.ds(n * TILE, TILE)
-        two[at, :] = (nt(big[at, pl.ds(0, hid)], wts[pl.ds(0, feat), :]) + nt(big[at, pl.ds(hid, hid)], wts[pl.ds(feat, feat), :])).astype(bf)
-        d = send(two.at[at, :], three.at[at, :], cs.at[2 + n], cr.at[2 + n], (core_nb, z))
-        d.start()
-        gs_swaps.append(d)
-    load("qkv", [(qkv_ref, big.at[:, pl.ds(0, 3 * half)]), (mixed_ref, big.at[:, pl.ds(3 * half, half)])])
-    load(
-        "wa",
-        [
-            (wa_ref.at[:, pl.ds(0, feat)], wts.at[pl.ds(0, feat), :]),
-            (wa_ref.at[:, pl.ds(feat, half)], wts.at[pl.ds(feat, feat), pl.ds(0, half)]),
-            (wob_ref.at[:, pl.ds(0, half)], wts.at[pl.ds(feat, half), pl.ds(half, half)]),
-            (wob_ref.at[:, pl.ds(half, half)], wts.at[pl.ds(feat + half, half), pl.ds(half, half)]),
-        ],
-    )
-    unit_c.step2()
-    unit_c.step1_sent()
-    load("middle", [(middle_ref, dc.at[pl.ds(0, seq), :])])
-    loaded("middle")
+        two[at, :] = (
+            nt(big[at, pl.ds(0, hid)], wts[pl.ds(0, feat), :]) + nt(big[at, pl.ds(hid, hid)], wts[pl.ds(feat, feat), :])
+        ).astype(bf)
+        gs_swaps[n].start()
+        if n == chunks - 1:
+            load("qkv", [(qkv_ref, big.at[:, pl.ds(0, 3 * half)]), (mixed_ref, big.at[:, pl.ds(3 * half, half)])])
+            load(
+                "wa",
+                [
+                    (wa_ref.at[:, pl.ds(0, feat)], wts.at[pl.ds(0, feat), :]),
+                    (wa_ref.at[:, pl.ds(feat, half)], wts.at[pl.ds(feat, feat), pl.ds(0, half)]),
+                    (wob_ref.at[:, pl.ds(0, half)], wts.at[pl.ds(feat, half), pl.ds(half, half)]),
+                    (wob_ref.at[:, pl.ds(half, half)], wts.at[pl.ds(feat + half, half), pl.ds(half, half)]),
+                ],
+            )
+
+    def middle_load():
+        unit_c.step1_sent()
+        load("middle", [(middle_ref, dc.at[pl.ds(0, seq), :])])
 
     def back_rows(n, carry):
         gain_sum, shift_sum, out_sum = carry
@@ -1278,32 +1353,34 @@
             out_sum + jnp.sum(got.astype(f32), axis=0, keepdims=True),
         )
 
-    zero_row = jnp.zeros((1, feat), f32)
-    carry = (zero_row, zero_row, zero_row)
-    for n in range(chunks):
-        gs_swaps[n].wait()
-        carry = lax.fori_loop(n * TILE // 64, (n + 1) * TILE // 64, back_rows, carry)
-    sums[0, 5:6, :] = carry[0] * first_core
-    sums[0, 6:7, :] = carry[1] * first_core
-    sums[0, 4:5, :] = carry[2] * first_core
-    load("normed", [(normed_ref, three)])
-    load("x", [(x_ref.at[rows_of(c * half_seq, half_seq), :], up.at[pl.ds(0, half_seq), :])])
-
-    loaded("qkv", "wa")
-    stage[...] = tn(big[:, pl.ds(3 * half, half)], two[:, cols_of((1 - c) * half, half)]).astype(bf)
+    def second_back():
+        loaded("middle")
+        carry = (zero_row, zero_row, zero_row)
+        for n in range(chunks):
+            gs_swaps[n].wait()
+            carry = lax.fori_loop(n * TILE // 64, (n + 1) * TILE // 64, back_rows, carry)
+        sums[0, 5:6, :] = carry[0] * first_core
+        sums[0, 6:7, :] = carry[1] * first_core
+        sums[0, 4:5, :] = carry[2] * first_core
+        load("normed", [(normed_ref, three)])
+        load("x", [(x_ref.at[rows_of(c * half_seq, half_seq), :], up.at[pl.ds(0, half_seq), :])])
+
     o_swap = send(stage, do.at[rows_of(c * half, half), :], cs.at[6], cr.at[6], (core_nb, z))
-    o_swap.start()
-    do[rows_of(c * half, half), :] = tn(big[:, pl.ds(3 * half, half)], two[:, cols_of(c * half, half)]).astype(bf)
-    o_swap.wait_recv()
-    unit_o.step1_all()
-    grad_mixed = (pl.ds(seq, seq), half)
-    for n in range(chunks):
-        at = pl.ds(n * TILE, TILE)
-        dc[pl.ds(seq + n * TILE, TILE), pl.ds(half, half)] = (
-            nt(two[at, pl.ds(0, half)], wts[pl.ds(feat, half), pl.ds(half, half)])
-            + nt(two[at, pl.ds(half, half)], wts[pl.ds(feat + half, half), pl.ds(half, half)])
-        ).astype(bf)
-    kx[:, 128:] = gk[...]
+
+    def output_grad():
+        loaded("qkv", "wa")
+        stage[...] = tn(big[:, pl.ds(3 * half, half)], two[:, cols_of((1 - c) * half, half)]).astype(bf)
+        o_swap.start()
+        do[rows_of(c * half, half), :] = tn(big[:, pl.ds(3 * half, half)], two[:, cols_of(c * half, half)]).astype(bf)
+
+    def mixed_grad():
+        for n in range(chunks):
+            at = pl.ds(n * TILE, TILE)
+            dc[pl.ds(seq + n * TILE, TILE), pl.ds(half, half)] = (
+                nt(two[at, pl.ds(0, half)], wts[pl.ds(feat, half), pl.ds(half, half)])
+                + nt(two[at, pl.ds(half, half)], wts[pl.ds(feat + half, half), pl.ds(half, half)])
+            ).astype(bf)
+        kx[:, 128:] = gk[...]
 
     lane = lax.broadcasted_iota(jnp.int32, (TILE, 128), 1)
     root = HEAD_DIM ** (-0.5)
@@ -1339,47 +1416,42 @@
         lax.fori_loop(0, chunks, chunk, 0)
         dc[pl.ds(0, seq), pl.ds(half + t * 128, 128)] = dkv[0].astype(bf)
         dc[pl.ds(seq, seq), pl.ds(t * 128, 128)] = dkv[1].astype(bf)
-
-    attend_back(0)
-    unit_b[0].step2()
-    attend_back(1)
-    unit_c.line()
-    unit_c.step2_sent()
-    pl.semaphore_signal(free_x, inc=1, device_id=(x_nb, z), device_id_type=mesh_id)
-    pl.semaphore_signal(free_y, inc=1, device_id=(y_nb, z), device_id_type=mesh_id)
-    attend_back(2)
-    unit_b[1].step2()
-    unit_o.step2()
-    attend_back(3)
-    unit_b[0].line()
-    attend_back(4)
-    unit_b[1].line()
-    unit_o.line()
-    sums[0, 2:3, cols_of(c * half, half)] = jnp.sum(dc[pl.ds(0, seq), pl.ds(0, half)].astype(f32), axis=0, keepdims=True)
-    sums[0, 3:4, cols_of(c * half, half)] = jnp.sum(dc[pl.ds(seq, seq), pl.ds(0, half)].astype(f32), axis=0, keepdims=True)
-
-    loaded("normed")
-    for u in unit_b:
-        u.step1_sent()
-
-    def qk_rows(m, _):
-        at = pl.ds(pl.multiple_of(m * TILE, TILE), TILE)
-        db[at, pl.ds(0, feat)] = tn(three[:, at], dc[pl.ds(0, seq), :]).astype(bf)
-        return _
-
-    def v_rows(m, _):
-        at = pl.ds(pl.multiple_of(m * TILE, TILE), TILE)
-        db[at, pl.ds(feat, half)] = tn(three[:, at], dc[pl.ds(seq, seq), pl.ds(0, half)]).astype(bf)
-        return _
-
-    lax.fori_loop(0, feat // TILE, qk_rows, 0)
-    pl.semaphore_wait(free_x, 1)
-    pl.semaphore_wait(free_y, 1)
-    unit_a[0].step1_all()
-    unit_a[1].step1_all()
-    lax.fori_loop(0, feat // TILE, v_rows, 0)
-    unit_a[2].step1_all()
-    unit_c.spread()
+        if t == half // 128 - 1:
+            sums[0, 2:3, cols_of(c * half, half)] = jnp.sum(
+                dc[pl.ds(0, seq), pl.ds(0, half)].astype(f32), axis=0, keepdims=True
+            )
+            sums[0, 3:4, cols_of(c * half, half)] = jnp.sum(
+                dc[pl.ds(seq, seq), pl.ds(0, half)].astype(f32), axis=0, keepdims=True
+            )
+
+    def free_landing():
+        unit_c.step2_sent()
+        pl.semaphore_signal(free_x, inc=1, device_id=(x_nb, z), device_id_type=mesh_id)
+        pl.semaphore_signal(free_y, inc=1, device_id=(y_nb, z), device_id_type=mesh_id)
+
+    def landing_free():
+        pl.semaphore_wait(free_x, 1)
+        pl.semaphore_wait(free_y, 1)
+
+    def query_key_grad():
+        loaded("normed")
+        for u in unit_b:
+            u.step1_sent()
+
+        def qk_rows(m, _):
+            at = pl.ds(pl.multiple_of(m * TILE, TILE), TILE)
+            db[at, pl.ds(0, feat)] = tn(three[:, at], dc[pl.ds(0, seq), :]).astype(bf)
+            return _
+
+        lax.fori_loop(0, feat // TILE, qk_rows, 0)
+
+    def value_grad():
+        def v_rows(m, _):
+            at = pl.ds(pl.multiple_of(m * TILE, TILE), TILE)
+            db[at, pl.ds(feat, half)] = tn(three[:, at], dc[pl.ds(seq, seq), pl.ds(0, half)]).astype(bf)
+            return _
+
+        lax.fori_loop(0, feat // TILE, v_rows, 0)
 
     def first_part(at):
         at_v = rows_of(at + seq, TILE)
@@ -1387,22 +1459,29 @@
             dc[at_v, pl.ds(0, half)], wts[pl.ds(feat, feat), pl.ds(0, half)]
         )
 
-    loaded("x")
-    gn_swaps = []
-    for n in range(half_seq // TILE):
-        to = pl.ds(half_seq + n * TILE, TILE)
-        up[to, :] = first_part((1 - c) * half_seq + n * TILE).astype(bf)
-        d = send(up.at[to, :], half_in.at[pl.ds(n * TILE, TILE), :], cs.at[7 + n], cr.at[7 + n], (core_nb, z))
-        d.start()
-        gn_swaps.append(d)
-    unit_c.cross()
-    block_sent()
-    carry = (zero_row, zero_row)
-    for n in range(half_seq // TILE):
+    gn_swaps = [
+        send(
+            up.at[pl.ds(half_seq + n * TILE, TILE), :], half_in.at[pl.ds(n * TILE, TILE), :], cs.at[7 + n], cr.at[7 + n],
+            (core_nb, z),
+        )
+        for n in range(half_seq // TILE)
+    ]
+
+    def to_first(n):
+        if n == 0:
+            loaded("x")
+        up[pl.ds(half_seq + n * TILE, TILE), :] = first_part((1 - c) * half_seq + n * TILE).astype(bf)
+        gn_swaps[n].start()
+
+    first_sums = [zero_row, zero_row]
+
+    def first_back(n):
+        if n == 0:
+            block_sent()
         acc[...] = first_part(c * half_seq + n * TILE)
         gn_swaps[n].wait_recv()
 
-        def first_rows(m, carry, n=n):
+        def first_rows(m, carry):
             gain_sum, shift_sum = carry
             at = pl.ds(pl.multiple_of(m * 64, 64), 64)
             here = pl.ds(pl.multiple_of(n * TILE + m * 64, 64), 64)
@@ -1420,60 +1499,114 @@
                 shift_sum + jnp.sum(g, axis=0, keepdims=True),
             )
 
-        carry = lax.fori_loop(0, TILE // 64, first_rows, carry)
-    sums[0, 0:1, :] = carry[0]
-    sums[0, 1:2, :] = carry[1]
+        first_sums[:] = lax.fori_loop(0, TILE // 64, first_rows, tuple(first_sums))
+        if n == half_seq // TILE - 1:
+            sums[0, 0:1, :] = first_sums[0]
+            sums[0, 1:2, :] = first_sums[1]
+
+    small_who = [(core_nb, z), (x_nb, z), (y_nb, z)]
+    small = [send(sums.at[n], sums_in.at[n], ss.at[n], sr.at[n], small_who[n]) for n in range(3)] + [
+        send(sums.at[3], sums_in.at[3 + d], ss.at[3 + d], sr.at[3 + d], (i, lax.rem(z + d + 1, LINE)))
+        for d in range(LINE - 1)
+    ]
+    small_out = pltpu.make_async_copy(sums.at[4], small_o, os.at[7])
+
+    def small_step(n):
+        if n > 0:
+            small[n - 1].wait_recv()
+            sums[n] = sums[n - 1] + sums_in[n - 1]
+        for d in small[3:] if n == 3 else small[n : n + 1]:
+            d.start()
+
+    def small_end():
+        for d in range(LINE - 1):
+            small[3 + d].wait_recv()
+        sums[4] = sums[3] + ((sums_in[3] + sums_in[4]) + sums_in[5])
+        small_out.start()
+
+    (unit_b0, unit_b1), (unit_q, unit_k, unit_v) = unit_b, unit_a
+
+    pl.semaphore_wait(barrier, len(line_ids) + 2)
+    mask()
+    outer_rows(0)
+    outer_rows(2)
+    block_other()
+    outer_rows(1)
+    outer_rows(3)
+    block_own()
+    through_gelu()
+    block_start()
+    inner_grad(0)
+    inner_grad(1)
+    to_second(0)
+    unit_c.step2()
+    middle_load()
+    to_second(1)
+    to_second(2)
+    to_second(3)
+    unit_b0.step1_all()
+    second_back()
+    unit_b1.step1_all()
+    output_grad()
+    mixed_grad()
+    unit_c.line()
+    free_landing()
+    attend_back(0)
+    attend_back(1)
+    unit_b0.step2()
+    attend_back(2)
+    attend_back(3)
+    unit_b1.step2()
+    attend_back(4)
+    unit_b0.line()
+    to_first(0)
+    o_swap.wait_recv()
+    to_first(1)
+    unit_o.step1_all()
+    query_key_grad()
+    unit_b1.line()
+    value_grad()
+    landing_free()
+    unit_v.step1_all()
+    unit_o.step2()
+    unit_v.step2()
+    unit_o.line()
+    unit_q.step1_all()
+    unit_k.step1_all()
+    unit_q.step2()
+    unit_v.line()
+    unit_k.step2()
+    unit_o.spread()
+    unit_q.line()
+    unit_b1.spread()
+    unit_k.line()
+    first_back(0)
+    unit_b0.spread()
+    first_back(1)
+    small_step(0)
+    unit_v.spread()
+    unit_q.spread()
+    unit_c.spread()
+    small_step(1)
+    unit_b1.cross()
     input_start()
-
-    def small_step(n, who):
-        d = send(sums.at[n], sums_in.at[n], ss.at[n], sr.at[n], who)
-        d.start()
-        return d
-
-    small = [small_step(0, (core_nb, z))]
-    unit_b[0].spread()
+    unit_b0.cross()
+    unit_k.spread()
+    small_step(2)
+    unit_o.cross()
+    unit_c.cross()
+    unit_q.cross()
+    small_step(3)
+    unit_v.cross()
+    unit_k.cross()
+    unit_v.to_core()
+    small_end()
+    unit_q.to_core()
+    unit_b1.to_core()
+    unit_k.to_core()
     unit_c.to_core()
-    small[0].wait_recv()
-    sums[1] = sums[0] + sums_in[0]
-    small.append(small_step(1, (x_nb, z)))
-    unit_b[1].spread()
-    unit_a[0].step2()
-    unit_b[0].cross()
-    small[1].wait_recv()
-    sums[2] = sums[1] + sums_in[1]
-    small.append(small_step(2, (y_nb, z)))
-    unit_a[1].step2()
-    unit_b[1].cross()
-    unit_o.spread()
-    small[2].wait_recv()
-    sums[3] = sums[2] + sums_in[2]
-    for d in range(LINE - 1):
-        small.append(
-            send(sums.at[3], sums_in.at[3 + d], ss.at[3 + d], sr.at[3 + d], (i, lax.rem(z + d + 1, LINE)))
-        )
-        small[-1].start()
-    unit_a[2].step2()
-    unit_b[0].to_core()
-    unit_a[0].line()
-    unit_b[1].to_core()
-    unit_o.cross()
-    unit_a[1].line()
-    for d in range(LINE - 1):
-        small[3 + d].wait_recv()
-    sums[4] = sums[3] + ((sums_in[3] + sums_in[4]) + sums_in[5])
-    small_out = pltpu.make_async_copy(sums.at[4], small_o, os.at[7])
-    small_out.start()
-    unit_a[2].line()
+    unit_b0.to_core()
     unit_o.to_core()
-    unit_a[0].spread()
-    unit_a[1].spread()
-    unit_a[0].cross()
-    unit_a[2].spread()
-    unit_a[1].cross()
-    unit_a[0].to_core()
-    unit_a[2].cross()
-    unit_a[1].to_core()
-    unit_a[2].to_core()
     small_out.wait()
     for d in small + gn_swaps + [o_swap]:
         d.wait_send()
@@ -1529,63 +1662,107 @@
     )(vec, x, ct, wa, wob, wb, wc, normed, qkv, mixed, lse, middle, second, active, slope, gq, gk)
 
 
-def flip(value, step):
-    count = lax.axis_size("cells")
-    return lax.ppermute(value, "cells", [(n, n ^ step) for n in range(count)])
-
-
-def take(value, index, axis):
-    return lax.dynamic_index_in_dim(value, index, axis, keepdims=False)
+def finish_kernel(
+    block_ref, input_ref, w2_ref, w1_ref, q_ref, k_ref, v_ref, o_ref, small_ref,
+    block_o, input_o, gain_o, shift_o, q_o, bq_o, k_o, v_o, bv_o, o_o, bo_o, gain_two_o, shift_two_o, w1_o, b1_o, w2_o, b2_o,
+    held, wide, blocks, sums, ins, outs,
+):
+    z = lax.axis_index("chrom")
+    rows, feat = q_ref.shape
+    tiles = [(ref, to, pl.ds(0, rows), pl.ds(0, feat)) for ref, to in ((q_ref, q_o), (k_ref, k_o), (v_ref, v_o), (o_ref, o_o))]
+    tiles += [(w1_ref, w1_o, pl.ds(0, rows), pl.ds(n * feat, feat)) for n in range(w1_ref.shape[1] // feat)]
+    tiles += [(w2_ref, w2_o, pl.ds(n * rows, rows), pl.ds(0, feat)) for n in range(w2_ref.shape[0] // rows)]
+    small_in = pltpu.make_async_copy(small_ref, sums, ins.at[len(tiles)])
+    small_in.start()
+    loads = [pltpu.make_async_copy(ref.at[at, cols], held.at[n], ins.at[n]) for n, (ref, _, at, cols) in enumerate(tiles)]
+    loads += [
+        pltpu.make_async_copy(ref, blocks.at[n], ins.at[len(tiles) + 1 + n]) for n, ref in enumerate((block_ref, input_ref))
+    ]
+    for d in loads:
+        d.start()
+    small_in.wait()
+    spots = (gain_o, shift_o, bq_o, bv_o, bo_o, gain_two_o, shift_two_o, b2_o)
+    for n, to in enumerate(spots):
+        value = sums[n : n + 1, 0:rows]
+        for s in range(1, LINE):
+            value = jnp.where(z == s, sums[n : n + 1, s * rows : (s + 1) * rows], value)
+        to[...] = value[0, :]
+    value = sums[VECTORS : VECTORS + 1, :]
+    for s in range(1, LINE):
+        value = jnp.where(z == s, sums[VECTORS + s : VECTORS + s + 1, :], value)
+    b1_o[...] = value[0, :]
+    stores = []
+    for n, (_, to, at, cols) in enumerate(tiles):
+        loads[n].wait()
+        wide[n] = held[n].astype(jnp.float32)
+        stores.append(pltpu.make_async_copy(wide.at[n], to.at[at, cols], outs.at[n]))
+        stores[-1].start()
+    for n, to in enumerate((block_o, input_o)):
+        loads[len(tiles) + n].wait()
+        stores.append(pltpu.make_async_copy(blocks.at[n], to, outs.at[len(tiles) + n]))
+        stores[-1].start()
+    for d in stores:
+        d.wait()
+
+
+def finish(block_out, input_grad, w2, w1, q, k, v, o, sums):
+    f32 = jnp.float32
+    rows, feat = q.shape
+    hid = w2.shape[0]
+    tiles = 4 + w1.shape[1] // feat + hid // rows
+    anywhere, here = pl.BlockSpec(memory_space=pl.ANY), pl.BlockSpec(memory_space=pltpu.VMEM)
+    matrix, vector = jax.ShapeDtypeStruct((rows, feat), f32), jax.ShapeDtypeStruct((rows,), f32)
+    block = jax.ShapeDtypeStruct(block_out.shape, block_out.dtype)
+    made = (
+        block, block, vector, vector, matrix, vector, matrix, matrix, vector, matrix, vector, vector, vector,
+        jax.ShapeDtypeStruct(w1.shape, f32), jax.ShapeDtypeStruct((hid,), f32), jax.ShapeDtypeStruct(w2.shape, f32), vector,
+    )
+    return pl.pallas_call(
+        finish_kernel,
+        out_shape=made,
+        in_specs=[anywhere] * 9,
+        out_specs=tuple(here if len(m.shape) == 1 else anywhere for m in made),
+        scratch_shapes=[
+            pltpu.VMEM((tiles, rows, feat), q.dtype), pltpu.VMEM((tiles, rows, feat), f32),
+            pltpu.VMEM((2,) + block_out.shape, block_out.dtype), pltpu.VMEM(sums.shape, f32),
+            pltpu.SemaphoreType.DMA((tiles + 3,)), pltpu.SemaphoreType.DMA((tiles + 2,)),
+        ],
+        compiler_params=pltpu.CompilerParams(vmem_limit_bytes=VMEM_LIMIT),
+        name="finish",
+    )(block_out, input_grad, w2, w1, q, k, v, o, sums)
 
 
 def paired_local(
     inputs, lengths, offsets, cotangent, norm_gain, norm_shift, query_proj, query_bias, key_proj, value_proj,
     value_bias, output_proj, output_bias, second_gain, second_shift, inner_proj, inner_bias, outer_proj, outer_bias,
 ):
-    f32, bf = jnp.float32, jnp.bfloat16
-    i, z = lax.axis_index("cells"), lax.axis_index("chrom")
-    p, c = i // 2, i % 2
-    px, py = p % 2, p // 2
-    cells_here, block, feat = inputs.shape
-    seq = block * LINE
-    half_seq, half = seq // 2, feat // 2
+    cells_here, _, feat = inputs.shape
     rows = feat // LINE
     hid = outer_proj.shape[0]
-    inv_root = HEAD_DIM ** (-0.5)
-    heads = HEADS // 2
 
     vectors = (norm_gain, norm_shift, query_bias, value_bias, output_bias, second_gain, second_shift, outer_bias)
-    small = jnp.concatenate([v.reshape(1, rows) for v in vectors] + [inner_bias.reshape(hid // rows, rows)], axis=0)
-    small = jnp.pad(small, ((0, 16 - small.shape[0]), (0, 384 - rows)))
-    ragged = jnp.concatenate([lengths[:, None], offsets], axis=1)
-    other = flip(ragged, 1)
-    ragged = take(jnp.where(z // 2 == c, ragged, other), z % 2, 0)
-    length, starts = ragged[0], ragged[1:]
-    places = jnp.arange(seq, dtype=jnp.int32)
-    live = places < length
-    groups = jnp.sum((places[:, None] >= starts[None, :]).astype(jnp.int32), axis=1)
-    lanes = jnp.arange(128, dtype=jnp.int32)[None, :]
-    same = (groups[:, None] == lanes).astype(bf)
-    mark_q = jnp.where(lanes == 127, jnp.ones((), bf), same * jnp.array(group_bias, bf))
-    mark_k = jnp.where(lanes == 127, jnp.where(live, 0.0, -1e30).astype(bf)[:, None], same)
+    entries = vectors + tuple(inner_bias[n * rows : (n + 1) * rows] for n in range(hid // rows))
+    row = lax.broadcasted_iota(jnp.int32, (16, rows), 0)
+    small = jnp.zeros((16, rows), entries[0].dtype)
+    for n, entry in enumerate(entries):
+        small = jnp.where(row == n, entry[None, :], small)
+    small = jnp.pad(small, ((0, 0), (0, 384 - rows)))
+    lanes, count = 128, offsets.shape[1]
+    first = jnp.pad(offsets, ((0, 0), (1, lanes - 1 - count)), constant_values=2 ** 30)
+    end = jnp.pad(offsets, ((0, 0), (0, lanes - count)), constant_values=2 ** 30)
+    group = lax.broadcasted_iota(jnp.int32, (cells_here, 8, lanes), 2)
+    kind = lax.broadcasted_iota(jnp.int32, (cells_here, 8, lanes), 1)
+    first = jnp.where(group == 0, 0, first[:, None, :])
+    bounds = jnp.where(kind == 0, first, jnp.where(kind == 1, end[:, None, :], lengths[:, None, None]))
     (
-        vec, xf, cf, wa, wob, wb, wc, normed, qkv, mixed, lse, middle, second, active, slope,
+        mark_q, mark_k, vec, xf, cf, wa, wob, wb, wc, normed, qkv, mixed, lse, middle, second, active, slope,
     ) = run_forward(
-        small, inputs, cotangent, query_proj, key_proj, value_proj, output_proj, inner_proj, outer_proj, mark_q, mark_k
-    )
-    block_out, input_grad, w2_grad, w1_grad, q_grad, k_grad, v_grad, o_grad, sums = run_backward(
+        small, bounds, inputs, cotangent, query_proj, key_proj, value_proj, output_proj, inner_proj, outer_proj
+    )
+    grads = run_backward(
         vec, xf, cf, wa, wob, wb, wc, normed, qkv, mixed, lse, middle, second, active, slope, mark_q, mark_k
     )
-
-    def shard(n):
-        return lax.dynamic_slice_in_dim(sums[n], z * rows, rows, 0)
-
-    inner_bias_grad = take(sums[8:12], z, 0)
-    return (
-        block_out, input_grad, shard(0), shard(1), q_grad.astype(f32), shard(2), k_grad.astype(f32),
-        v_grad.astype(f32), shard(3), o_grad.astype(f32), shard(4), shard(5), shard(6), w1_grad.astype(f32),
-        inner_bias_grad, w2_grad.astype(f32), shard(7),
-    )
+    return finish(*grads)
 
 
 def solution(mesh):

time: 471 us -> 417 us (0.89)
  Pallas kernels: 434 us -> 403 us
  other arithmetic: 15.8 us -> 2.26 us
  local copies, waits for them, and re-layouts: 15.7 us -> 2.34 us
    pallas_call x1, Pallas kernels: 253 us -> 228 us  [run_backward(): pl.pallas_call(backward_kernel, out_shape=tuple((jax.ShapeDtypeStruct(sha...]
    pallas_call x1, Pallas kernels: 181 us -> 163 us  [run_forward(): pl.pallas_call(forward_kernel, out_shape=tuple((jax.ShapeDtypeStruct(shap...]
    convert_element_type x7 -> x0, other arithmetic: 13.1 us -> none  [the longest x1 3.57 us: paired_local(): w1_grad.astype(f32)]
    pallas_call x0 -> x1, Pallas kernels: none -> 12.2 us  [finish(): pl.pallas_call(finish_kernel, out_shape=made, in_specs=[anywhere] * 9, ou...]
    reshape x9 -> x0, local copies, waits for them, and re-layouts: 6.22 us -> none  [the longest x8 5.45 us: paired_local(): v.reshape(1, rows)]
  transfers between devices with their start and end apart: 1 -> 0, of which waited for: 0 -> 0; matrix products, arithmetic and copies ran while one was open for 1% -> 0% of each run, Pallas kernels for 0% -> 0%
where the time goes in v4:
time: 417 us; the launch traced here: 409 us
  Pallas kernels  403 us (97%)
    pallas_call x1, Pallas kernels, run_backward(): pl.pallas_call(backward_kernel, out_shape=tuple((jax.ShapeDtypeStruct(sha...  228 us
    pallas_call x1, Pallas kernels, run_forward(): pl.pallas_call(forward_kernel, out_shape=tuple((jax.ShapeDtypeStruct(shap...  163 us
    pallas_call x1, Pallas kernels, finish(): pl.pallas_call(finish_kernel, out_shape=made, in_specs=[anywhere] * 9, ou...  12.2 us

profile of v4, /device:TPU:0, one launch (start us, length us, event | category | flops | bytes accessed | tf_op | source)
XLA Modules:
  0.0 408.9 jit_solution(9934257397395987641)
XLA Ops:
  0.8 0.8 fusion.1
  1.6 0.9 fusion
  2.5 0.9 select_select_fusion
  3.4 0.6 pad.12.small_ref
  4.0 1.3 select_select_fusion.1.rag_ref
  5.3 162.8 %forward.1 = (bf16[1024,128]{1,0:T(8,128)(2,1)}, bf16[1024,128]{1,0:T(8,128)(2,1)}, f32[16,1280]{1,0:T(8,128)}, bf16[1024,1280]{1,0:T(8,128)(2,1)}, bf16[1024,12...) custom-call(bf16[16,384]{1,0:T(8,128)(2,1)} %pad.12.small_ref, ...), custom_call_target="tpu_custom_call" | custom-call | tf_op jit(solution)/shard_map/forward/pallas_call | solution.py:960
  168.1 228.4 %backward.1 = (bf16[2,256,1280]{2,1,0:T(8,128)(2,1)}, bf16[2,256,1280]{2,1,0:T(8,128)(2,1)}, bf16[1280,1280]{1,0:T(8,128)(2,1)}, bf16[320,5120]{1,0:T(8,128)(2,1...) custom-call(f32[16,1280]{1,0:T(8,128)} %get-tuple-element.43.vec_ref, ...), custom_call_target="tpu_custom_call" | custom-call | tf_op jit(solution)/shard_map/backward/pallas_call | solution.py:1648
  396.5 12.2 %finish.1 = (bf16[2,256,1280]{2,1,0:T(8,128)(2,1)}, bf16[2,256,1280]{2,1,0:T(8,128)(2,1)}, f32[320]{0:T(512)}, f32[320]{0:T(512)}, f32[320,1280]{1,0:T(8,128)}, ...) custom-call(bf16[2,256,1280]{2,1,0:T(8,128)(2,1)} %get-tuple-element, ...), custom_call_target="tpu_custom_call" | custom-call | tf_op jit(solution)/shard_map/finish/pallas_call | solution.py:1720
  (8 shorter events, 0.0 us)

commit v5 on v4

--- a/solution.py
+++ b/solution.py
@@ -440,12 +440,17 @@
     return u * phi_sum, phi_sum + u * gauss * 0.3989422804014327
 
 
-def forward_kernel(
-    small_ref, rag_ref, x_ref, ct_ref, wq_ref, wk_ref, wv_ref, wo_ref, w1_ref, w2_ref,
-    gq_o, gk_o, vec_o, x_o, ct_o, wa_o, wob_o, wb_o, wc, normed_o, qkv_o, mixed_o, lse_o, middle_o, second_o, active_o, slope_o,
-    smalls, rag, vec, bias_in, xf, cf, wa, wol, wob, wb, normed, qkv, gq, gk, kx, mixed, lse, part, part_in, middle, second,
-    act, slp,
-    sm_s, sm_r, ex_s, ex_r, fw_s, fw_r, ln_s, un_s, un_r, loc, wo_s, wo_r, pa_s, pa_r, out_s, act_s,
+def tn(left, right):
+    return lax.dot_general(left, right, (((0,), (0,)), ((), ())), preferred_element_type=jnp.float32)
+
+
+def layer_kernel(
+    len_ref, off_ref, v0, v1, v2, v3, v4, v5, v6, v7, b_ref, x_ref, ct_ref, wq_ref, wk_ref, wv_ref, wo_ref, w1_ref, w2_ref,
+    block_o, input_o, w2_o, w1_o, q_o, k_o, v_o, o_o, small_o, x_o, normed_o, qkv_o, wa_o, wob_o,
+    small_ref, rag_ref, smalls, rag, vec, bias_in, xf, up, dc, do, wb, wts, big, db, two, three, r1c, r2c, zc, r1o, r2a, za, kx, gq, gk, lse,
+    half_in, home, acc, sums, sums_in,
+    sm_s, sm_r, ex_s, ex_r, fw_s, fw_r, ln_s, un_s, un_r, loc, wo_s, wo_r, pa_s, pa_r, out_s,
+    ld, us, ur, hs, hr, cs, cr, ss, sr, os, free_x, free_y, freed_x, freed_y, freed_z,
 ):
     f32, bf = jnp.float32, jnp.bfloat16
     i, z = lax.axis_index("cells"), lax.axis_index("chrom")
@@ -459,7 +464,26 @@
     hid = w2_ref.shape[0]
     block = x_ref.shape[1]
     seq = block * LINE
+    half_seq = seq // 2
+    chunks = seq // TILE
+    wide = hid // 2
+    mesh_id = pl.DeviceIdType.MESH
     part_rows, hid_part = rows // PLANE, hid // 2 // PLANE
+
+    small_ref[...] = jnp.zeros(small_ref.shape, bf)
+    for n, ref in enumerate((v0, v1, v2, v3, v4, v5, v6, v7)):
+        small_ref[n : n + 1, 0:rows] = ref[...][None, :]
+    for n in range(hid // rows):
+        small_ref[VECTORS + n : VECTORS + n + 1, 0:rows] = b_ref[n * rows : (n + 1) * rows][None, :]
+    count = off_ref.shape[1]
+    never = 2 ** 30
+    for n in range(rag_ref.shape[0]):
+        rag_ref[n] = jnp.full(rag_ref.shape[1:], never, jnp.int32)
+        rag_ref[n, 1:2, 0:count] = off_ref[n : n + 1, :]
+        end = rag_ref[n, 1:2, :]
+        group = lax.broadcasted_iota(jnp.int32, end.shape, 1)
+        rag_ref[n, 0:1, :] = jnp.where(group == 0, 0, pltpu.roll(end, 1, 1))
+        rag_ref[n, 2:3, :] = jnp.full(end.shape, len_ref[n], jnp.int32)
 
     barrier = pltpu.get_barrier_semaphore()
     line_ids = [
@@ -525,10 +549,11 @@
         ]
 
     x_start, x_arrived, x_sent = exchange(x_ref, xf, 0)
-    c_start, c_arrived, c_sent = exchange(ct_ref, cf, 1)
-    x_fw, c_fw = forward(xf, 0), forward(cf, 1)
-
-    lands = (wa, wol, wb, wc)
+    c_start, c_arrived, c_sent = exchange(ct_ref, up, 1)
+    x_fw, c_fw = forward(xf, 0), forward(up, 1)
+
+    wa, wol = dc.at[:, pl.ds(0, 3 * half)], dc.at[:, pl.ds(3 * half, half)]
+    lands = (wa, wol, wb, wts)
     groups = range(4)
     partner, inner = z + 1 - 2 * lax.rem(z, 2), 3 - z
     low = z < 2
@@ -616,20 +641,18 @@
     def own_start(g):
         shard, _ = shape_of(g)
         for src, cols in own_parts(g, 0, shard):
-            to = second.at[pl.ds(0, shard), :] if g == 3 else lands[g].at[rows_of(z * shard, shard), cols]
-            pltpu.make_async_copy(src, to, loc.at[1 + g]).start()
+            pltpu.make_async_copy(src, lands[g].at[rows_of(z * shard, shard), cols], loc.at[1 + g]).start()
 
     def own_wait(g):
         shard, _ = shape_of(g)
-        ref = second.at[pl.ds(0, shard), :] if g == 3 else lands[g].at[rows_of(z * shard, shard), :]
+        ref = lands[g].at[rows_of(z * shard, shard), :]
         pltpu.make_async_copy(ref, ref, loc.at[1 + g]).wait()
 
     def whole(g):
         for slot in range(3):
             for d in cross(g, slot):
                 d.wait_recv()
-        if g < 3:
-            own_wait(g)
+        own_wait(g)
 
     def all_sent(g):
         line_send(g, z, 0, 0, partner).wait_send()
@@ -644,12 +667,11 @@
             for d in spread(g, slot) + cross(g, slot):
                 d.wait_send()
 
-    outs = []
-
-    def keep(src, dst):
-        d = pltpu.make_async_copy(src, dst, out_s.at[len(outs)])
-        d.start()
-        outs.append(d)
+    kept = {}
+
+    def keep(name, src, dst):
+        kept[name] = pltpu.make_async_copy(src, dst, out_s.at[len(kept)])
+        kept[name].start()
 
     def begin():
         small_own.start()
@@ -680,8 +702,6 @@
                 picked = jnp.where(which == VECTORS + c * (hid // 2 // rows) + n, nn(smalls[s], place), 0.0)
                 line_bias += jnp.sum(picked, axis=0, keepdims=True)
             bias_in[:, pl.ds(s * (hid // 2), hid // 2)] = line_bias
-        keep(vec, vec_o)
-
         rag_own.wait()
         rag_out.wait()
         bounds = jnp.where(c == z // 2, rag[0], rag[1])
@@ -694,8 +714,6 @@
             gq[at, :] = jnp.where(lanes == 127, 1.0, jnp.where(same, group_bias, 0.0)).astype(bf)
             gk[at, :] = jnp.where(lanes == 127, dead, jnp.where(same, 1.0, 0.0)).astype(bf)
         kx[:, 128:] = gk[...]
-        keep(gq, gq_o)
-        keep(gk, gk_o)
 
     def x_spread():
         x_arrived()
@@ -705,7 +723,7 @@
     def norm_rows(n, _):
         at = pl.ds(pl.multiple_of(n * 64, 64), 64)
         center, r = moments(xf[at, :].astype(f32))
-        normed[at, :] = (center * r * vec[0:1, :] + vec[1:2, :]).astype(bf)
+        db[at, pl.ds(0, feat)] = (center * r * vec[0:1, :] + vec[1:2, :]).astype(bf)
         return _
 
     def norm_own():
@@ -717,8 +735,8 @@
         for d in x_fw:
             d.wait_recv()
         lax.fori_loop((1 - c) * steps, (2 - c) * steps, norm_rows, 0)
-        keep(normed, normed_o)
-        keep(xf, x_o)
+        keep("normed", db.at[pl.ds(0, seq), pl.ds(0, feat)], normed_o)
+        keep("x", xf.at[rows_of(c * half_seq, half_seq), :], x_o)
 
     def project(start, stop):
         bias_row = jnp.concatenate(
@@ -726,22 +744,21 @@
         )
         for at in range(start, stop, TILE):
             width = min(TILE, stop - at)
-            got = nn(normed[...], wa[:, pl.ds(at, width)])
-            qkv[:, pl.ds(at, width)] = (got + bias_row[:, at : at + width]).astype(bf)
+            got = nn(db[pl.ds(0, seq), pl.ds(0, feat)], dc[:, pl.ds(at, width)])
+            big[:, pl.ds(at, width)] = (got + bias_row[:, at : at + width]).astype(bf)
         if stop == 3 * half:
-            keep(qkv, qkv_o)
-            keep(wa, wa_o)
+            keep("wa", wa, wa_o)
 
     lane = lax.broadcasted_iota(jnp.int32, (TILE, 128), 1)
 
     def attend(t):
-        k2 = qkv[:, pl.ds(half + t * 128, 128)]
-        v2t = jnp.transpose(qkv[:, pl.ds(2 * half + t * 128, 128)])
+        k2 = big[:, pl.ds(half + t * 128, 128)]
+        v2t = jnp.transpose(big[:, pl.ds(2 * half + t * 128, 128)])
         kx[:, :128] = k2
 
         def chunk(n, _):
             at = pl.ds(pl.multiple_of(n * TILE, TILE), TILE)
-            q2 = qkv[at, pl.ds(t * 128, 128)] * jnp.array(HEAD_DIM ** (-0.5), bf)
+            q2 = big[at, pl.ds(t * 128, 128)] * jnp.array(HEAD_DIM ** (-0.5), bf)
             both = []
             for h in range(2):
                 own = lane < HEAD_DIM if h == 0 else lane >= HEAD_DIM
@@ -753,20 +770,19 @@
                 o = nn(v2t[h * HEAD_DIM : (h + 1) * HEAD_DIM, :], e.astype(bf))
                 both.append(o / total)
                 lse[2 * t + h : 2 * t + h + 1, at] = top + jnp.log(total)
-            mixed[at, pl.ds(t * 128, 128)] = jnp.transpose(jnp.concatenate(both, axis=0)).astype(bf)
+            big[at, pl.ds(3 * half + t * 128, 128)] = jnp.transpose(jnp.concatenate(both, axis=0)).astype(bf)
             return _
 
         lax.fori_loop(0, seq // TILE, chunk, 0)
         if t == half // 128 - 1:
-            keep(mixed, mixed_o)
-            keep(lse, lse_o)
+            keep("qkv", big, qkv_o)
 
     wo_own = pltpu.make_async_copy(
-        wol.at[rows_of(c * half, half), :], wob.at[:, cols_of(c * half, half)], loc.at[5]
+        wol.at[rows_of(c * half, half), :], do.at[rows_of(c * half, half), :], loc.at[5]
     )
     wo_out = send(
         wol.at[rows_of((1 - c) * half, half), :],
-        wob.at[:, cols_of(c * half, half)], wo_s.at[0], wo_r.at[0], (core_nb, z),
+        do.at[rows_of(c * half, half), :], wo_s.at[0], wo_r.at[0], (core_nb, z),
     )
 
     def wo_swap():
@@ -776,239 +792,62 @@
     def wo_ready():
         wo_own.wait()
         wo_out.wait()
-        keep(wob, wob_o)
-
-    chunks = seq // TILE
-    swaps = [
-        send(part.at[pl.ds(n * TILE, TILE), :], part_in.at[pl.ds(n * TILE, TILE), :], pa_s.at[n], pa_r.at[n], (core_nb, z))
+        keep("wob", do, wob_o)
+
+    part = db.at[pl.ds(0, seq), pl.ds(feat, feat)]
+    part_swaps = [
+        send(part.at[pl.ds(n * TILE, TILE), :], three.at[pl.ds(n * TILE, TILE), :], pa_s.at[n], pa_r.at[n], (core_nb, z))
         for n in range(chunks)
     ]
 
     def output_rows(n):
         at = pl.ds(n * TILE, TILE)
-        part[at, :] = nn(mixed[at, :], wob[...]).astype(bf)
-        swaps[n].start()
-
-    def own_outer():
-        own_wait(3)
-        out_own = pltpu.make_async_copy(
-            second.at[pl.ds(0, hid // 2), :], wc.at[rows_of(z * (hid // 2), hid // 2), :], loc.at[4]
-        )
-        out_own.start()
-        out_own.wait()
+        for m in range(2):
+            db[at, pl.ds(feat + m * half, half)] = nn(
+                big[at, pl.ds(3 * half, half)], do[pl.ds(m * half, half), :]
+            ).astype(bf)
+        part_swaps[n].start()
 
     def second_rows(n, _):
         at = pl.ds(pl.multiple_of(n * 64, 64), 64)
-        sums = xf[at, :].astype(f32) + (part[at, :].astype(f32) + part_in[at, :].astype(f32) + vec[4:5, :])
-        middle[at, :] = sums.astype(bf)
-        center, r = moments(sums)
-        second[at, :] = (center * r * vec[5:6, :] + vec[6:7, :]).astype(bf)
+        total = xf[at, :].astype(f32) + (
+            db[at, pl.ds(feat, feat)].astype(f32) + three[at, :].astype(f32) + vec[4:5, :]
+        )
+        xf[at, :] = total.astype(bf)
+        center, r = moments(total)
+        two[at, :] = (center * r * vec[5:6, :] + vec[6:7, :]).astype(bf)
         return _
 
     def second_norm(n):
-        swaps[n].wait_recv()
+        if n == 0:
+            kept["x"].wait()
+            for d in x_fw:
+                d.wait_send()
+        part_swaps[n].wait()
         lax.fori_loop(n * TILE // 64, (n + 1) * TILE // 64, second_rows, 0)
-        if n == chunks - 1:
-            keep(middle, middle_o)
-            keep(second, second_o)
 
     tiles = 2 * hid // TILE
 
-    def tile_out(n, slot):
+    def inner_tile(n):
+        if n == 0:
+            for name in ("qkv", "normed"):
+                kept[name].wait()
         cols = pl.ds(n * TILE, TILE)
-        return [
-            pltpu.make_async_copy(act.at[slot], active_o.at[:, cols], act_s.at[slot, 0]),
-            pltpu.make_async_copy(slp.at[slot], slope_o.at[:, cols], act_s.at[slot, 1]),
-        ]
-
-    def inner_tile(n):
-        slot = n % 2
-        cols = pl.ds(n * TILE, TILE)
-        if n >= 2:
-            for d in tile_out(n - 2, slot):
-                d.wait()
 
         def tile_rows(m, _):
             at = pl.ds(pl.multiple_of(m * TILE, TILE), TILE)
-            u = nn(second[at, :], wb[:, cols]) + bias_in[:, cols]
+            u = nn(two[at, :], wb[:, cols]) + bias_in[:, cols]
             value, slope = gelu_and_slope(u)
-            act[slot, at, :] = value.astype(bf)
-            slp[slot, at, :] = slope.astype(bf)
+            big[at, cols] = value.astype(bf)
+            db[at, cols] = slope.astype(bf)
             return _
 
         lax.fori_loop(0, chunks, tile_rows, 0)
-        for d in tile_out(n, slot):
-            d.start()
-        if n == tiles - 1:
-            keep(wb, wb_o)
 
     def c_spread():
         c_arrived()
         for d in c_fw:
             d.start()
-
-    begin()
-    first(0)
-    for g in groups:
-        own_start(g)
-    first(1)
-    land(1, 1)
-    land(1, 0)
-    land(0, 0)
-    land(0, 1)
-    x_start()
-    land(1, 2)
-    turn(0, 0)
-    land(0, 2)
-    first(2)
-    turn(0, 1)
-    vectors()
-    turn(1, 1)
-    x_spread()
-    first(3)
-    turn(0, 2)
-    turn(1, 2)
-    turn(1, 0)
-    norm_own()
-    norm_other()
-    land(2, 0)
-    whole(0)
-    project(0, 512)
-    project(512, 1024)
-    project(1024, 1536)
-    project(1536, 3 * half)
-    land(3, 0)
-    land(2, 1)
-    attend(0)
-    whole(1)
-    turn(2, 0)
-    attend(1)
-    land(2, 2)
-    attend(2)
-    turn(2, 1)
-    land(3, 2)
-    attend(3)
-    wo_swap()
-    attend(4)
-    turn(2, 2)
-    land(3, 1)
-    wo_ready()
-    c_start()
-    output_rows(0)
-    output_rows(1)
-    output_rows(2)
-    output_rows(3)
-    turn(3, 0)
-    turn(3, 2)
-    own_outer()
-    second_norm(0)
-    second_norm(1)
-    whole(2)
-    second_norm(2)
-    second_norm(3)
-    inner_tile(0)
-    inner_tile(1)
-    inner_tile(2)
-    inner_tile(3)
-    inner_tile(4)
-    turn(3, 1)
-    inner_tile(5)
-    inner_tile(6)
-    inner_tile(7)
-    c_spread()
-    inner_tile(8)
-    inner_tile(9)
-    whole(3)
-    for n in (tiles - 2, tiles - 1):
-        for d in tile_out(n, n % 2):
-            d.wait()
-    for d in c_fw:
-        d.wait()
-    keep(cf, ct_o)
-    for d in x_fw + swaps:
-        d.wait_send()
-    x_sent()
-    c_sent()
-    for g in groups:
-        all_sent(g)
-    for d in outs:
-        d.wait()
-
-
-def run_forward(small, bounds, x, ct, wq, wk, wv, wo, w1, w2):
-    rows, feat = wq.shape
-    hid = w2.shape[0]
-    seq = x.shape[1] * LINE
-    half = feat // 2
-    heads = half // HEAD_DIM
-    f32, bf = jnp.float32, jnp.bfloat16
-    dma = pltpu.SemaphoreType.DMA
-    anywhere = pl.BlockSpec(memory_space=pl.ANY)
-    made = [
-        ((seq, 128), bf), ((seq, 128), bf),
-        ((small.shape[0], feat), f32), ((seq, feat), bf), ((seq, feat), bf), ((feat, 3 * half), bf), ((half, feat), bf),
-        ((feat, 2 * hid), bf), ((2 * hid, feat), bf), ((seq, feat), bf), ((seq, 3 * half), bf), ((seq, half), bf),
-        ((16, seq), f32), ((seq, feat), bf), ((seq, feat), bf), ((seq, 2 * hid), bf), ((seq, 2 * hid), bf),
-    ]
-    held = [
-        ((LINE,) + small.shape, bf), (bounds.shape, jnp.int32), ((small.shape[0], feat), f32), ((1, 2 * hid), f32), ((seq, feat), bf), ((seq, feat), bf),
-        ((feat, 3 * half), bf), ((feat, half), bf), ((half, feat), bf), ((feat, 2 * hid), bf), ((seq, feat), bf),
-        ((seq, 3 * half), bf), ((seq, 128), bf), ((seq, 128), bf), ((seq, 256), bf), ((seq, half), bf),
-        ((16, seq), f32), ((seq, feat), bf), ((seq, feat), bf), ((seq, feat), bf), ((seq, feat), bf),
-        ((2, seq, TILE), bf), ((2, seq, TILE), bf),
-    ]
-    return pl.pallas_call(
-        forward_kernel,
-        out_shape=tuple(jax.ShapeDtypeStruct(shape, dtype) for shape, dtype in made),
-        in_specs=[anywhere] * 10,
-        out_specs=(anywhere,) * len(made),
-        scratch_shapes=[pltpu.VMEM(shape, dtype) for shape, dtype in held]
-        + [
-            dma((3,)), dma((3,)), dma((4,)), dma((4,)), dma((4,)), dma((4,)),
-            dma((4, 5)), dma((12, 4)), dma((12, 5)), dma((7,)), dma((2,)), dma((2,)),
-            dma((4,)), dma((4,)), dma((16,)), dma((2, 2)),
-        ],
-        compiler_params=pltpu.CompilerParams(
-            collective_id=0, has_side_effects=True, vmem_limit_bytes=VMEM_LIMIT
-        ),
-        name="forward",
-    )(small, bounds, x, ct, wq, wk, wv, wo, w1, w2)
-
-
-def tn(left, right):
-    return lax.dot_general(left, right, (((0,), (0,)), ((), ())), preferred_element_type=jnp.float32)
-
-
-def backward_kernel(
-    vec_ref, x_ref, ct_ref, wa_ref, wob_ref, wb_ref, wc_ref, normed_ref, qkv_ref, mixed_ref, lse_ref, middle_ref,
-    second_ref, active_ref, slope_ref, gq_ref, gk_ref,
-    block_o, input_o, w2_o, w1_o, q_o, k_o, v_o, o_o, small_o,
-    vec, up, big, two, three, wts, dc, db, do, r1c, r2c, zc, r1b, r2b, zb, r1o, r2a, za, kx, gq, gk, lse, half_in, home,
-    acc, stage, sums, sums_in, bias_row, dkv,
-    ld, us, ur, hs, hr, cs, cr, ss, sr, os, free_x, free_y,
-):
-    f32, bf = jnp.float32, jnp.bfloat16
-    i, z = lax.axis_index("cells"), lax.axis_index("chrom")
-    p, c = i // 2, lax.rem(i, 2)
-    px, py = lax.rem(p, 2), p // 2
-    x_nb, y_nb, core_nb = i + 2 - 4 * px, i + 4 - 8 * py, i + 1 - 2 * c
-    p_x, p_y = p + 1 - 2 * px, p + 2 - 4 * py
-    seq, feat = up.shape
-    half, half_seq, block = feat // 2, seq // 2, seq // LINE
-    rows = feat // LINE
-    hid = wc_ref.shape[0] // 2
-    chunks = seq // TILE
-    mesh_id = pl.DeviceIdType.MESH
-
-    barrier = pltpu.get_barrier_semaphore()
-    line_ids = [
-        (i - c + lax.rem(c + dc_, 2), lax.rem(z + dz, LINE))
-        for dc_ in range(2)
-        for dz in range(LINE)
-        if dc_ or dz
-    ]
-    for who in line_ids + [(x_nb, z), (y_nb, z)]:
-        pl.semaphore_signal(barrier, inc=1, device_id=who, device_id_type=mesh_id)
 
     loads = {}
 
@@ -1027,19 +866,6 @@
                 d.wait()
             here.add(name)
 
-    load("ct", [(ct_ref, up)])
-    load("marks", [(gk_ref, gk), (gq_ref, gq), (vec_ref, vec), (lse_ref, lse)])
-    load("active", [(active_ref, big)])
-    load("wc", [(wc_ref, wts)])
-    load("mid half", [(middle_ref.at[rows_of(c * half_seq, half_seq), :], home)])
-    load("slope", [(slope_ref, db.at[pl.ds(0, seq), :])])
-    load("second", [(second_ref, two)])
-
-    def send(src, dst, s, r, who):
-        return pltpu.make_async_remote_copy(
-            src_ref=src, dst_ref=dst, send_sem=s, recv_sem=r, device_id=who, device_id_type=mesh_id
-        )
-
     class Unit:
         def __init__(self, n, d, col, r, w, r1, r2, zl, parts):
             self.n, self.d, self.col, self.r, self.w = n, d, col, r, w
@@ -1050,6 +876,8 @@
             return ref.at[rows_of(row0 + row * self.r, count * self.r), pl.ds(col0, self.w)]
 
         def own(self, s, a, b):
+            if self.col is None:
+                return self.region((self.d, 0, s // 2 * self.w), (s % 2 * 2 + a) * 2 + b)
             return self.region((self.d, 0, self.col), (s * 2 + a) * 2 + b)
 
         def r1(self, side, m, n):
@@ -1181,10 +1009,10 @@
         return place
 
     r_big, r_small = hid // 2 // PLANE, rows // PLANE
-    unit_c = Unit(0, dc, 0, r_big, feat, (r1c, 0, 0), (r2c, 0, 0), (zc, 0, 0), [(0, feat, place_w2)])
+    unit_c = Unit(0, dc, None, r_big, feat, (r1c, 0, 0), (r2c, 0, 0), (zc, 0, 0), [(0, feat, place_w2)])
     unit_b = [
         Unit(
-            1 + n, db, n * hid, r_small, hid, (r1b, 0, n * hid), (r2b, 0, n * hid), (zb, 0, n * hid),
+            1 + n, db, n * hid, r_small, hid, (wb, 0, n * hid), (wb, 8 * r_small, n * hid), (wb, 12 * r_small, n * hid),
             [(m * (hid // 2), hid // 2, place_w1(2 * n + m)) for m in range(2)],
         )
         for n in range(2)
@@ -1231,11 +1059,11 @@
 
     first_core = jnp.where(c == 0, 1.0, 0.0)
     zero_row = jnp.zeros((1, feat), f32)
-    wide = hid // 2
 
     def mask():
         sums[0] = jnp.zeros(sums.shape[1:], f32)
-        loaded("ct", "marks")
+        for d in c_fw:
+            d.wait()
 
         def mask_rows(n, total):
             at = pl.ds(pl.multiple_of(n * TILE, TILE), TILE)
@@ -1246,10 +1074,12 @@
 
         up_sum = lax.fori_loop(0, chunks, mask_rows, zero_row)
         sums[0, 7:8, :] = up_sum * first_core
-        loaded("active")
+        kept["wa"].wait()
+        for g in (0, 1):
+            all_sent(g)
 
     def outer_rows(s):
-        dc[s * wide : (s + 1) * wide, :] = tn(big[:, s * wide : (s + 1) * wide], up[...]).astype(bf)
+        dc[s % 2 * wide : (s % 2 + 1) * wide, s // 2 * feat : (s // 2 + 1) * feat] = tn(big[:, s * wide : (s + 1) * wide], up[...]).astype(bf)
         unit_c.step1(s)
 
     swaps = [
@@ -1258,7 +1088,7 @@
     ]
 
     def block_other():
-        loaded("wc", "mid half")
+        kept["wob"].wait()
         for n in range(half_seq // TILE):
             at = rows_of((1 - c) * half_seq + n * TILE, TILE)
             to = pl.ds(n * TILE, TILE)
@@ -1277,24 +1107,20 @@
             acc[...] = nn(big[at, :], wts[...])
             swaps[n].wait_recv()
             gone = gk[at, 127:128].astype(f32) < 0.0
-            value = home[to, :].astype(f32) + acc[...] + half_in[to, :].astype(f32) + vec[7:8, :]
+            value = xf[at, :].astype(f32) + acc[...] + half_in[to, :].astype(f32) + vec[7:8, :]
             home[to, :] = jnp.where(gone, 0.0, value).astype(bf)
 
     def through_gelu():
-        loaded("wc", "slope")
-
         def tile(n, _):
             cols = pl.ds(pl.multiple_of(n * TILE, TILE), TILE)
             got = (nt(up[...], wts[cols, :]) * db[pl.ds(0, seq), cols].astype(f32)).astype(bf)
             big[:, cols] = got
-            bias_row[:, cols] = jnp.sum(got.astype(f32), axis=0, keepdims=True)
+            bias_in[:, cols] = jnp.sum(got.astype(f32), axis=0, keepdims=True)
             return _
 
         lax.fori_loop(0, 2 * hid // TILE, tile, 0)
         for s in range(LINE):
-            sums[0, 8 + s : 9 + s, cols_of(c * wide, wide)] = bias_row[:, s * wide : (s + 1) * wide]
-        load("wb", [(wb_ref.at[:, pl.ds(n * hid, hid)], wts.at[pl.ds(n * feat, feat), :]) for n in range(2)])
-        loaded("second")
+            sums[0, 8 + s : 9 + s, cols_of(c * wide, wide)] = bias_in[:, s * wide : (s + 1) * wide]
 
     def inner_grad(n):
         def inner_rows(m, _):
@@ -1305,48 +1131,58 @@
         lax.fori_loop(0, feat // TILE, inner_rows, 0)
 
     gs_swaps = [
-        send(two.at[pl.ds(n * TILE, TILE), :], three.at[pl.ds(n * TILE, TILE), :], cs.at[2 + n], cr.at[2 + n], (core_nb, z))
+        send(db.at[pl.ds(n * TILE, TILE), pl.ds(0, feat)], three.at[pl.ds(n * TILE, TILE), :], cs.at[2 + n], cr.at[2 + n], (core_nb, z))
         for n in range(chunks)
     ]
 
     def to_second(n):
         if n == 0:
-            loaded("wb")
             for d in swaps:
                 d.wait_send()
         at = pl.ds(n * TILE, TILE)
-        two[at, :] = (
-            nt(big[at, pl.ds(0, hid)], wts[pl.ds(0, feat), :]) + nt(big[at, pl.ds(hid, hid)], wts[pl.ds(feat, feat), :])
-        ).astype(bf)
+        db[at, pl.ds(0, feat)] = nt(big[at, :], wb[...]).astype(bf)
         gs_swaps[n].start()
         if n == chunks - 1:
-            load("qkv", [(qkv_ref, big.at[:, pl.ds(0, 3 * half)]), (mixed_ref, big.at[:, pl.ds(3 * half, half)])])
-            load(
-                "wa",
-                [
-                    (wa_ref.at[:, pl.ds(0, feat)], wts.at[pl.ds(0, feat), :]),
-                    (wa_ref.at[:, pl.ds(feat, half)], wts.at[pl.ds(feat, feat), pl.ds(0, half)]),
-                    (wob_ref.at[:, pl.ds(0, half)], wts.at[pl.ds(feat, half), pl.ds(half, half)]),
-                    (wob_ref.at[:, pl.ds(half, half)], wts.at[pl.ds(feat + half, half), pl.ds(half, half)]),
-                ],
-            )
-
-    def middle_load():
-        unit_c.step1_sent()
-        load("middle", [(middle_ref, dc.at[pl.ds(0, seq), :])])
+            all_sent(2)
+            pl.semaphore_signal(freed_x, inc=1, device_id=(x_nb, z), device_id_type=mesh_id)
+            pl.semaphore_signal(freed_y, inc=1, device_id=(y_nb, z), device_id_type=mesh_id)
+            for d in range(1, LINE):
+                pl.semaphore_signal(
+                    freed_z, inc=1, device_id=(i, lax.rem(z + d, LINE)), device_id_type=mesh_id
+                )
+
+    def inner_free():
+        pl.semaphore_wait(freed_x, 1)
+        pl.semaphore_wait(freed_y, 1)
+        pl.semaphore_wait(freed_z, LINE - 1)
+
+    def weights_load():
+        all_sent(3)
+        load(
+            "wa",
+            [
+                (wa_o.at[:, pl.ds(0, feat)], wts.at[pl.ds(0, feat), :]),
+                (wa_o.at[:, pl.ds(feat, half)], wts.at[pl.ds(feat, feat), pl.ds(0, half)]),
+                (wob_o, wts.at[pl.ds(feat, feat), pl.ds(half, half)]),
+            ],
+        )
+
+    def qkv_load():
+        load("qkv", [(qkv_o, big)])
+        load("normed", [(normed_o, two)])
 
     def back_rows(n, carry):
         gain_sum, shift_sum, out_sum = carry
         at = pl.ds(pl.multiple_of(n * 64, 64), 64)
-        g = two[at, :].astype(f32) + three[at, :].astype(f32)
-        center, r = moments(dc[at, :].astype(f32))
+        g = db[at, pl.ds(0, feat)].astype(f32) + three[at, :].astype(f32)
+        center, r = moments(xf[at, :].astype(f32))
         hat = center * r
         gh = g * hat
         h = g * vec[5:6, :]
         first = jnp.mean(h, axis=-1, keepdims=True)
         slant = jnp.mean(h * hat, axis=-1, keepdims=True)
         got = (up[at, :].astype(f32) + r * (h - first - hat * slant)).astype(bf)
-        two[at, :] = got
+        three[at, :] = got
         return (
             gain_sum + jnp.sum(gh, axis=0, keepdims=True),
             shift_sum + jnp.sum(g, axis=0, keepdims=True),
@@ -1354,7 +1190,6 @@
         )
 
     def second_back():
-        loaded("middle")
         carry = (zero_row, zero_row, zero_row)
         for n in range(chunks):
             gs_swaps[n].wait()
@@ -1362,40 +1197,41 @@
         sums[0, 5:6, :] = carry[0] * first_core
         sums[0, 6:7, :] = carry[1] * first_core
         sums[0, 4:5, :] = carry[2] * first_core
-        load("normed", [(normed_ref, three)])
-        load("x", [(x_ref.at[rows_of(c * half_seq, half_seq), :], up.at[pl.ds(0, half_seq), :])])
-
+        load("x", [(x_o, up.at[pl.ds(0, half_seq), :])])
+
+    stage = dc.at[pl.ds(0, half), pl.ds(0, half)]
     o_swap = send(stage, do.at[rows_of(c * half, half), :], cs.at[6], cr.at[6], (core_nb, z))
 
     def output_grad():
-        loaded("qkv", "wa")
-        stage[...] = tn(big[:, pl.ds(3 * half, half)], two[:, cols_of((1 - c) * half, half)]).astype(bf)
+        loaded("qkv")
+        unit_c.step1_sent()
+        dc[pl.ds(0, half), pl.ds(0, half)] = tn(
+            big[:, pl.ds(3 * half, half)], three[:, cols_of((1 - c) * half, half)]
+        ).astype(bf)
         o_swap.start()
-        do[rows_of(c * half, half), :] = tn(big[:, pl.ds(3 * half, half)], two[:, cols_of(c * half, half)]).astype(bf)
+        do[rows_of(c * half, half), :] = tn(big[:, pl.ds(3 * half, half)], three[:, cols_of(c * half, half)]).astype(bf)
 
     def mixed_grad():
+        loaded("wa")
         for n in range(chunks):
             at = pl.ds(n * TILE, TILE)
-            dc[pl.ds(seq + n * TILE, TILE), pl.ds(half, half)] = (
-                nt(two[at, pl.ds(0, half)], wts[pl.ds(feat, half), pl.ds(half, half)])
-                + nt(two[at, pl.ds(half, half)], wts[pl.ds(feat + half, half), pl.ds(half, half)])
+            dc[at, pl.ds(3 * half, half)] = (
+                nt(three[at, pl.ds(0, half)], wts[pl.ds(feat, half), pl.ds(half, half)])
+                + nt(three[at, pl.ds(half, half)], wts[pl.ds(feat + half, half), pl.ds(half, half)])
             ).astype(bf)
-        kx[:, 128:] = gk[...]
-
-    lane = lax.broadcasted_iota(jnp.int32, (TILE, 128), 1)
+
     root = HEAD_DIM ** (-0.5)
 
     def attend_back(t):
         k2 = big[:, pl.ds(half + t * 128, 128)]
         k2t = jnp.transpose(k2)
         kx[:, :128] = k2
-        dkv[...] = jnp.zeros(dkv.shape, f32)
+        acc[...] = jnp.zeros(acc.shape, f32)
 
         def chunk(n, _):
             at = pl.ds(pl.multiple_of(n * TILE, TILE), TILE)
-            g_at = pl.ds(pl.multiple_of(seq + n * TILE, TILE), TILE)
             q2 = big[at, pl.ds(t * 128, 128)] * jnp.array(root, bf)
-            g2 = dc[g_at, pl.ds(half + t * 128, 128)]
+            g2 = dc[at, pl.ds(3 * half + t * 128, 128)]
             both = []
             for h in range(2):
                 own = lane < HEAD_DIM if h == 0 else lane >= HEAD_DIM
@@ -1407,21 +1243,25 @@
                 both_of = prob * grad
                 dot = jnp.sum(both_of, axis=0, keepdims=True)
                 ds = (both_of - prob * dot).astype(bf)
-                dkv[0] += nn(ds, qm)
-                dkv[1] += nn(prob.astype(bf), gm)
+                for which, got in enumerate((nn(ds, qm), nn(prob.astype(bf), gm))):
+                    for m in range(chunks):
+                        acc[:, pl.ds((which * chunks + m) * 128, 128)] += got[m * TILE : (m + 1) * TILE]
                 both.append(nn(k2t[h * HEAD_DIM : (h + 1) * HEAD_DIM, :], ds))
             dc[at, pl.ds(t * 128, 128)] = (jnp.transpose(jnp.concatenate(both, axis=0)) * root).astype(bf)
             return _
 
         lax.fori_loop(0, chunks, chunk, 0)
-        dc[pl.ds(0, seq), pl.ds(half + t * 128, 128)] = dkv[0].astype(bf)
-        dc[pl.ds(seq, seq), pl.ds(t * 128, 128)] = dkv[1].astype(bf)
+        for which in range(2):
+            for m in range(chunks):
+                dc[pl.ds(m * TILE, TILE), pl.ds((1 + which) * half + t * 128, 128)] = acc[
+                    :, pl.ds((which * chunks + m) * 128, 128)
+                ].astype(bf)
         if t == half // 128 - 1:
             sums[0, 2:3, cols_of(c * half, half)] = jnp.sum(
                 dc[pl.ds(0, seq), pl.ds(0, half)].astype(f32), axis=0, keepdims=True
             )
             sums[0, 3:4, cols_of(c * half, half)] = jnp.sum(
-                dc[pl.ds(seq, seq), pl.ds(0, half)].astype(f32), axis=0, keepdims=True
+                dc[pl.ds(0, seq), pl.ds(2 * half, half)].astype(f32), axis=0, keepdims=True
             )
 
     def free_landing():
@@ -1440,7 +1280,7 @@
 
         def qk_rows(m, _):
             at = pl.ds(pl.multiple_of(m * TILE, TILE), TILE)
-            db[at, pl.ds(0, feat)] = tn(three[:, at], dc[pl.ds(0, seq), :]).astype(bf)
+            db[at, pl.ds(0, feat)] = tn(two[:, at], dc[pl.ds(0, seq), pl.ds(0, feat)]).astype(bf)
             return _
 
         lax.fori_loop(0, feat // TILE, qk_rows, 0)
@@ -1448,15 +1288,15 @@
     def value_grad():
         def v_rows(m, _):
             at = pl.ds(pl.multiple_of(m * TILE, TILE), TILE)
-            db[at, pl.ds(feat, half)] = tn(three[:, at], dc[pl.ds(seq, seq), pl.ds(0, half)]).astype(bf)
+            db[at, pl.ds(feat, half)] = tn(two[:, at], dc[pl.ds(0, seq), pl.ds(feat, half)]).astype(bf)
             return _
 
         lax.fori_loop(0, feat // TILE, v_rows, 0)
 
     def first_part(at):
-        at_v = rows_of(at + seq, TILE)
-        return nt(dc[rows_of(at, TILE), :], wts[pl.ds(0, feat), :]) + nt(
-            dc[at_v, pl.ds(0, half)], wts[pl.ds(feat, feat), pl.ds(0, half)]
+        at = rows_of(at, TILE)
+        return nt(dc[at, pl.ds(0, feat)], wts[pl.ds(0, feat), :]) + nt(
+            dc[at, pl.ds(feat, half)], wts[pl.ds(feat, feat), pl.ds(0, half)]
         )
 
     gn_swaps = [
@@ -1492,7 +1332,7 @@
             h = g * vec[0:1, :]
             first = jnp.mean(h, axis=-1, keepdims=True)
             slant = jnp.mean(h * hat, axis=-1, keepdims=True)
-            got = two[rows_of(c * half_seq + n * TILE + m * 64, 64), :].astype(f32) + r * (h - first - hat * slant)
+            got = three[rows_of(c * half_seq + n * TILE + m * 64, 64), :].astype(f32) + r * (h - first - hat * slant)
             home[here, :] = got.astype(bf)
             return (
                 gain_sum + jnp.sum(gh, axis=0, keepdims=True),
@@ -1509,7 +1349,7 @@
         send(sums.at[3], sums_in.at[3 + d], ss.at[3 + d], sr.at[3 + d], (i, lax.rem(z + d + 1, LINE)))
         for d in range(LINE - 1)
     ]
-    small_out = pltpu.make_async_copy(sums.at[4], small_o, os.at[7])
+    sums_out = pltpu.make_async_copy(sums.at[4], small_o, os.at[7])
 
     def small_step(n):
         if n > 0:
@@ -1522,94 +1362,168 @@
         for d in range(LINE - 1):
             small[3 + d].wait_recv()
         sums[4] = sums[3] + ((sums_in[3] + sums_in[4]) + sums_in[5])
-        small_out.start()
+        sums_out.start()
 
     (unit_b0, unit_b1), (unit_q, unit_k, unit_v) = unit_b, unit_a
 
-    pl.semaphore_wait(barrier, len(line_ids) + 2)
+    begin()
+    first(0)
+    for g in groups:
+        own_start(g)
+    first(1)
+    land(1, 0)
+    first(2)
+    land(1, 1)
+    turn(1, 0)
+    land(0, 0)
+    land(0, 1)
+    vectors()
+    x_start()
+    turn(0, 0)
+    turn(0, 1)
+    land(0, 2)
+    land(1, 2)
+    turn(0, 2)
+    first(3)
+    turn(1, 1)
+    land(2, 0)
+    x_spread()
+    norm_own()
+    norm_other()
+    whole(0)
+    project(0, 512)
+    turn(1, 2)
+    project(512, 1024)
+    project(1024, 1536)
+    project(1536, 3 * half)
+    turn(2, 0)
+    land(2, 1)
+    attend(0)
+    attend(1)
+    whole(1)
+    land(2, 2)
+    land(3, 0)
+    wo_swap()
+    attend(2)
+    wo_ready()
+    attend(3)
+    turn(2, 1)
+    turn(2, 2)
+    land(3, 2)
+    attend(4)
+    output_rows(0)
+    output_rows(1)
+    land(3, 1)
+    c_start()
+    output_rows(2)
+    output_rows(3)
+    turn(3, 0)
+    second_norm(0)
+    second_norm(1)
+    second_norm(2)
+    second_norm(3)
+    whole(2)
+    inner_tile(0)
+    inner_tile(1)
+    inner_tile(2)
+    inner_tile(3)
+    inner_tile(4)
+    inner_tile(5)
+    inner_tile(6)
+    inner_tile(7)
+    inner_tile(8)
+    c_spread()
+    turn(3, 1)
+    inner_tile(9)
+    turn(3, 2)
     mask()
     outer_rows(0)
     outer_rows(2)
+    whole(3)
     block_other()
     outer_rows(1)
+    block_own()
     outer_rows(3)
-    block_own()
     through_gelu()
+    weights_load()
+    to_second(0)
+    to_second(1)
     block_start()
+    to_second(2)
+    to_second(3)
+    unit_c.step2()
+    second_back()
     inner_grad(0)
     inner_grad(1)
-    to_second(0)
-    unit_c.step2()
-    middle_load()
-    to_second(1)
-    to_second(2)
-    to_second(3)
-    unit_b0.step1_all()
-    second_back()
+    qkv_load()
+    inner_free()
     unit_b1.step1_all()
     output_grad()
     mixed_grad()
+    o_swap.wait()
+    unit_b0.step1_all()
+    attend_back(0)
     unit_c.line()
     free_landing()
-    attend_back(0)
     attend_back(1)
+    attend_back(2)
+    unit_b1.step2()
+    attend_back(3)
+    unit_o.step1_all()
+    attend_back(4)
     unit_b0.step2()
-    attend_back(2)
-    attend_back(3)
-    unit_b1.step2()
-    attend_back(4)
-    unit_b0.line()
+    unit_b1.line()
+    query_key_grad()
     to_first(0)
-    o_swap.wait_recv()
     to_first(1)
-    unit_o.step1_all()
-    query_key_grad()
-    unit_b1.line()
-    value_grad()
     landing_free()
-    unit_v.step1_all()
-    unit_o.step2()
-    unit_v.step2()
-    unit_o.line()
     unit_q.step1_all()
     unit_k.step1_all()
+    unit_o.step2()
+    value_grad()
+    unit_b0.line()
+    unit_k.step2()
+    unit_o.line()
     unit_q.step2()
+    unit_k.line()
+    unit_v.step1_all()
+    unit_q.line()
+    unit_c.spread()
+    unit_v.step2()
+    unit_b0.spread()
+    first_back(0)
+    unit_b1.spread()
+    unit_q.spread()
+    unit_o.spread()
     unit_v.line()
-    unit_k.step2()
-    unit_o.spread()
-    unit_q.line()
-    unit_b1.spread()
-    unit_k.line()
-    first_back(0)
-    unit_b0.spread()
     first_back(1)
     small_step(0)
+    input_start()
+    unit_k.spread()
+    unit_c.cross()
+    unit_o.cross()
+    small_step(1)
+    unit_b0.cross()
     unit_v.spread()
-    unit_q.spread()
-    unit_c.spread()
-    small_step(1)
+    unit_k.cross()
+    small_step(2)
     unit_b1.cross()
-    input_start()
-    unit_b0.cross()
-    unit_k.spread()
-    small_step(2)
-    unit_o.cross()
-    unit_c.cross()
+    unit_c.to_core()
     unit_q.cross()
     small_step(3)
     unit_v.cross()
-    unit_k.cross()
-    unit_v.to_core()
+    unit_b1.to_core()
+    unit_b0.to_core()
     small_end()
     unit_q.to_core()
-    unit_b1.to_core()
     unit_k.to_core()
-    unit_c.to_core()
-    unit_b0.to_core()
     unit_o.to_core()
-    small_out.wait()
-    for d in small + gn_swaps + [o_swap]:
+    unit_v.to_core()
+    sums_out.wait()
+    for d in small + gn_swaps:
         d.wait_send()
+    x_sent()
+    c_sent()
     input_sent()
     block_arrived()
     input_arrived()
@@ -1622,44 +1536,50 @@
         u.end()
 
 
-def run_backward(vec, x, ct, wa, wob, wb, wc, normed, qkv, mixed, lse, middle, second, active, slope, gq, gk):
-    seq, feat = x.shape
+def run_layer(lengths, offsets, vectors, inner_bias, x, ct, wq, wk, wv, wo, w1, w2):
+    rows, feat = wq.shape
+    hid = w2.shape[0]
+    seq = x.shape[1] * LINE
     half = feat // 2
-    hid = wc.shape[0] // 2
-    rows = feat // LINE
     r_big, r_small = hid // 2 // PLANE, rows // PLANE
     f32, bf = jnp.float32, jnp.bfloat16
-    dma = pltpu.SemaphoreType.DMA
+    dma, plain = pltpu.SemaphoreType.DMA, pltpu.SemaphoreType.REGULAR
     anywhere = pl.BlockSpec(memory_space=pl.ANY)
+    here, scalars = pl.BlockSpec(memory_space=pltpu.VMEM), pl.BlockSpec(memory_space=pltpu.SMEM)
+    small, bounds = (16, 384), (lengths.shape[0], 8, 128)
     made = [
-        ((2, seq // LINE, feat), bf), ((2, seq // LINE, feat), bf), ((hid, feat), bf), ((rows, LINE * hid), bf),
+        (x.shape, bf), (x.shape, bf), ((hid, feat), bf), ((rows, LINE * hid), bf),
         ((rows, feat), bf), ((rows, feat), bf), ((rows, feat), bf), ((rows, feat), bf), ((16, feat), f32),
+        ((seq // 2, feat), bf), ((seq, feat), bf), ((seq, 4 * half), bf), ((feat, 3 * half), bf), ((feat, half), bf),
     ]
     held = [
-        (vec.shape, f32), ((seq, feat), bf), ((seq, 2 * hid), bf), ((seq, feat), bf), ((seq, feat), bf),
-        ((2 * hid, feat), bf), ((2 * hid, feat), bf), ((feat, 2 * hid), bf), ((feat, half), bf),
+        (small, bf), (bounds, jnp.int32), ((LINE,) + small, bf), (bounds, jnp.int32), ((small[0], feat), f32), ((1, 2 * hid), f32),
+        ((seq, feat), bf), ((seq, feat), bf), ((feat, 4 * half), bf), ((feat, half), bf), ((feat, 2 * hid), bf),
+        ((2 * hid, feat), bf), ((seq, 2 * hid), bf), ((feat, 2 * hid), bf), ((seq, feat), bf), ((seq, feat), bf),
         ((8 * r_big, feat), bf), ((4 * r_big, feat), bf), ((3 * r_big, feat), bf),
-        ((8 * r_small, 2 * hid), bf), ((4 * r_small, 2 * hid), bf), ((3 * r_small, 2 * hid), bf),
         ((8 * r_small, half), bf), ((4 * r_small, 4 * half), bf), ((3 * r_small, 4 * half), bf),
-        ((seq, 256), bf), ((seq, 128), bf), ((seq, 128), bf), ((16, seq), f32),
-        ((seq // 2, feat), bf), ((seq // 2, feat), bf), ((TILE, feat), f32), ((half, half), bf),
-        ((5, 16, feat), f32), ((6, 16, feat), f32), ((1, 2 * hid), f32), ((2, seq, 128), f32),
+        ((seq, 256), bf), ((seq, 128), bf), ((seq, 128), bf), ((half // HEAD_DIM, seq), f32),
+        ((seq // 2, feat), bf), ((seq // 2, feat), bf), ((TILE, feat), f32),
+        ((5, 16, feat), f32), ((6, 16, feat), f32),
     ]
-    return pl.pallas_call(
-        backward_kernel,
+    out = pl.pallas_call(
+        layer_kernel,
         out_shape=tuple(jax.ShapeDtypeStruct(shape, dtype) for shape, dtype in made),
-        in_specs=[anywhere] * 17,
+        in_specs=[scalars] + [here] * (2 + len(vectors)) + [anywhere] * 8,
         out_specs=(anywhere,) * len(made),
         scratch_shapes=[pltpu.VMEM(shape, dtype) for shape, dtype in held]
         + [
-            dma((14, 4)), dma((7, 12)), dma((7, 12)), dma((2, 2)), dma((2, 2)), dma((9,)), dma((9,)), dma((6,)), dma((6,)),
-            dma((8,)), pltpu.SemaphoreType.REGULAR, pltpu.SemaphoreType.REGULAR,
+            dma((3,)), dma((3,)), dma((4,)), dma((4,)), dma((4,)), dma((4,)),
+            dma((4, 5)), dma((12, 4)), dma((12, 5)), dma((7,)), dma((2,)), dma((2,)), dma((4,)), dma((4,)), dma((5,)),
+            dma((4, 3)), dma((7, 12)), dma((7, 12)), dma((2, 2)), dma((2, 2)), dma((9,)), dma((9,)), dma((6,)), dma((6,)),
+            dma((8,)), plain, plain, plain, plain, plain,
         ],
         compiler_params=pltpu.CompilerParams(
-            collective_id=1, has_side_effects=True, vmem_limit_bytes=VMEM_LIMIT
-        ),
-        name="backward",
-    )(vec, x, ct, wa, wob, wb, wc, normed, qkv, mixed, lse, middle, second, active, slope, gq, gk)
+            collective_id=0, has_side_effects=True, vmem_limit_bytes=VMEM_LIMIT
+        ),
+        name="layer",
+    )(lengths, offsets, *vectors, inner_bias, x, ct, wq, wk, wv, wo, w1, w2)
+    return out[:9]
 
 
 def finish_kernel(
@@ -1736,31 +1656,10 @@
     inputs, lengths, offsets, cotangent, norm_gain, norm_shift, query_proj, query_bias, key_proj, value_proj,
     value_bias, output_proj, output_bias, second_gain, second_shift, inner_proj, inner_bias, outer_proj, outer_bias,
 ):
-    cells_here, _, feat = inputs.shape
-    rows = feat // LINE
-    hid = outer_proj.shape[0]
-
     vectors = (norm_gain, norm_shift, query_bias, value_bias, output_bias, second_gain, second_shift, outer_bias)
-    entries = vectors + tuple(inner_bias[n * rows : (n + 1) * rows] for n in range(hid // rows))
-    row = lax.broadcasted_iota(jnp.int32, (16, rows), 0)
-    small = jnp.zeros((16, rows), entries[0].dtype)
-    for n, entry in enumerate(entries):
-        small = jnp.where(row == n, entry[None, :], small)
-    small = jnp.pad(small, ((0, 0), (0, 384 - rows)))
-    lanes, count = 128, offsets.shape[1]
-    first = jnp.pad(offsets, ((0, 0), (1, lanes - 1 - count)), constant_values=2 ** 30)
-    end = jnp.pad(offsets, ((0, 0), (0, lanes - count)), constant_values=2 ** 30)
-    group = lax.broadcasted_iota(jnp.int32, (cells_here, 8, lanes), 2)
-    kind = lax.broadcasted_iota(jnp.int32, (cells_here, 8, lanes), 1)
-    first = jnp.where(group == 0, 0, first[:, None, :])
-    bounds = jnp.where(kind == 0, first, jnp.where(kind == 1, end[:, None, :], lengths[:, None, None]))
-    (
-        mark_q, mark_k, vec, xf, cf, wa, wob, wb, wc, normed, qkv, mixed, lse, middle, second, active, slope,
-    ) = run_forward(
-        small, bounds, inputs, cotangent, query_proj, key_proj, value_proj, output_proj, inner_proj, outer_proj
-    )
-    grads = run_backward(
-        vec, xf, cf, wa, wob, wb, wc, normed, qkv, mixed, lse, middle, second, active, slope, mark_q, mark_k
+    grads = run_layer(
+        lengths, offsets, vectors, inner_bias, inputs, cotangent,
+        query_proj, key_proj, value_proj, output_proj, inner_proj, outer_proj,
     )
     return finish(*grads)
 

time: 417 us -> 399 us (0.957)
  Pallas kernels: 403 us -> 394 us
    pallas_call x2 -> x1, Pallas kernels: 391 us -> 382 us  [run_layer(): pl.pallas_call(layer_kernel, out_shape=tuple((jax.ShapeDtypeStruct(shape,...]
where the time goes in v5:
time: 399 us; the launch traced here: 395 us
  Pallas kernels  394 us (99%)
    pallas_call x1, Pallas kernels, run_layer(): pl.pallas_call(layer_kernel, out_shape=tuple((jax.ShapeDtypeStruct(shape,...  382 us
    pallas_call x1, Pallas kernels, finish(): pl.pallas_call(finish_kernel, out_shape=made, in_specs=[anywhere] * 9, ou...  12.2 us

profile of v5, /device:TPU:0, one launch (start us, length us, event | category | flops | bytes accessed | tf_op | source)
XLA Modules:
  0.0 394.6 jit_solution(11544447485156632570)
XLA Ops:
  0.7 381.6 %layer.1 = (bf16[2,256,1280]{2,1,0:T(8,128)(2,1)}, bf16[2,256,1280]{2,1,0:T(8,128)(2,1)}, bf16[1280,1280]{1,0:T(8,128)(2,1)}, bf16[320,5120]{1,0:T(8,128)(2,1)},...) custom-call(s32[2]{0:T(128)} %len_ref.1, ...), custom_call_target="tpu_custom_call" | custom-call | tf_op jit(solution)/shard_map/layer/pallas_call | solution.py:1565
  382.2 12.2 %finish.1 = (bf16[2,256,1280]{2,1,0:T(8,128)(2,1)}, bf16[2,256,1280]{2,1,0:T(8,128)(2,1)}, f32[320]{0:T(512)}, f32[320]{0:T(512)}, f32[320,1280]{1,0:T(8,128)}, ...) custom-call(bf16[2,256,1280]{2,1,0:T(8,128)(2,1)} %get-tuple-element, ...), custom_call_target="tpu_custom_call" | custom-call | tf_op jit(solution)/shard_map/finish/pallas_call | solution.py:1640

commit v6 on v5

--- a/solution.py
+++ b/solution.py
@@ -400,7 +400,7 @@
 
 PLANE = 4
 LINE = 4
-VMEM_LIMIT = 62 * 1024 * 1024
+VMEM_LIMIT = 65000 * 1024
 
 
 def rows_of(start, count):
@@ -413,6 +413,8 @@
 
 VECTORS = 8
 TILE = 256
+AHEAD = 1024
+BACK = 512
 
 
 def nt(left, right):
@@ -447,7 +449,7 @@
 def layer_kernel(
     len_ref, off_ref, v0, v1, v2, v3, v4, v5, v6, v7, b_ref, x_ref, ct_ref, wq_ref, wk_ref, wv_ref, wo_ref, w1_ref, w2_ref,
     block_o, input_o, w2_o, w1_o, q_o, k_o, v_o, o_o, small_o, x_o, normed_o, qkv_o, wa_o, wob_o,
-    small_ref, rag_ref, smalls, rag, vec, bias_in, xf, up, dc, do, wb, wts, big, db, two, three, r1c, r2c, zc, r1o, r2a, za, kx, gq, gk, lse,
+    small_ref, rag_ref, smalls, rag, vec, bias_in, xf, up, dc, do, wb, wts, big, db, two, three, r1c, r2c, zc, r2a, za, kx, lse,
     half_in, home, acc, sums, sums_in,
     sm_s, sm_r, ex_s, ex_r, fw_s, fw_r, ln_s, un_s, un_r, loc, wo_s, wo_r, pa_s, pa_r, out_s,
     ld, us, ur, hs, hr, cs, cr, ss, sr, os, free_x, free_y, freed_x, freed_y, freed_z,
@@ -711,9 +713,11 @@
             token = lax.broadcasted_iota(jnp.int32, (TILE, 128), 0) + n * TILE
             same = jnp.logical_and(token >= bounds[0:1, :], token < bounds[1:2, :])
             dead = jnp.where(token < bounds[2:3, :], 0.0, -1e30)
-            gq[at, :] = jnp.where(lanes == 127, 1.0, jnp.where(same, group_bias, 0.0)).astype(bf)
-            gk[at, :] = jnp.where(lanes == 127, dead, jnp.where(same, 1.0, 0.0)).astype(bf)
-        kx[:, 128:] = gk[...]
+            kx[at, pl.ds(128, 128)] = jnp.where(lanes == 127, dead, jnp.where(same, 1.0, 0.0)).astype(bf)
+
+    def query_mark(at, lane):
+        same = kx[at, pl.ds(128, 128)] * jnp.array(group_bias, bf)
+        return jnp.where(lane == 127, jnp.ones((), bf), same)
 
     def x_spread():
         x_arrived()
@@ -749,20 +753,20 @@
         if stop == 3 * half:
             keep("wa", wa, wa_o)
 
-    lane = lax.broadcasted_iota(jnp.int32, (TILE, 128), 1)
-
     def attend(t):
+        lane = lax.broadcasted_iota(jnp.int32, (AHEAD, 128), 1)
         k2 = big[:, pl.ds(half + t * 128, 128)]
         v2t = jnp.transpose(big[:, pl.ds(2 * half + t * 128, 128)])
         kx[:, :128] = k2
 
         def chunk(n, _):
-            at = pl.ds(pl.multiple_of(n * TILE, TILE), TILE)
+            at = pl.ds(pl.multiple_of(n * AHEAD, AHEAD), AHEAD)
             q2 = big[at, pl.ds(t * 128, 128)] * jnp.array(HEAD_DIM ** (-0.5), bf)
+            mark = query_mark(at, lane)
             both = []
             for h in range(2):
                 own = lane < HEAD_DIM if h == 0 else lane >= HEAD_DIM
-                qx = jnp.concatenate([jnp.where(own, q2, jnp.zeros((), bf)), gq[at, :]], axis=1)
+                qx = jnp.concatenate([jnp.where(own, q2, jnp.zeros((), bf)), mark], axis=1)
                 s = nt(kx[...], qx)
                 top = jnp.max(s, axis=0, keepdims=True)
                 e = jnp.exp(s - top)
@@ -773,7 +777,7 @@
             big[at, pl.ds(3 * half + t * 128, 128)] = jnp.transpose(jnp.concatenate(both, axis=0)).astype(bf)
             return _
 
-        lax.fori_loop(0, seq // TILE, chunk, 0)
+        lax.fori_loop(0, seq // AHEAD, chunk, 0)
         if t == half // 128 - 1:
             keep("qkv", big, qkv_o)
 
@@ -842,7 +846,7 @@
             db[at, cols] = slope.astype(bf)
             return _
 
-        lax.fori_loop(0, chunks, tile_rows, 0)
+        lax.fori_loop(0, chunks, tile_rows, 0, unroll=4)
 
     def c_spread():
         c_arrived()
@@ -1017,8 +1021,8 @@
         )
         for n in range(2)
     ]
-    unit_o = Unit(3, do, 0, r_small, half, (r1o, 0, 0), (r2a, 0, 0), (za, 0, 0), [(0, half, place_of(o_o))])
-    spots = ((0, 0), (0, half), (8 * r_small, 0))
+    spots = ((0, 0), (0, half), (8 * r_small, 0), (8 * r_small, half))
+    unit_o = Unit(3, do, 0, r_small, half, (r1c,) + spots[3], (r2a, 0, 0), (za, 0, 0), [(0, half, place_of(o_o))])
     unit_a = [
         Unit(
             4 + n, db, n * half, r_small, half, (r1c,) + spots[n], (r2a, 0, (1 + n) * half), (za, 0, (1 + n) * half),
@@ -1067,7 +1071,7 @@
 
         def mask_rows(n, total):
             at = pl.ds(pl.multiple_of(n * TILE, TILE), TILE)
-            gone = gk[at, 127:128].astype(f32) < 0.0
+            gone = kx[at, 255:256].astype(f32) < 0.0
             value = jnp.where(gone, 0.0, up[at, :].astype(f32))
             up[at, :] = value.astype(bf)
             return total + jnp.sum(value, axis=0, keepdims=True)
@@ -1106,7 +1110,7 @@
             to = pl.ds(n * TILE, TILE)
             acc[...] = nn(big[at, :], wts[...])
             swaps[n].wait_recv()
-            gone = gk[at, 127:128].astype(f32) < 0.0
+            gone = kx[at, 255:256].astype(f32) < 0.0
             value = xf[at, :].astype(f32) + acc[...] + half_in[to, :].astype(f32) + vec[7:8, :]
             home[to, :] = jnp.where(gone, 0.0, value).astype(bf)
 
@@ -1223,21 +1227,23 @@
     root = HEAD_DIM ** (-0.5)
 
     def attend_back(t):
+        lane = lax.broadcasted_iota(jnp.int32, (BACK, 128), 1)
         k2 = big[:, pl.ds(half + t * 128, 128)]
         k2t = jnp.transpose(k2)
         kx[:, :128] = k2
         acc[...] = jnp.zeros(acc.shape, f32)
 
         def chunk(n, _):
-            at = pl.ds(pl.multiple_of(n * TILE, TILE), TILE)
+            at = pl.ds(pl.multiple_of(n * BACK, BACK), BACK)
             q2 = big[at, pl.ds(t * 128, 128)] * jnp.array(root, bf)
+            mark = query_mark(at, lane)
             g2 = dc[at, pl.ds(3 * half + t * 128, 128)]
             both = []
             for h in range(2):
                 own = lane < HEAD_DIM if h == 0 else lane >= HEAD_DIM
                 qm = jnp.where(own, q2, jnp.zeros((), bf))
                 gm = jnp.where(own, g2, jnp.zeros((), bf))
-                s = nt(kx[...], jnp.concatenate([qm, gq[at, :]], axis=1))
+                s = nt(kx[...], jnp.concatenate([qm, mark], axis=1))
                 prob = jnp.exp(s - lse[2 * t + h : 2 * t + h + 1, at])
                 grad = nt(big[:, pl.ds(2 * half + t * 128, 128)], gm)
                 both_of = prob * grad
@@ -1250,7 +1256,7 @@
             dc[at, pl.ds(t * 128, 128)] = (jnp.transpose(jnp.concatenate(both, axis=0)) * root).astype(bf)
             return _
 
-        lax.fori_loop(0, chunks, chunk, 0)
+        lax.fori_loop(0, seq // BACK, chunk, 0)
         for which in range(2):
             for m in range(chunks):
                 dc[pl.ds(m * TILE, TILE), pl.ds((1 + which) * half + t * 128, 128)] = acc[
@@ -1345,23 +1351,23 @@
             sums[0, 1:2, :] = first_sums[1]
 
     small_who = [(core_nb, z), (x_nb, z), (y_nb, z)]
-    small = [send(sums.at[n], sums_in.at[n], ss.at[n], sr.at[n], small_who[n]) for n in range(3)] + [
-        send(sums.at[3], sums_in.at[3 + d], ss.at[3 + d], sr.at[3 + d], (i, lax.rem(z + d + 1, LINE)))
+    small = [send(sums.at[0], sums_in.at[n], ss.at[n], sr.at[n], small_who[n]) for n in range(3)] + [
+        send(sums.at[0], sums_in.at[3 + d], ss.at[3 + d], sr.at[3 + d], (i, lax.rem(z + d + 1, LINE)))
         for d in range(LINE - 1)
     ]
-    sums_out = pltpu.make_async_copy(sums.at[4], small_o, os.at[7])
+    sums_out = pltpu.make_async_copy(sums.at[0], small_o, os.at[7])
 
     def small_step(n):
         if n > 0:
-            small[n - 1].wait_recv()
-            sums[n] = sums[n - 1] + sums_in[n - 1]
+            small[n - 1].wait()
+            sums[0] = sums[0] + sums_in[n - 1]
         for d in small[3:] if n == 3 else small[n : n + 1]:
             d.start()
 
     def small_end():
         for d in range(LINE - 1):
-            small[3 + d].wait_recv()
-        sums[4] = sums[3] + ((sums_in[3] + sums_in[4]) + sums_in[5])
+            small[3 + d].wait()
+        sums[0] = sums[0] + ((sums_in[3] + sums_in[4]) + sums_in[5])
         sums_out.start()
 
     (unit_b0, unit_b1), (unit_q, unit_k, unit_v) = unit_b, unit_a
@@ -1371,57 +1377,58 @@
     for g in groups:
         own_start(g)
     first(1)
+    land(0, 1)
+    land(0, 0)
     land(1, 0)
     first(2)
-    land(1, 1)
-    turn(1, 0)
-    land(0, 0)
-    land(0, 1)
-    vectors()
-    x_start()
-    turn(0, 0)
     turn(0, 1)
     land(0, 2)
     land(1, 2)
+    land(1, 1)
+    x_start()
+    turn(0, 0)
+    vectors()
     turn(0, 2)
+    land(2, 0)
+    land(2, 1)
+    turn(1, 2)
+    turn(1, 0)
     first(3)
+    x_spread()
+    whole(0)
     turn(1, 1)
-    land(2, 0)
-    x_spread()
     norm_own()
     norm_other()
-    whole(0)
+    turn(2, 1)
     project(0, 512)
-    turn(1, 2)
+    turn(2, 0)
     project(512, 1024)
     project(1024, 1536)
     project(1536, 3 * half)
-    turn(2, 0)
-    land(2, 1)
-    attend(0)
-    attend(1)
     whole(1)
-    land(2, 2)
     land(3, 0)
     wo_swap()
+    land(2, 2)
+    attend(0)
+    wo_ready()
+    land(3, 1)
+    attend(1)
     attend(2)
-    wo_ready()
+    c_start()
     attend(3)
-    turn(2, 1)
-    turn(2, 2)
-    land(3, 2)
     attend(4)
     output_rows(0)
     output_rows(1)
-    land(3, 1)
-    c_start()
     output_rows(2)
     output_rows(3)
+    turn(2, 2)
     turn(3, 0)
     second_norm(0)
     second_norm(1)
     second_norm(2)
     second_norm(3)
+    land(3, 2)
+    turn(3, 1)
     whole(2)
     inner_tile(0)
     inner_tile(1)
@@ -1430,97 +1437,96 @@
     inner_tile(4)
     inner_tile(5)
     inner_tile(6)
+    c_spread()
     inner_tile(7)
     inner_tile(8)
-    c_spread()
-    turn(3, 1)
     inner_tile(9)
     turn(3, 2)
     mask()
     outer_rows(0)
     outer_rows(2)
+    outer_rows(1)
+    outer_rows(3)
     whole(3)
     block_other()
-    outer_rows(1)
     block_own()
-    outer_rows(3)
     through_gelu()
     weights_load()
     to_second(0)
     to_second(1)
-    block_start()
     to_second(2)
     to_second(3)
     unit_c.step2()
     second_back()
+    block_start()
     inner_grad(0)
+    inner_free()
+    unit_b0.step1_all()
     inner_grad(1)
     qkv_load()
-    inner_free()
-    unit_b1.step1_all()
     output_grad()
+    o_swap.wait()
     mixed_grad()
-    o_swap.wait()
-    unit_b0.step1_all()
     attend_back(0)
     unit_c.line()
     free_landing()
+    unit_b1.step1_all()
     attend_back(1)
     attend_back(2)
+    unit_b0.step2()
+    landing_free()
+    unit_o.step1_all()
+    attend_back(3)
     unit_b1.step2()
-    attend_back(3)
-    unit_o.step1_all()
     attend_back(4)
-    unit_b0.step2()
+    query_key_grad()
+    unit_q.step1_all()
+    to_first(0)
+    unit_b0.line()
+    value_grad()
     unit_b1.line()
-    query_key_grad()
-    to_first(0)
+    unit_o.step2()
+    unit_k.step1_all()
+    unit_q.step2()
+    unit_v.step1_all()
     to_first(1)
-    landing_free()
-    unit_q.step1_all()
-    unit_k.step1_all()
-    unit_o.step2()
-    value_grad()
-    unit_b0.line()
+    unit_o.line()
+    unit_q.line()
     unit_k.step2()
-    unit_o.line()
-    unit_q.step2()
+    unit_v.step2()
+    unit_b1.spread()
+    unit_o.spread()
     unit_k.line()
-    unit_v.step1_all()
-    unit_q.line()
     unit_c.spread()
-    unit_v.step2()
-    unit_b0.spread()
+    unit_q.spread()
+    unit_v.line()
+    unit_o.cross()
     first_back(0)
-    unit_b1.spread()
-    unit_q.spread()
-    unit_o.spread()
-    unit_v.line()
     first_back(1)
     small_step(0)
+    unit_k.spread()
     input_start()
-    unit_k.spread()
+    unit_q.cross()
+    unit_b0.spread()
+    small_step(1)
+    unit_v.spread()
+    unit_b1.cross()
+    unit_q.to_core()
+    small_step(2)
     unit_c.cross()
-    unit_o.cross()
-    small_step(1)
+    unit_v.cross()
     unit_b0.cross()
-    unit_v.spread()
+    small_step(3)
+    unit_c.to_core()
+    unit_b1.to_core()
     unit_k.cross()
-    small_step(2)
-    unit_b1.cross()
-    unit_c.to_core()
-    unit_q.cross()
-    small_step(3)
-    unit_v.cross()
-    unit_b1.to_core()
+    small_end()
     unit_b0.to_core()
-    small_end()
-    unit_q.to_core()
+    unit_v.to_core()
+    unit_o.to_core()
     unit_k.to_core()
-    unit_o.to_core()
-    unit_v.to_core()
     sums_out.wait()
-    for d in small + gn_swaps:
+    for d in gn_swaps:
         d.wait_send()
     x_sent()
     c_sent()
@@ -1557,10 +1563,10 @@
         ((seq, feat), bf), ((seq, feat), bf), ((feat, 4 * half), bf), ((feat, half), bf), ((feat, 2 * hid), bf),
         ((2 * hid, feat), bf), ((seq, 2 * hid), bf), ((feat, 2 * hid), bf), ((seq, feat), bf), ((seq, feat), bf),
         ((8 * r_big, feat), bf), ((4 * r_big, feat), bf), ((3 * r_big, feat), bf),
-        ((8 * r_small, half), bf), ((4 * r_small, 4 * half), bf), ((3 * r_small, 4 * half), bf),
-        ((seq, 256), bf), ((seq, 128), bf), ((seq, 128), bf), ((half // HEAD_DIM, seq), f32),
+        ((4 * r_small, 4 * half), bf), ((3 * r_small, 4 * half), bf),
+        ((seq, 256), bf), ((half // HEAD_DIM, seq), f32),
         ((seq // 2, feat), bf), ((seq // 2, feat), bf), ((TILE, feat), f32),
-        ((5, 16, feat), f32), ((6, 16, feat), f32),
+        ((1, 16, feat), f32), ((6, 16, feat), f32),
     ]
     out = pl.pallas_call(
         layer_kernel,

time: 399 us -> 380 us (0.952)
  Pallas kernels: 394 us -> 376 us
    pallas_call x1, Pallas kernels: 382 us -> 363 us  [run_layer(): pl.pallas_call(layer_kernel, out_shape=tuple((jax.ShapeDtypeStruct(shape,...]
where the time goes in v6:
time: 380 us; the launch traced here: 377 us
  Pallas kernels  376 us (99%)
    pallas_call x1, Pallas kernels, run_layer(): pl.pallas_call(layer_kernel, out_shape=tuple((jax.ShapeDtypeStruct(shape,...  363 us
    pallas_call x1, Pallas kernels, finish(): pl.pallas_call(finish_kernel, out_shape=made, in_specs=[anywhere] * 9, ou...  12.2 us

profile of v6, /device:TPU:0, one launch (start us, length us, event | category | flops | bytes accessed | tf_op | source)
XLA Modules:
  0.0 376.6 jit_solution(5382665918974406745)
XLA Ops:
  0.7 363.4 %layer.1 = (bf16[2,256,1280]{2,1,0:T(8,128)(2,1)}, bf16[2,256,1280]{2,1,0:T(8,128)(2,1)}, bf16[1280,1280]{1,0:T(8,128)(2,1)}, bf16[320,5120]{1,0:T(8,128)(2,1)},...) custom-call(s32[2]{0:T(128)} %len_ref.1, ...), custom_call_target="tpu_custom_call" | custom-call | tf_op jit(solution)/shard_map/layer/pallas_call | solution.py:1571
  364.1 12.2 %finish.1 = (bf16[2,256,1280]{2,1,0:T(8,128)(2,1)}, bf16[2,256,1280]{2,1,0:T(8,128)(2,1)}, f32[320]{0:T(512)}, f32[320]{0:T(512)}, f32[320,1280]{1,0:T(8,128)}, ...) custom-call(bf16[2,256,1280]{2,1,0:T(8,128)(2,1)} %get-tuple-element, ...), custom_call_target="tpu_custom_call" | custom-call | tf_op jit(solution)/shard_map/finish/pallas_call | solution.py:1646

commit v7 on v6

--- a/solution.py
+++ b/solution.py
@@ -1056,10 +1056,18 @@
             pl.when(jnp.logical_not(stay))(outs[0].wait_recv)
             outs[1].wait_recv()
 
-        return start, sent, arrived
-
-    block_start, block_sent, block_arrived = going_home(home, block_o, 0)
-    input_start, input_sent, input_arrived = going_home(home, input_o, 1)
+        def start_one(b):
+            k = lax.rem(z + b, 2)
+            part, to = src.at[pl.ds(b * block, block), :], dst.at[lax.rem(z, 2)]
+            here = jnp.logical_and(stay, k == 0)
+            pl.when(here)(pltpu.make_async_copy(part, to, hr.at[e, k]).start)
+            away = send(part, to, hs.at[e, k], hr.at[e, k], (i - c + z // 2, 2 * c + b))
+            pl.when(jnp.logical_not(here))(away.start)
+
+        return start, sent, arrived, start_one
+
+    block_start, block_sent, block_arrived, _ = going_home(home, block_o, 0)
+    _, input_sent, input_arrived, input_one = going_home(home, input_o, 1)
 
     first_core = jnp.where(c == 0, 1.0, 0.0)
     zero_row = jnp.zeros((1, feat), f32)
@@ -1346,6 +1354,7 @@
             )
 
         first_sums[:] = lax.fori_loop(0, TILE // 64, first_rows, tuple(first_sums))
+        input_one(n)
         if n == half_seq // TILE - 1:
             sums[0, 0:1, :] = first_sums[0]
             sums[0, 1:2, :] = first_sums[1]
@@ -1505,7 +1514,6 @@
     first_back(1)
     small_step(0)
     unit_k.spread()
-    input_start()
     unit_q.cross()
     unit_b0.spread()
     small_step(1)

time: 380 us -> 380 us (level)
  no operation moved by 1% of the time
where the time goes in v7:
time: 380 us; the launch traced here: 377 us
  Pallas kernels  376 us (99%)
    pallas_call x1, Pallas kernels, run_layer(): pl.pallas_call(layer_kernel, out_shape=tuple((jax.ShapeDtypeStruct(shape,...  363 us
    pallas_call x1, Pallas kernels, finish(): pl.pallas_call(finish_kernel, out_shape=made, in_specs=[anywhere] * 9, ou...  12.2 us

profile of v7, /device:TPU:0, one launch (start us, length us, event | category | flops | bytes accessed | tf_op | source)
XLA Modules:
  0.0 376.6 jit_solution(15362561297418058281)
XLA Ops:
  0.7 363.4 %layer.1 = (bf16[2,256,1280]{2,1,0:T(8,128)(2,1)}, bf16[2,256,1280]{2,1,0:T(8,128)(2,1)}, bf16[1280,1280]{1,0:T(8,128)(2,1)}, bf16[320,5120]{1,0:T(8,128)(2,1)},...) custom-call(s32[2]{0:T(128)} %len_ref.1, ...), custom_call_target="tpu_custom_call" | custom-call | tf_op jit(solution)/shard_map/layer/pallas_call | solution.py:1579
  364.1 12.2 %finish.1 = (bf16[2,256,1280]{2,1,0:T(8,128)(2,1)}, bf16[2,256,1280]{2,1,0:T(8,128)(2,1)}, f32[320]{0:T(512)}, f32[320]{0:T(512)}, f32[320,1280]{1,0:T(8,128)}, ...) custom-call(bf16[2,256,1280]{2,1,0:T(8,128)(2,1)} %get-tuple-element, ...), custom_call_target="tpu_custom_call" | custom-call | tf_op jit(solution)/shard_map/finish/pallas_call | solution.py:1654
